TPU v7x, 128 devices: a whole 4x4x4 slice. The times are simulated.
128 devices in a mesh: grp: 4 (over x), dev: 32 (over y, z, core).
Axes of the slice: x: 4, y: 4, z: 4, core: 2. Of those that a mesh axis runs over, the one named last changes fastest.
Arguments:
- query: bfloat16 [256, 8192], P(('grp', 'dev')), may hold values from -64 to 64
- key_cache: bfloat16 [256, 2048, 256], P(('grp', 'dev')), may hold values from -8 to 8
- value_cache: bfloat16 [256, 2048, 256], P(('grp', 'dev')), may hold values from -6 to 6
- lengths: int32 [256], P(('grp', 'dev')), may hold values from 0 to 2048, as said below
- hidden: bfloat16 [256, 7168], P(('grp', 'dev')), may hold values from -40 to 40
- out_weight: bfloat16 [8192, 7168], P(None, 'dev'), may hold values from -1 to 1
- ffn_gain: float32 [7168], replicated, may hold values from 0.1 to 1.9
- gate_weight: bfloat16 [7168, 16384], P(None, ('grp', 'dev')), may hold values from -0.0625 to 0.0625
- up_weight: bfloat16 [7168, 16384], P(None, ('grp', 'dev')), may hold values from -0.0625 to 0.0625
- down_weight: bfloat16 [7168, 16384], P(None, ('grp', 'dev')), may hold values from -0.1875 to 0.1875
Outputs:
- mixed: bfloat16 [256, 7168], P(('grp', 'dev'))
Inputs may be any that keep to these rules, and one draw needn't show every extreme that they name: `lengths`: each slot holds 0 or 2 to 2048; the first slot holds 2048.
All inputs are finite; a program needn't handle non-finite values.
Results may differ from a plain program's by a relative error of at most 0.0075.
Values may be sent and summed in bfloat16 or wider, within the bound.
No kernel may reach another device: no remote copies, remote signals or barrier semaphores. Data moves between devices by JAX's collectives and lax.ppermute only.
A program may use at most 128 MiB of HBM per device.

v0:
```python
import jax
import jax.numpy as jnp
from jax import lax
from jax.sharding import PartitionSpec as P


def attend(query, key_cache, value_cache, lengths):
    slot_count = query.shape[0]
    head_dim = key_cache.shape[2]
    head_count = query.shape[1] // head_dim
    queries = query.reshape(slot_count, head_count, head_dim)
    scores = jnp.einsum(
        "shd,std->sht", queries, key_cache, preferred_element_type=jnp.float32
    ) * head_dim ** (-0.5)
    positions = lax.broadcasted_iota(jnp.int32, (1, 1, key_cache.shape[1]), 2)
    in_range = positions < jnp.maximum(lengths, 1)[:, None, None]
    scores = jnp.where(in_range, scores, -jnp.inf)
    highest = jnp.max(scores, axis=2, keepdims=True)
    weights = jnp.exp(scores - highest)
    probs = (weights / jnp.sum(weights, axis=2, keepdims=True)).astype(jnp.bfloat16)
    attended = jnp.einsum("sht,std->shd", probs, value_cache, preferred_element_type=jnp.float32)
    return attended.reshape(slot_count, head_count * head_dim).astype(jnp.bfloat16)


def feed_terms(rows_in, gate_weight, up_weight, down_weight):
    gate_act = jnp.dot(rows_in, gate_weight, preferred_element_type=jnp.float32)
    up_act = jnp.dot(rows_in, up_weight, preferred_element_type=jnp.float32)
    activated = (jax.nn.silu(gate_act) * up_act).astype(jnp.bfloat16)
    return lax.dot_general(
        activated, down_weight, (((1,), (1,)), ((), ())), preferred_element_type=jnp.float32
    )


def shards(
    query,
    key_cache,
    value_cache,
    lengths,
    hidden,
    out_weight,
    ffn_gain,
    gate_weight,
    up_weight,
    down_weight,
):
    attended = attend(query, key_cache, value_cache, lengths)
    columns = jnp.dot(
        lax.all_gather(attended, "dev", axis=0, tiled=True),
        out_weight,
        preferred_element_type=jnp.float32,
    ).astype(jnp.bfloat16)
    projected = lax.all_to_all(columns, "dev", split_axis=0, concat_axis=1, tiled=True)
    residual = hidden.astype(jnp.float32) + projected.astype(jnp.float32)
    scale = lax.rsqrt(jnp.mean(residual * residual, axis=1, keepdims=True) + 1e-05)
    normed = (residual * scale * ffn_gain).astype(jnp.bfloat16)
    everyone = lax.all_gather(normed, ("grp", "dev"), axis=0, tiled=True)
    partial_value = feed_terms(everyone, gate_weight, up_weight, down_weight)
    feed = lax.psum_scatter(partial_value, ("grp", "dev"), scatter_dimension=0, tiled=True)
    live_rows = (lengths > 0)[:, None]
    return jnp.where(live_rows, residual + feed, 0.0).astype(jnp.bfloat16)


def solution(mesh):
    in_specs = (
        P(("grp", "dev"), None),
        P(("grp", "dev"), None, None),
        P(("grp", "dev"), None, None),
        P(("grp", "dev")),
        P(("grp", "dev"), None),
        P(None, "dev"),
        P(),
        P(None, ("grp", "dev")),
        P(None, ("grp", "dev")),
        P(None, ("grp", "dev")),
    )
    out_specs = P(("grp", "dev"), None)
    return jax.shard_map(shards, mesh=mesh, in_specs=in_specs, out_specs=out_specs, check_vma=False)
```

profile of v0, /device:TPU:1, one launch (start us, length us, event | category | flops | bytes accessed | tf_op | source)
XLA Modules:
  0.0 327.3 jit_solution(972901001639888107)
XLA Ops:
  6.5 0.0 copy-start
  6.5 0.0 all-gather.5.cloned.1.call-start
  6.5 0.8 broadcast_maximum_fusion
  7.3 0.1 iota_compare_fusion
  7.4 0.7 copy-done
  8.1 1.5 fusion.3
  9.6 0.2 fusion.20
  9.9 2.1 convolution_convert_fusion.1
  12.0 0.6 reshape.45
  12.6 0.0 all-gather.5.cloned.1.call-update
  12.6 0.0 all-gather.7.cloned.1.call-start
  12.7 46.7 %all-gather.5.cloned.1.call-done = bf16[32,2,8192]{2,1,0:T(2,128)(2,1)} async-done(((bf16[1,2,8192]{2,1,0:T(2,128)(2,1)}), bf16[32,2,8192]{2,1,0:T(2,128)(2,1)}) %all-gather.5.cloned.1.call-update) | async-done | bytes 1048592 | tf_op jit(solution)/shard_map/all_gather | solution.py:48
  59.4 1.5 reshape.46
  60.8 0.0 copy-start.1
  60.9 0.0 copy-start.2
  60.9 3.3 %convolution_convert_fusion = bf16[64,224]{1,0:T(8,128)(2,1)S(1)} fusion(bf16[64,8192]{1,0:T(8,128)(2,1)S(1)} %reshape.46, bf16[8192,224]{0,1:T(8,128)(2,1)} %param.15), kind=kOutput, calls=%fused_computation.8 | convolution fusion | flops 234895360 | bytes 4747264 | tf_op jit(solution)/shard_map/dot_general | solution.py:47
  64.2 12.3 %all_to_all.13 = bf16[32,2,224]{2,1,0:T(2,128)(2,1)S(1)} all-to-all(bf16[32,2,224]{2,1,0:T(2,128)(2,1)S(1)} %all_to_all.10), channel_id=1, replica_groups=mesh['grp'=4,'dev'=32] {'dev'}, dimensions={0} | all-to-all | bytes 57344 | tf_op jit(solution)/shard_map/all_to_all | solution.py:52
  76.5 0.1 reshape.44
  76.6 0.0 copy-done.1
  76.7 0.2 multiply_reduce_fusion
  76.8 0.0 copy-done.2
  76.8 0.7 fusion.17
  77.6 0.0 all-gather.7.cloned.1.call-update
  77.6 0.0 all-reduce.3.cloned.1.call-start
  77.6 64.1 %all-gather.7.cloned.1.call-done = bf16[128,2,7168]{2,1,0:T(2,128)(2,1)} async-done(((bf16[1,2,7168]{2,1,0:T(2,128)(2,1)}), bf16[128,2,7168]{2,1,0:T(2,128)(2,1)}) %all-gather.7.cloned.1.call-update) | async-done | bytes 3670032 | tf_op jit(solution)/shard_map/all_gather | solution.py:56
  141.7 8.4 %reshape.48 = bf16[256,7168]{1,0:T(8,128)(2,1)} reshape(bf16[128,2,7168]{2,1,0:T(2,128)(2,1)} %all-gather.7.cloned.1.call-done) | data formatting | bytes 7340032
  150.1 3.7 %fusion.21 = f32[256,128]{1,0:T(8,128)S(1)} fusion(bf16[256,7168]{1,0:T(8,128)(2,1)} %reshape.48, bf16[7168,128]{1,0:T(8,128)(2,1)} %param.17), kind=kOutput, calls=%fused_computation.35 | convolution fusion | flops 469762048 | bytes 5636096 | tf_op jit(solution)/shard_map/dot_general | solution.py:26
  153.9 8.2 %fusion.5 = f32[256,7168]{1,0:T(8,128)} fusion(bf16[7168,128]{1,0:T(8,128)(2,1)} %param.19, bf16[256,7168]{1,0:T(8,128)(2,1)} %reshape.48, bf16[7168,128]{1,0:T(8,128)(2,1)} %param.18, f32[256,128]{1,0:T(8,128)S(1)} %fusion.21), kind=kOutput, calls=%fused_computation.7 | convolution fusion | flops 939720704 | bytes 14811136 | tf_op jit(solution)/shard_map/dot_general | solution.py:29
  162.1 0.0 copy-start.3
  162.1 0.0 all-reduce.3.cloned.1.call-update
  162.1 0.6 copy-done.3
  162.8 156.4 %all-reduce.3.cloned.1.call-done = f32[256,7168]{1,0:T(8,128)} async-done(((f32[256,7168]{1,0:T(8,128)}), f32[256,7168]{1,0:T(8,128)}) %all-reduce.3.cloned.1.call-update) | async-done | bytes 7340048
  319.1 1.6 fusion.14
  (5 shorter events, 0.1 us)
Async XLA Ops:
  6.5 1.6 copy-start
  6.5 52.8 %all-gather.5.cloned.1.call-start = ((), (), s32[]{:S(2)}) async-start(), calls=%async_computation.1 | async-start | bytes 1081344 | tf_op jit(solution)/shard_map/all_gather | solution.py:48
  12.6 129.1 %all-gather.7.cloned.1.call-start = ((), (), s32[]{:S(2)}) async-start(), calls=%async_computation.2 | async-start | bytes 3698688 | tf_op jit(solution)/shard_map/all_gather | solution.py:56
  60.8 15.8 %copy-start.1 = (bf16[2,7168]{1,0:T(2,128)(2,1)S(1)}, bf16[2,7168]{1,0:T(2,128)(2,1)}, u32[]{:S(2)}) copy-start(bf16[2,7168]{1,0:T(2,128)(2,1)} %param.14) | copy-start | bytes 86020
  60.9 16.0 %copy-start.2 = (f32[7168]{0:T(1024)S(1)}, f32[7168]{0:T(1024)}, u32[]{:S(2)}) copy-start(f32[7168]{0:T(1024)} %param.16) | copy-start | bytes 86020
  77.6 241.6 %all-reduce.3.cloned.1.call-start = ((), (), s32[]{:S(2)}) async-start(), calls=%async_computation.3 | async-start | bytes 14680064
  162.1 0.7 copy-start.3
Sparse Core Ops, SparseCore 0:
  12.8 46.5 all-gather.4
  77.7 63.9 all-gather.6
  162.2 156.8 all-reduce.2
where the time goes:
time: 328 us; the launch traced here: 327 us
  waiting for transfers between devices  267 us (81%)
  matrix products  18.9 us (6%)
  between operations  13.2 us (4%)
  blocking collectives  12.3 us (4%)
  local copies, waits for them, and re-layouts  12 us (4%)
  other arithmetic  3.69 us (1%)
    unnamed x4, waiting for transfers between devices  156 us
    all_gather x1, waiting for transfers between devices, shards(): everyone = lax.all_gather(normed, ('grp', 'dev'), axis=0, tiled=True)  64.1 us
    all_gather x1, waiting for transfers between devices, shards(): lax.all_gather(attended, 'dev', axis=0, tiled=True)  46.7 us
    all_to_all x1, blocking collectives, shards(): lax.all_to_all(columns, 'dev', split_axis=0, concat_axis=1, tiled=True)  12.3 us
    unnamed x11, local copies, waits for them, and re-layouts  11.8 us
    dot_general x1, matrix products, feed_terms(): lax.dot_general(activated, down_weight, (((1,), (1,)), ((), ())), preferr...  8.25 us
  transfers between devices with their start and end apart: 3, of which 3 were waited for; matrix products, arithmetic and copies ran while one was open for 0% of the time, Pallas kernels for 0%

commit v1 on v0

v1 whole, which is shorter than its diff:
```python
import jax
import jax.numpy as jnp
from jax import lax
from jax.sharding import PartitionSpec as P

BF16 = jnp.bfloat16
F32 = jnp.float32
EPS = 1e-05


def attend(query, key_cache, value_cache, lengths):
    slot_count = query.shape[0]
    head_dim = key_cache.shape[2]
    head_count = query.shape[1] // head_dim
    queries = query.reshape(slot_count, head_count, head_dim)
    scores = jnp.einsum(
        "shd,std->sht", queries, key_cache, preferred_element_type=jnp.float32
    ) * head_dim ** (-0.5)
    positions = lax.broadcasted_iota(jnp.int32, (1, 1, key_cache.shape[1]), 2)
    in_range = positions < jnp.maximum(lengths, 1)[:, None, None]
    scores = jnp.where(in_range, scores, -jnp.inf)
    highest = jnp.max(scores, axis=2, keepdims=True)
    weights = jnp.exp(scores - highest)
    probs = (weights / jnp.sum(weights, axis=2, keepdims=True)).astype(jnp.bfloat16)
    attended = jnp.einsum("sht,std->shd", probs, value_cache, preferred_element_type=jnp.float32)
    return attended.reshape(slot_count, head_count * head_dim).astype(jnp.bfloat16)


def make_shards(groups, devs):
    chips = devs // 2
    peers = groups * chips
    plane = [[2 * k + c for k in range(chips)] for c in range(2)]
    cube = [[2 * k + c for k in range(peers)] for c in range(2)]
    other = [(i, i ^ 1) for i in range(devs)]

    def shards(
        query,
        key_cache,
        value_cache,
        lengths,
        hidden,
        out_weight,
        ffn_gain,
        gate_weight,
        up_weight,
        down_weight,
    ):
        me = lax.axis_index("dev")
        core = lax.rem(me, 2)
        chip = lax.div(me, 2)
        slots, width = hidden.shape
        cols = width // chips

        def swap(w):
            return lax.ppermute(w, "dev", other)

        out_other = swap(out_weight)
        gate_other = swap(gate_weight)
        up_other = swap(up_weight)
        down_other = swap(down_weight)

        attended = attend(query, key_cache, value_cache, lengths)
        kdim = attended.shape[1]
        pieces = hidden.reshape(slots, chips, cols).transpose(1, 0, 2)
        message = jnp.concatenate(
            [jnp.broadcast_to(attended[None], (chips, slots, kdim)), pieces], axis=2
        )
        got = lax.all_to_all(message, "dev", 0, 0, axis_index_groups=plane)
        got = got.reshape(chips * slots, kdim + cols)
        rows_in, hid = got[:, :kdim], got[:, kdim:]

        own = jnp.dot(rows_in, out_weight, preferred_element_type=F32).astype(BF16)
        oth = jnp.dot(rows_in, out_other, preferred_element_type=F32).astype(BF16)
        first = jnp.where(core == 0, own, oth)
        second = jnp.where(core == 0, oth, own)
        projected = jnp.concatenate([first, second], axis=1)
        residual = hid.astype(F32) + projected.astype(F32)
        gain = lax.dynamic_slice(ffn_gain, (chip * cols,), (cols,))
        sent = (residual * gain).astype(BF16)
        block = jnp.broadcast_to(sent[None], (peers,) + sent.shape)
        blocks = lax.all_to_all(block, ("grp", "dev"), 0, 0, axis_index_groups=cube)
        x = blocks.reshape(groups, chips, chips * slots, cols).transpose(0, 2, 1, 3)
        x = x.reshape(groups * chips * slots, width)

        res = x.astype(F32) / ffn_gain
        scale = lax.rsqrt(jnp.mean(res * res, axis=1, keepdims=True) + EPS)

        def wide(a, b):
            return jnp.concatenate(
                [jnp.dot(x, a, preferred_element_type=F32), jnp.dot(x, b, preferred_element_type=F32)], axis=1
            )

        gate_act = wide(gate_weight, gate_other) * scale
        up_act = wide(up_weight, up_other) * scale
        activated = (jax.nn.silu(gate_act) * up_act).astype(BF16)
        down = jnp.concatenate([down_weight, down_other], axis=1)
        partial = lax.dot_general(
            activated, down, (((1,), (1,)), ((), ())), preferred_element_type=F32
        ).astype(BF16)
        parts = lax.all_to_all(
            partial.reshape(peers, slots, width), ("grp", "dev"), 0, 0, axis_index_groups=cube
        )
        feed = jnp.sum(parts.astype(F32), axis=0)
        mine = lax.dynamic_slice(
            res, ((lax.axis_index("grp") * chips + chip) * slots, 0), (slots, width)
        )
        live_rows = (lengths > 0)[:, None]
        return jnp.where(live_rows, mine + feed, 0.0).astype(BF16)

    return shards


def solution(mesh):
    both = ("grp", "dev")
    in_specs = (
        P(both, None),
        P(both, None, None),
        P(both, None, None),
        P(both),
        P(both, None),
        P(None, "dev"),
        P(),
        P(None, both),
        P(None, both),
        P(None, both),
    )
    body = make_shards(mesh.shape["grp"], mesh.shape["dev"])
    return jax.shard_map(body, mesh=mesh, in_specs=in_specs, out_specs=P(both, None), check_vma=False)
```

time: 328 us -> 138 us (0.42)
  the two profiles are of different devices: /device:TPU:1 before, /device:TPU:0 now
where the time goes in v1:
time: 138 us; the launch traced here: 137 us
  waiting for transfers between devices  64.8 us (47%)
  matrix products  22.9 us (17%)
  starting transfers between devices  22.2 us (16%)
  local copies, waits for them, and re-layouts  17.1 us (12%)
  other arithmetic  9.42 us (7%)
    all_to_all x1, waiting for transfers between devices, shards(): blocks = lax.all_to_all(block, ('grp', 'dev'), 0, 0, axis_index_groups=cube)  27.5 us
    all_to_all x1, waiting for transfers between devices, shards(): lax.all_to_all(partial.reshape(peers, slots, width), ('grp', 'dev'), 0, 0...  25.8 us
    all_to_all x1, waiting for transfers between devices, shards(): got = lax.all_to_all(message, 'dev', 0, 0, axis_index_groups=plane)  11.4 us
    all_to_all x1, starting transfers between devices, shards(): got = lax.all_to_all(message, 'dev', 0, 0, axis_index_groups=plane)  8.13 us
    all_to_all x1, starting transfers between devices, shards(): blocks = lax.all_to_all(block, ('grp', 'dev'), 0, 0, axis_index_groups=cube)  7.41 us
    all_to_all x1, starting transfers between devices, shards(): lax.all_to_all(partial.reshape(peers, slots, width), ('grp', 'dev'), 0, 0...  5.98 us
    dot_general x2, matrix products, wide(): jnp.dot(x, b, preferred_element_type=F32)  4.85 us
    reshape x1, local copies, waits for them, and re-layouts, shards(): partial.reshape(peers, slots, width)  4.75 us
  transfers between devices with their start and end apart: 7, of which 3 were waited for; matrix products, arithmetic and copies ran while one was open for 22% of the time, Pallas kernels for 0%

profile of v1, /device:TPU:0, one launch (start us, length us, event | category | flops | bytes accessed | tf_op | source)
XLA Modules:
  0.0 136.7 jit_solution(13840488433950735975)
XLA Ops:
  0.0 0.0 copy-start
  0.0 0.0 collective-permute-start
  0.0 0.8 broadcast_maximum_fusion
  0.8 0.1 iota_compare_fusion
  0.9 0.7 copy-done
  1.6 1.5 %fusion.6 = f32[2,32,2048]{2,1,0:T(8,128)S(1)} fusion(bf16[2,2048,256]{2,1,0:T(8,128)(2,1)S(1)} %copy-done, pred[2,2048]{1,0:T(4,128)(4,1)S(1)} %iota_compare_fusion, bf16[1,2,32,256]{3,1,2,0:T(2,128)(2,1)} %bitcast.31), kind=kOutput, calls=%fused_computation.10 | convolution fusion | flops 67371008 | bytes 2658304 | tf_op jit(solution)/shard_map/shd,std->sht/dot_general | solution.py:16
  3.1 0.2 fusion.22
  3.3 2.1 %fusion.7 = bf16[1,2,32,256]{3,2,1,0:T(8,128)(2,1)S(1)} fusion(bf16[2,2048,256]{2,1,0:T(8,128)(2,1)} %param.12, f32[2,32]{1,0:T(2,128)S(1)} %fusion.22, f32[2,32,2048]{2,1,0:T(8,128)S(1)} %fusion.6), kind=kOutput, calls=%fused_computation.12 | convolution fusion | flops 67520576 | bytes 2654464 | tf_op jit(solution)/shard_map/sht,std->shd/dot_general | solution.py:25
  5.5 0.0 copy-start.3
  5.5 0.0 copy-done.4
  5.5 0.1 reshape.74
  5.7 0.4 broadcast_in_dim.46
  6.1 1.3 pad_maximum_fusion
  7.4 8.1 %all-to-all-start = ((bf16[16,2,8640]{2,1,0:T(2,128)(2,1)}), bf16[16,2,8640]{2,1,0:T(2,128)(2,1)S(1)}, u32[]{:S(2)}, u32[]{:S(2)}) async-start(bf16[16,2,8640]{2,1,0:T(2,128)(2,1)} %pad_maximum_fusion), calls=%async_computation | async-start | bytes 1114112 | tf_op jit(solution)/shard_map/all_to_all | solution.py:68
  15.6 0.1 dynamic_slice.6
  15.7 11.4 %all-to-all-done = bf16[16,2,8640]{2,1,0:T(2,128)(2,1)S(1)} async-done(((bf16[16,2,8640]{2,1,0:T(2,128)(2,1)}), bf16[16,2,8640]{2,1,0:T(2,128)(2,1)S(1)}, u32[]{:S(2)}, u32[]{:S(2)}) %all-to-all-start) | async-done | bytes 552992 | tf_op jit(solution)/shard_map/all_to_all | solution.py:68
  27.1 0.4 reshape.75
  27.5 3.3 %convolution_convert_fusion.3 = bf16[32,224]{1,0:T(8,128)(2,1)S(1)} fusion(bf16[8192,224]{0,1:T(8,128)(2,1)} %param.15, bf16[32,8640]{1,0:T(8,128)(2,1)S(1)} %reshape.75), kind=kOutput, calls=%fused_computation.14 | convolution fusion | flops 117447680 | bytes 4208640 | tf_op jit(solution)/shard_map/dot_general | solution.py:72
  30.7 0.0 collective-permute-done
  30.7 3.2 %broadcast_select_fusion.1 = (bf16[32,224]{1,0:T(8,128)(2,1)S(1)}, bf16[32,224]{1,0:T(8,128)(2,1)S(1)}) fusion(bf16[32,224]{1,0:T(8,128)(2,1)S(1)} %convolution_convert_fusion.3, pred[]{:T(512)S(6)} %eq.4, bf16[8192,224]{0,1:T(8,128)(2,1)} %collective-permute-done, bf16[32,8640]{1,0:T(8,128)(2,1)S(1)} %reshape.75), kind=kOutput, calls=%fused_computation.34 | convolution fusion | flops 117462016 | bytes 4239361 | tf_op jit(solution)/shard_map/dot_general | solution.py:73
  34.0 0.1 multiply_convert_fusion
  34.1 1.6 %broadcast_in_dim.47 = bf16[64,32,448]{2,1,0:T(8,128)(2,1)} broadcast(bf16[32,448]{1,0:T(8,128)(2,1)S(1)} %multiply_convert_fusion), dimensions={1,2} | broadcast | bytes 1863680 | tf_op jit(solution)/shard_map/broadcast_in_dim | solution.py:80
  35.6 7.4 %all-to-all-start.1 = ((bf16[64,32,448]{2,1,0:T(8,128)(2,1)}), bf16[64,32,448]{2,1,0:T(8,128)(2,1)}, u32[]{:S(2)}, u32[]{:S(2)}) async-start(bf16[64,32,448]{2,1,0:T(8,128)(2,1)} %broadcast_in_dim.47), calls=%async_computation.1 | async-start | bytes 4194304 | tf_op jit(solution)/shard_map/all_to_all | solution.py:81
  43.1 0.1 collective-permute-start.1
  43.2 0.5 collective-permute-start.2
  43.7 0.1 collective-permute-start.3
  43.8 0.1 div.47
  43.8 27.5 %all-to-all-done.1 = bf16[64,32,448]{2,1,0:T(8,128)(2,1)} async-done(((bf16[64,32,448]{2,1,0:T(8,128)(2,1)}), bf16[64,32,448]{2,1,0:T(8,128)(2,1)}, u32[]{:S(2)}, u32[]{:S(2)}) %all-to-all-start.1) | async-done | bytes 1835040 | tf_op jit(solution)/shard_map/all_to_all | solution.py:81
  71.4 4.1 %copy.14 = bf16[4,32,16,448]{3,2,1,0:T(8,128)(2,1)} copy(bf16[4,32,16,448]{3,1,2,0:T(8,128)(2,1)} %bitcast.2) | data formatting | bytes 3670016 | tf_op jit(solution)/shard_map/transpose | solution.py:82
  75.4 4.7 %reshape.77 = bf16[128,7168]{1,0:T(8,128)(2,1)} reshape(bf16[4,32,16,448]{3,2,1,0:T(8,128)(2,1)} %copy.14) | data formatting | bytes 3670016 | tf_op jit(solution)/shard_map/reshape | solution.py:83
  80.1 2.3 %multiply_reduce_fusion = f32[4,32]{1,0:T(4,128)S(1)} fusion(bf16[4,32,16,448]{3,1,2,0:T(8,128)(2,1)} %bitcast.2, f32[16,448]{1,0:T(8,128)S(1)} %div.47), kind=kLoop, calls=%fused_computation.2 | loop fusion | flops 3669888 | bytes 1864192 | tf_op jit(solution)/shard_map/reduce_sum | solution.py:86
  82.4 0.1 rsqrt.12
  82.5 3.0 %fusion.23 = f32[128,128]{0,1:T(8,128)S(1)} fusion(bf16[128,7168]{1,0:T(8,128)(2,1)} %reshape.77, bf16[7168,128]{1,0:T(8,128)(2,1)} %param.17), kind=kOutput, calls=%fused_computation.43 | convolution fusion | flops 234881024 | bytes 3735552 | tf_op jit(solution)/shard_map/dot_general | solution.py:90
  85.6 0.0 copy-done.1
  85.6 0.1 copy-done.2
  85.7 0.8 fusion.25
  86.5 0.0 collective-permute-done.1
  86.5 2.4 %fusion.24 = f32[128,128]{0,1:T(8,128)S(1)} fusion(bf16[128,7168]{1,0:T(8,128)(2,1)S(1)} %copy-done.1, bf16[7168,128]{1,0:T(8,128)(2,1)} %collective-permute-done.1), kind=kOutput, calls=%fused_computation.44 | convolution fusion | flops 234881024 | bytes 3735552 | tf_op jit(solution)/shard_map/dot_general | solution.py:90
  88.9 0.0 copy-start.5
  88.9 0.0 collective-permute-done.2
  88.9 2.5 %fusion.26 = f32[128,128]{0,1:T(8,128)S(1)} fusion(bf16[128,7168]{1,0:T(8,128)(2,1)S(1)} %copy-done.1, bf16[7168,128]{1,0:T(8,128)(2,1)} %collective-permute-done.2), kind=kOutput, calls=%fused_computation.46 | convolution fusion | flops 234881024 | bytes 3735552 | tf_op jit(solution)/shard_map/dot_general | solution.py:90
  91.4 0.0 collective-permute-done.3
  91.4 4.1 %convolution_convert_fusion = bf16[128,7168]{1,0:T(8,128)(2,1)} fusion(bf16[7168,128]{1,0:T(8,128)(2,1)} %collective-permute-done.3, bf16[7168,128]{1,0:T(8,128)(2,1)S(1)} %copy-done.5, f32[128,128]{0,1:T(8,128)S(1)} %fusion.26, f32[128,128]{0,1:T(8,128)S(1)} %fusion.25, f32[128,128]{0,1:T(8,128)S(1)} %fusion.24, f32[128,128]{0,1:T(8,128)S(1)} %fusion.23, ...), kind=kOutput, calls=%fused_computation.1 | convolution fusion | flops 478347264 | bytes 5767680 | tf_op jit(solution)/shard_map/dot_general | solution.py:97
  95.5 4.8 %reshape.78 = bf16[64,2,7168]{2,1,0:T(2,128)(2,1)} reshape(bf16[128,7168]{1,0:T(8,128)(2,1)} %convolution_convert_fusion) | data formatting | bytes 3670016 | tf_op jit(solution)/shard_map/reshape | solution.py:101
  100.3 6.0 %all-to-all-start.2 = ((bf16[64,2,7168]{2,1,0:T(2,128)(2,1)}), bf16[64,2,7168]{2,1,0:T(2,128)(2,1)}, u32[]{:S(2)}, u32[]{:S(2)}) async-start(bf16[64,2,7168]{2,1,0:T(2,128)(2,1)} %reshape.78), calls=%async_computation.2 | async-start | bytes 3670016 | tf_op jit(solution)/shard_map/all_to_all | solution.py:100
  106.3 25.8 %all-to-all-done.2 = bf16[64,2,7168]{2,1,0:T(2,128)(2,1)} async-done(((bf16[64,2,7168]{2,1,0:T(2,128)(2,1)}), bf16[64,2,7168]{2,1,0:T(2,128)(2,1)}, u32[]{:S(2)}, u32[]{:S(2)}) %all-to-all-start.2) | async-done | bytes 1835040 | tf_op jit(solution)/shard_map/all_to_all | solution.py:100
  132.1 3.0 %convert_reduce_fusion = f32[2,7168]{1,0:T(2,128)S(1)} fusion(bf16[64,2,7168]{2,1,0:T(2,128)(2,1)} %all-to-all-done.2), kind=kLoop, calls=%fused_computation.6 | loop fusion | flops 1820672 | bytes 1892352 | tf_op jit(solution)/shard_map/reduce_sum | solution.py:103
  135.1 1.6 %select_convert_fusion = bf16[2,7168]{1,0:T(2,128)(2,1)} fusion(pred[2]{0:T(512)(128)(4,1)S(1)} %broadcast_compare_fusion, f32[2,7168]{1,0:T(2,128)S(1)} %convert_reduce_fusion, f32[7168]{0:T(1024)S(1)} %copy-done.3, bf16[128,7168]{1,0:T(8,128)(2,1)} %reshape.77, s32[]{:T(128)S(6)} %select_n.31), kind=kLoop, calls=%fused_computation.28 | loop fusion | flops 71680 | bytes 143366 | tf_op jit(solution)/shard_map/convert_element_type | solution.py:108
  (11 shorter events, 0.1 us)
Async XLA Ops:
  0.0 1.6 %copy-start = (bf16[2,2048,256]{2,1,0:T(8,128)(2,1)S(1)}, bf16[2,2048,256]{2,1,0:T(8,128)(2,1)}, u32[]{:S(2)}) copy-start(bf16[2,2048,256]{2,1,0:T(8,128)(2,1)} %param.11) | copy-start | bytes 6291460
  0.0 30.7 %collective-permute-start = (bf16[8192,224]{0,1:T(8,128)(2,1)}, bf16[8192,224]{0,1:T(8,128)(2,1)}, u32[]{:S(2)}, u32[]{:S(2)}) collective-permute-start(bf16[8192,224]{0,1:T(8,128)(2,1)} %param.15), channel_id=1, source_target_pairs={{0,1},{1,0},{2,3},{3,2},{4,5},{5,4},{6,7},{7,6},{8,9},{9,8},{10,11... | collective-permute-start | bytes 11010056 | tf_op jit(solution)/shard_map/ppermute | solution.py:55
  3.3 2.2 %copy-start.4 = (bf16[2,7168]{1,0:T(2,128)(2,1)S(1)}, bf16[2,7168]{1,0:T(2,128)(2,1)}, u32[]{:S(2)}) copy-start(bf16[2,7168]{1,0:T(2,128)(2,1)} %param.14) | copy-start | bytes 86020
  5.5 10.1 %copy-start.3 = (f32[7168]{0:T(1024)S(1)}, f32[7168]{0:T(1024)}, u32[]{:S(2)}) copy-start(f32[7168]{0:T(1024)} %param.16) | copy-start | bytes 86020
  7.4 19.7 %all-to-all-start = ((bf16[16,2,8640]{2,1,0:T(2,128)(2,1)}), bf16[16,2,8640]{2,1,0:T(2,128)(2,1)S(1)}, u32[]{:S(2)}, u32[]{:S(2)}) async-start(bf16[16,2,8640]{2,1,0:T(2,128)(2,1)} %pad_maximum_fusion), calls=%async_computation | async-start | bytes 1114112 | tf_op jit(solution)/shard_map/all_to_all | solution.py:68
  35.6 35.7 %all-to-all-start.1 = ((bf16[64,32,448]{2,1,0:T(8,128)(2,1)}), bf16[64,32,448]{2,1,0:T(8,128)(2,1)}, u32[]{:S(2)}, u32[]{:S(2)}) async-start(bf16[64,32,448]{2,1,0:T(8,128)(2,1)} %broadcast_in_dim.47), calls=%async_computation.1 | async-start | bytes 4194304 | tf_op jit(solution)/shard_map/all_to_all | solution.py:81
  43.1 43.5 %collective-permute-start.1 = (bf16[7168,128]{1,0:T(8,128)(2,1)}, bf16[7168,128]{1,0:T(8,128)(2,1)}, u32[]{:S(2)}, u32[]{:S(2)}) collective-permute-start(bf16[7168,128]{1,0:T(8,128)(2,1)} %param.17), channel_id=1, source_target_pairs={{0,1},{1,0},{2,3},{3,2},{4,5},{5,4},{6,7},{7,6},{8,9},{9,8},{10,11... | collective-permute-start | bytes 5505032 | tf_op jit(solution)/shard_map/ppermute | solution.py:55
  43.2 45.8 %collective-permute-start.2 = (bf16[7168,128]{1,0:T(8,128)(2,1)}, bf16[7168,128]{1,0:T(8,128)(2,1)}, u32[]{:S(2)}, u32[]{:S(2)}) collective-permute-start(bf16[7168,128]{1,0:T(8,128)(2,1)} %param.18), channel_id=1, source_target_pairs={{0,1},{1,0},{2,3},{3,2},{4,5},{5,4},{6,7},{7,6},{8,9},{9,8},{10,11... | collective-permute-start | bytes 5505032 | tf_op jit(solution)/shard_map/ppermute | solution.py:55
  43.7 47.8 %collective-permute-start.3 = (bf16[7168,128]{1,0:T(8,128)(2,1)}, bf16[7168,128]{1,0:T(8,128)(2,1)}, u32[]{:S(2)}, u32[]{:S(2)}) collective-permute-start(bf16[7168,128]{1,0:T(8,128)(2,1)} %param.19), channel_id=1, source_target_pairs={{0,1},{1,0},{2,3},{3,2},{4,5},{5,4},{6,7},{7,6},{8,9},{9,8},{10,11... | collective-permute-start | bytes 5505032 | tf_op jit(solution)/shard_map/ppermute | solution.py:55
  82.5 3.0 %copy-start.1 = (bf16[128,7168]{1,0:T(8,128)(2,1)S(1)}, bf16[128,7168]{1,0:T(8,128)(2,1)}, u32[]{:S(2)}) copy-start(bf16[128,7168]{1,0:T(8,128)(2,1)} %reshape.77) | copy-start | bytes 5505028
  82.5 3.2 %copy-start.2 = (bf16[7168,128]{1,0:T(8,128)(2,1)S(1)}, bf16[7168,128]{1,0:T(8,128)(2,1)}, u32[]{:S(2)}) copy-start(bf16[7168,128]{1,0:T(8,128)(2,1)} %param.18) | copy-start | bytes 5505028
  88.9 2.5 %copy-start.5 = (bf16[7168,128]{1,0:T(8,128)(2,1)S(1)}, bf16[7168,128]{1,0:T(8,128)(2,1)}, u32[]{:S(2)}) copy-start(bf16[7168,128]{1,0:T(8,128)(2,1)} %param.19) | copy-start | bytes 5505028
  100.3 6.0 %copy-start.6 = (s32[2]{0:T(128)S(1)}, s32[2]{0:T(128)}, u32[]{:S(2)}) copy-start(s32[2]{0:T(128)} %param.13) | copy-start | bytes 28
  100.3 31.8 %all-to-all-start.2 = ((bf16[64,2,7168]{2,1,0:T(2,128)(2,1)}), bf16[64,2,7168]{2,1,0:T(2,128)(2,1)}, u32[]{:S(2)}, u32[]{:S(2)}) async-start(bf16[64,2,7168]{2,1,0:T(2,128)(2,1)} %reshape.78), calls=%async_computation.2 | async-start | bytes 3670016 | tf_op jit(solution)/shard_map/all_to_all | solution.py:100

commit v2 on v1

v2 whole, which is shorter than its diff:
```python
import functools

import jax
import jax.numpy as jnp
from jax import lax
from jax.experimental import pallas as pl
from jax.experimental.pallas import tpu as pltpu
from jax.sharding import PartitionSpec as P

BF16 = jnp.bfloat16
F32 = jnp.float32
EPS = 1e-05
NT = (((1,), (1,)), ((), ()))


def attend(query, key_cache, value_cache, lengths):
    slot_count = query.shape[0]
    head_dim = key_cache.shape[2]
    head_count = query.shape[1] // head_dim
    queries = query.reshape(slot_count, head_count, head_dim)
    scores = jnp.einsum(
        "shd,std->sht", queries, key_cache, preferred_element_type=jnp.float32
    ) * head_dim ** (-0.5)
    positions = lax.broadcasted_iota(jnp.int32, (1, 1, key_cache.shape[1]), 2)
    in_range = positions < jnp.maximum(lengths, 1)[:, None, None]
    scores = jnp.where(in_range, scores, -jnp.inf)
    highest = jnp.max(scores, axis=2, keepdims=True)
    weights = jnp.exp(scores - highest)
    probs = (weights / jnp.sum(weights, axis=2, keepdims=True)).astype(jnp.bfloat16)
    attended = jnp.einsum("sht,std->shd", probs, value_cache, preferred_element_type=jnp.float32)
    return attended.reshape(slot_count, head_count * head_dim).astype(jnp.bfloat16)


def project_kernel(steps, cols, x_ref, own_ref, oth_ref, hid_ref, gain_ref, out_ref, acc_own, acc_oth):
    k = pl.program_id(0)

    @pl.when(k == 0)
    def _():
        acc_own[...] = jnp.zeros_like(acc_own)
        acc_oth[...] = jnp.zeros_like(acc_oth)

    x = x_ref[...]
    acc_own[...] += lax.dot_general(x, own_ref[...], NT, preferred_element_type=F32)
    acc_oth[...] += lax.dot_general(x, oth_ref[...], NT, preferred_element_type=F32)

    @pl.when(k == steps - 1)
    def _():
        rows = x_ref.shape[0]
        pad = jnp.zeros((rows, 256 - cols), F32)

        def half(acc, at):
            projected = acc[...].astype(BF16).astype(F32)
            projected = jnp.concatenate([projected, pad], axis=1)
            return hid_ref[:, at : at + 256].astype(F32) + projected

        first, second = half(acc_own, 0), half(acc_oth, 256)
        squares = jnp.sum(first * first, axis=1, keepdims=True) + jnp.sum(
            second * second, axis=1, keepdims=True
        )
        high = squares.astype(BF16).astype(F32)
        low = squares - high
        lane = lax.broadcasted_iota(jnp.int32, (rows, 256), 1)
        sent = first * gain_ref[:, :256]
        sent = jnp.where(lane == cols, high, jnp.where(lane == cols + 1, low, sent))
        block = jnp.concatenate([sent, second * gain_ref[:, 256:]], axis=1).astype(BF16)
        for p in range(out_ref.shape[0]):
            out_ref[p] = block


def project(rows_in, hid, gain, out_own, out_oth, peers):
    rows = rows_in.shape[0]
    cols, depth = out_own.shape
    chunk = 2048
    steps = depth // chunk
    return pl.pallas_call(
        functools.partial(project_kernel, steps, cols),
        grid=(steps,),
        in_specs=[
            pl.BlockSpec((rows, chunk), lambda k: (0, k)),
            pl.BlockSpec((cols, chunk), lambda k: (0, k)),
            pl.BlockSpec((cols, chunk), lambda k: (0, k)),
            pl.BlockSpec((rows, 512), lambda k: (0, 0)),
            pl.BlockSpec((1, 512), lambda k: (0, 0)),
        ],
        out_specs=pl.BlockSpec((peers, rows, 512), lambda k: (0, 0, 0)),
        out_shape=jax.ShapeDtypeStruct((peers, rows, 512), BF16),
        scratch_shapes=[pltpu.VMEM((rows, cols), F32), pltpu.VMEM((rows, cols), F32)],
        compiler_params=pltpu.CompilerParams(vmem_limit_bytes=32 * 2**20),
        cost_estimate=pl.CostEstimate(
            flops=4 * rows * cols * depth, bytes_accessed=4 * cols * depth, transcendentals=0
        ),
    )(rows_in, out_own, out_oth, hid, gain)


def ffn_kernel(
    steps1, steps2, per1, per2, cols, width,
    core_ref, x_ref, go_ref, gx_ref, uo_ref, ux_ref, do_ref, dx_ref,
    out_ref, acc, sq, act, held,
):
    s = pl.program_id(0)
    groups, _, rows, _ = x_ref.shape
    total = groups * rows
    units = go_ref.shape[1]

    @pl.when(s == 0)
    def _():
        acc[...] = jnp.zeros_like(acc)
        sq[...] = jnp.zeros_like(sq)

    @pl.when(s < steps1)
    def _():
        core = core_ref[0]
        sums = acc[...]
        tails = sq[...]
        for b in range(per1):
            x = x_ref[:, b].reshape(total, 512)
            at_own = pl.multiple_of(2 * cols * b + cols * core, 32)
            at_oth = pl.multiple_of(2 * cols * b + cols * (1 - core), 32)
            for at, lo in ((at_own, 0), (at_oth, 256)):
                w = jnp.concatenate(
                    [r[pl.ds(at, cols), :] for r in (go_ref, gx_ref, uo_ref, ux_ref)], axis=1
                )
                sums += jnp.dot(x[:, lo : lo + cols], w, preferred_element_type=F32)
            tails += x[:, 128:256].astype(F32)
        acc[...] = sums
        sq[...] = tails

    @pl.when(s == steps1 - 1)
    def _():
        lane = lax.broadcasted_iota(jnp.int32, (total, 128), 1)
        keep = (lane == cols - 128) | (lane == cols - 127)
        squares = jnp.sum(jnp.where(keep, sq[...], 0.0), axis=1, keepdims=True)
        scale = lax.rsqrt(squares / width + EPS)
        gate = acc[:, : 2 * units] * scale
        up = acc[:, 2 * units :] * scale
        act[...] = (gate / (1.0 + jnp.exp(-gate)) * up).astype(BF16)

    @pl.when(s >= steps1)
    def _():
        span = held.shape[2]
        a = act[...]
        for b in range(per2):
            w = jnp.concatenate(
                [do_ref[b * span : (b + 1) * span, :], dx_ref[b * span : (b + 1) * span, :]], axis=1
            )
            y = lax.dot_general(a, w, NT, preferred_element_type=F32)
            held[(s - steps1) * per2 + b] = y.astype(BF16)

    @pl.when(s == steps1 + steps2 - 1)
    def _():
        spans, _, span = held.shape
        slots = 16 // spans
        r = lax.broadcasted_iota(jnp.int32, (128, 128), 0)
        q = lax.broadcasted_iota(jnp.int32, (128, 128), 1)
        peer, piece, slot = r // 16, (r // slots) % spans, r % slots
        order = jnp.where(q == piece * 16 + peer * slots + slot, 1.0, 0.0).astype(BF16)
        for g in range(total // 16):
            stack = jnp.concatenate([held[b, g * 16 : (g + 1) * 16, :] for b in range(spans)], axis=0)
            moved = jnp.dot(order, stack, preferred_element_type=F32).astype(BF16)
            out_ref[g * 8 : (g + 1) * 8] = moved.reshape(8, 16, span)


def feed_forward(core, blocks, gate, up, down, chips, slots):
    peers, rows, _ = blocks.shape
    groups = peers // chips
    total = groups * rows
    width, units = gate[0].shape
    cols = width // chips // 2
    per1, per2, spans = 4, 2, 16 // slots
    steps1, steps2 = chips // per1, spans // per2
    span = width // spans
    x = blocks.reshape(groups, chips, rows, 512)
    in1 = pl.BlockSpec((per1 * 2 * cols, units), lambda s: (jnp.minimum(s, steps1 - 1), 0))
    in2 = pl.BlockSpec((per2 * span, units), lambda s: (jnp.maximum(s - steps1, 0), 0))
    return pl.pallas_call(
        functools.partial(ffn_kernel, steps1, steps2, per1, per2, cols, width),
        grid=(steps1 + steps2,),
        in_specs=[
            pl.BlockSpec(memory_space=pltpu.SMEM),
            pl.BlockSpec((groups, per1, rows, 512), lambda s: (0, jnp.minimum(s, steps1 - 1), 0, 0)),
            in1, in1, in1, in1, in2, in2,
        ],
        out_specs=pl.BlockSpec((peers, 16, span), lambda s: (0, 0, 0)),
        out_shape=jax.ShapeDtypeStruct((peers, 16, span), BF16),
        scratch_shapes=[
            pltpu.VMEM((total, 4 * units), F32),
            pltpu.VMEM((total, 128), F32),
            pltpu.VMEM((total, 2 * units), BF16),
            pltpu.VMEM((spans, total, span), BF16),
        ],
        compiler_params=pltpu.CompilerParams(vmem_limit_bytes=40 * 2**20),
        cost_estimate=pl.CostEstimate(
            flops=12 * total * units * width, bytes_accessed=14 * width * units, transcendentals=0
        ),
    )(core, x, gate[0], gate[1], up[0], up[1], down[0], down[1])


def final_kernel(lengths_ref, parts_ref, res_ref, out_ref):
    total = res_ref[...]
    for p in range(parts_ref.shape[0]):
        total += parts_ref[p].astype(F32)
    row = lax.broadcasted_iota(jnp.int32, total.shape, 0)
    live = jnp.where(row % 2 == 0, lengths_ref[0], lengths_ref[1]) > 0
    out_ref[...] = jnp.where(live, total, 0.0).astype(BF16)


def finish(lengths, parts, res):
    vmem = pl.BlockSpec(memory_space=pltpu.VMEM)
    return pl.pallas_call(
        final_kernel,
        in_specs=[pl.BlockSpec(memory_space=pltpu.SMEM), vmem, vmem],
        out_specs=vmem,
        out_shape=jax.ShapeDtypeStruct(res.shape, BF16),
        compiler_params=pltpu.CompilerParams(vmem_limit_bytes=16 * 2**20),
    )(lengths, parts, res)


def make_shards(groups, devs):
    chips = devs // 2
    peers = groups * chips
    plane = [[2 * k + c for k in range(chips)] for c in range(2)]
    cube = [[2 * k + c for k in range(peers)] for c in range(2)]
    other = [(i, i ^ 1) for i in range(devs)]

    def shards(
        query,
        key_cache,
        value_cache,
        lengths,
        hidden,
        out_weight,
        ffn_gain,
        gate_weight,
        up_weight,
        down_weight,
    ):
        me = lax.axis_index("dev")
        core = lax.rem(me, 2)
        chip = lax.div(me, 2)
        slots, width = hidden.shape
        cols = width // devs

        def swap(w):
            return lax.ppermute(w, "dev", other)

        out_own = out_weight.T
        out_oth = swap(out_own)
        gate_oth = swap(gate_weight)
        up_oth = swap(up_weight)
        down_oth = swap(down_weight)

        def halves(v):
            v = v.reshape(v.shape[0], chips, 2, cols)
            v = jnp.where(core == 0, v, v[:, :, ::-1])
            return jnp.pad(v, ((0, 0), (0, 0), (0, 0), (0, 256 - cols))).reshape(v.shape[0], chips, 512)

        attended = attend(query, key_cache, value_cache, lengths)
        kdim = attended.shape[1]
        message = jnp.concatenate(
            [
                jnp.broadcast_to(attended[None], (chips, slots, kdim)),
                halves(hidden).transpose(1, 0, 2),
            ],
            axis=2,
        )
        got = lax.all_to_all(message, "dev", 0, 0, axis_index_groups=plane)
        got = got.reshape(chips * slots, kdim + 512)
        gains = halves(ffn_gain.reshape(1, width))
        gain = lax.dynamic_slice(gains, (0, chip, 0), (1, 1, 512)).reshape(1, 512)
        block = project(got, got[:, kdim:], gain, out_own, out_oth, peers)
        blocks = lax.all_to_all(block, ("grp", "dev"), 0, 0, axis_index_groups=cube)

        partial = feed_forward(
            core.reshape(1),
            blocks,
            (gate_weight, gate_oth),
            (up_weight, up_oth),
            (down_weight, down_oth),
            chips,
            slots,
        )
        parts = lax.all_to_all(partial, ("grp", "dev"), 0, 0, axis_index_groups=cube)

        mine = lax.dynamic_slice(
            blocks, (lax.axis_index("grp") * chips, chip * slots, 0), (chips, slots, 512)
        )
        mine = mine.reshape(chips, slots, 2, 256)[:, :, :, :cols].astype(F32)
        mine = jnp.where(core == 0, mine, mine[:, :, ::-1])
        mine = mine.transpose(1, 0, 2, 3).reshape(slots, width) / ffn_gain
        spans = 16 // slots
        mine = mine.reshape(slots, spans, width // spans).transpose(1, 0, 2).reshape(16, width // spans)
        out = finish(lengths, parts, mine)
        return out.reshape(spans, slots, width // spans).transpose(1, 0, 2).reshape(slots, width)

    return shards


def solution(mesh):
    both = ("grp", "dev")
    in_specs = (
        P(both, None),
        P(both, None, None),
        P(both, None, None),
        P(both),
        P(both, None),
        P(None, "dev"),
        P(),
        P(None, both),
        P(None, both),
        P(None, both),
    )
    body = make_shards(mesh.shape["grp"], mesh.shape["dev"])
    return jax.shard_map(body, mesh=mesh, in_specs=in_specs, out_specs=P(both, None), check_vma=False)
```

time: 138 us -> 125 us (0.906)
  matrix products: 22.9 us -> 3.6 us
  Pallas kernels: 0 us -> 12.9 us
  other arithmetic: 9.42 us -> 2.38 us
  local copies, waits for them, and re-layouts: 17.1 us -> 21.7 us
  waiting for transfers between devices: 64.8 us -> 61.1 us
    dot_general x7 -> x0, matrix products: 19.3 us -> none  [the longest x2 4.85 us: wide(): jnp.dot(x, b, preferred_element_type=F32)]
    unnamed x15 -> x31, local copies, waits for them, and re-layouts: 0.88 us -> 17.4 us
    pallas_call x0 -> x3, Pallas kernels: none -> 12.9 us  [the longest x1 6.16 us: feed_forward(): pl.pallas_call(functools.partial(ffn_kernel, steps1, steps2, per1, per2,...]
    all_to_all x1, waiting for transfers between devices: 27.5 us -> 18.3 us  [shards(): blocks = lax.all_to_all(block, ('grp', 'dev'), 0, 0, axis_index_groups=cube)]
    reshape x5 -> x10, local copies, waits for them, and re-layouts: 9.94 us -> 2.14 us  [the longest x1 1 us: halves(): v = v.reshape(v.shape[0], chips, 2, cols)]
    ppermute x4, waiting for transfers between devices: 0.02 us -> 6.16 us  [swap(): return lax.ppermute(w, 'dev', other)]
    reduce_sum x2 -> x0, other arithmetic: 5.28 us -> none  [the longest x1 2.98 us: shards(): feed = jnp.sum(parts.astype(F32), axis=0)]
    transpose x1, local copies, waits for them, and re-layouts: 4.08 us -> 0.03 us  [shards(): mine.reshape(slots, spans, width // spans).transpose(1, 0, 2)]
  transfers between devices with their start and end apart: 7 -> 7, of which waited for: 3 -> 6; matrix products, arithmetic and copies ran while one was open for 22% -> 8% of each run, Pallas kernels for 0% -> 0%
where the time goes in v2:
time: 125 us; the launch traced here: 124 us
  waiting for transfers between devices  61.1 us (49%)
  local copies, waits for them, and re-layouts  21.7 us (17%)
  starting transfers between devices  21.6 us (17%)
  Pallas kernels  12.9 us (10%)
  matrix products  3.6 us (3%)
  other arithmetic  2.38 us (2%)
    all_to_all x1, waiting for transfers between devices, shards(): lax.all_to_all(partial, ('grp', 'dev'), 0, 0, axis_index_groups=cube)  24.7 us
    all_to_all x1, waiting for transfers between devices, shards(): blocks = lax.all_to_all(block, ('grp', 'dev'), 0, 0, axis_index_groups=cube)  18.3 us
    unnamed x31, local copies, waits for them, and re-layouts  17.4 us
    all_to_all x1, waiting for transfers between devices, shards(): got = lax.all_to_all(message, 'dev', 0, 0, axis_index_groups=plane)  12 us
    all_to_all x1, starting transfers between devices, shards(): got = lax.all_to_all(message, 'dev', 0, 0, axis_index_groups=plane)  8.14 us
    all_to_all x1, starting transfers between devices, shards(): blocks = lax.all_to_all(block, ('grp', 'dev'), 0, 0, axis_index_groups=cube)  7.08 us
    ppermute x4, waiting for transfers between devices, swap(): return lax.ppermute(w, 'dev', other)  6.16 us
    pallas_call x1, Pallas kernels, feed_forward(): pl.pallas_call(functools.partial(ffn_kernel, steps1, steps2, per1, per2,...  6.16 us
  transfers between devices with their start and end apart: 7, of which 6 were waited for; matrix products, arithmetic and copies ran while one was open for 8% of the time, Pallas kernels for 0%

profile of v2, /device:TPU:0, one launch (start us, length us, event | category | flops | bytes accessed | tf_op | source)
XLA Modules:
  0.0 123.6 jit_solution(16371116379765342310)
XLA Ops:
  0.0 0.0 copy-start
  0.0 0.0 collective-permute-start
  0.0 1.0 reshape.79
  1.0 0.2 rev.9
  1.4 0.7 broadcast_maximum_fusion
  2.0 0.1 iota_compare_fusion
  2.1 1.5 %fusion.3 = f32[2,32,2048]{2,1,0:T(8,128)S(1)} fusion(bf16[2,2048,256]{2,1,0:T(8,128)(2,1)S(1)} %copy-done, pred[2,2048]{1,0:T(4,128)(4,1)S(1)} %iota_compare_fusion, bf16[1,2,32,256]{3,1,2,0:T(2,128)(2,1)} %bitcast.42), kind=kOutput, calls=%fused_computation.4 | convolution fusion | flops 67371008 | bytes 2658304 | tf_op jit(solution)/shard_map/shd,std->sht/dot_general | solution.py:21
  3.6 0.2 fusion.9
  3.9 2.1 %fusion.4 = bf16[1,2,32,256]{3,2,1,0:T(8,128)(2,1)S(1)} fusion(bf16[2,2048,256]{2,1,0:T(8,128)(2,1)} %param.12, f32[2,32]{1,0:T(2,128)S(1)} %fusion.9, f32[2,32,2048]{2,1,0:T(8,128)S(1)} %fusion.3), kind=kOutput, calls=%fused_computation.6 | convolution fusion | flops 67520576 | bytes 2654464 | tf_op jit(solution)/shard_map/sht,std->shd/dot_general | solution.py:30
  6.0 0.0 copy-start.14
  6.1 0.4 broadcast_in_dim.24
  6.5 1.3 %pad_maximum_fusion = bf16[16,2,8704]{2,1,0:T(2,128)(2,1)} fusion(bf16[16,2,512]{2,1,0:T(2,128)(2,1)S(1)} %bitcast.36, bf16[16,2,8192]{2,1,0:T(2,128)(2,1)S(1)} %broadcast_in_dim.24), kind=kLoop, calls=%fused_computation.7 | loop fusion | flops 1114112 | bytes 1114112 | tf_op jit(solution)/shard_map/concatenate | solution.py:259
  7.8 8.1 %all-to-all-start = ((bf16[16,2,8704]{2,1,0:T(2,128)(2,1)}), bf16[16,2,8704]{2,1,0:T(2,128)(2,1)S(1)}, u32[]{:S(2)}, u32[]{:S(2)}) async-start(bf16[16,2,8704]{2,1,0:T(2,128)(2,1)} %pad_maximum_fusion), calls=%async_computation | async-start | bytes 1114112 | tf_op jit(solution)/shard_map/all_to_all | solution.py:266
  15.9 0.1 reshape_reshape.3
  16.0 0.2 rev.10
  16.3 12.0 %all-to-all-done = bf16[16,2,8704]{2,1,0:T(2,128)(2,1)S(1)} async-done(((bf16[16,2,8704]{2,1,0:T(2,128)(2,1)}), bf16[16,2,8704]{2,1,0:T(2,128)(2,1)S(1)}, u32[]{:S(2)}, u32[]{:S(2)}) %all-to-all-start) | async-done | bytes 557088 | tf_op jit(solution)/shard_map/all_to_all | solution.py:266
  28.3 0.2 reshape.81.x_ref
  28.5 0.0 collective-permute-done.oth_ref
  28.5 0.0 copy-start.3
  28.5 2.0 %copy-done.3 = bf16[8192,224]{0,1:T(8,128)(2,1)S(1)} copy-done((bf16[8192,224]{0,1:T(8,128)(2,1)S(1)}, bf16[8192,224]{0,1:T(8,128)(2,1)}, u32[]{:S(2)}) %copy-start.3) | copy-done | bytes 3670040
  30.5 5.0 %shard_map.100 = bf16[64,32,512]{2,1,0:T(8,128)(2,1)S(1)} custom-call(bf16[32,8704]{1,0:T(8,128)(2,1)S(1)} %reshape.81.x_ref, bf16[224,8192]{1,0:T(8,128)(2,1)S(1)} %bitcast.33, bf16[224,8192]{1,0:T(8,128)(2,1)} %collective-permute-done.oth_ref, bf16[32,512]{1,0:T(8,128)(2,1)S(1)} %slice.8.hid_ref, f32[1,512]{1,0:T(1,128)S(1)} %dynamic-slice_bitcast_fusion.gain_ref), custom_call_target="tpu_custom_call" | custom-call | flops 234881024 | bytes 7340032 | tf_op jit(solution)/shard_map/pallas_call | solution.py:75
  35.5 1.3 %copy-done.1 = bf16[64,32,512]{2,1,0:T(8,128)(2,1)} copy-done((bf16[64,32,512]{2,1,0:T(8,128)(2,1)}, bf16[64,32,512]{2,1,0:T(8,128)(2,1)S(1)}, u32[]{:S(2)}) %copy-start.1) | copy-done | bytes 2097176
  36.9 7.1 %all-to-all-start.1 = ((bf16[64,32,512]{2,1,0:T(8,128)(2,1)}), bf16[64,32,512]{2,1,0:T(8,128)(2,1)}, u32[]{:S(2)}, u32[]{:S(2)}) async-start(bf16[64,32,512]{2,1,0:T(8,128)(2,1)} %copy-done.1), calls=%async_computation.1 | async-start | bytes 4194304 | tf_op jit(solution)/shard_map/all_to_all | solution.py:271
  44.0 0.1 collective-permute-start.1
  44.1 0.5 collective-permute-start.2
  44.5 0.1 collective-permute-start.3
  44.6 3.4 %collective-permute-done.1.gx_ref = bf16[7168,128]{1,0:T(8,128)(2,1)S(1)} collective-permute-done((bf16[7168,128]{1,0:T(8,128)(2,1)}, bf16[7168,128]{1,0:T(8,128)(2,1)S(1)}, u32[]{:S(2)}, u32[]{:S(2)}) %collective-permute-start.1) | collective-permute-done | bytes 1835040 | tf_op jit(solution)/shard_map/ppermute | solution.py:244
  48.0 1.2 %copy-done.7 = bf16[7168,128]{1,0:T(8,128)(2,1)} copy-done((bf16[7168,128]{1,0:T(8,128)(2,1)}, bf16[7168,128]{1,0:T(8,128)(2,1)S(1)}, u32[]{:S(2)}) %copy-start.7) | copy-done | bytes 1835032
  49.3 1.4 %collective-permute-done.2.ux_ref = bf16[7168,128]{1,0:T(8,128)(2,1)S(1)} collective-permute-done((bf16[7168,128]{1,0:T(8,128)(2,1)}, bf16[7168,128]{1,0:T(8,128)(2,1)S(1)}, u32[]{:S(2)}, u32[]{:S(2)}) %collective-permute-start.2) | collective-permute-done | bytes 1835040 | tf_op jit(solution)/shard_map/ppermute | solution.py:244
  50.7 1.2 copy-done.9
  51.9 1.4 %collective-permute-done.3.dx_ref = bf16[7168,128]{1,0:T(8,128)(2,1)S(1)} collective-permute-done((bf16[7168,128]{1,0:T(8,128)(2,1)}, bf16[7168,128]{1,0:T(8,128)(2,1)S(1)}, u32[]{:S(2)}, u32[]{:S(2)}) %collective-permute-start.3) | collective-permute-done | bytes 1835040 | tf_op jit(solution)/shard_map/ppermute | solution.py:244
  53.3 1.3 %copy-done.11 = bf16[7168,128]{1,0:T(8,128)(2,1)} copy-done((bf16[7168,128]{1,0:T(8,128)(2,1)}, bf16[7168,128]{1,0:T(8,128)(2,1)S(1)}, u32[]{:S(2)}) %copy-start.11) | copy-done | bytes 1835032
  54.6 18.3 %all-to-all-done.1 = bf16[64,32,512]{2,1,0:T(8,128)(2,1)} async-done(((bf16[64,32,512]{2,1,0:T(8,128)(2,1)}), bf16[64,32,512]{2,1,0:T(8,128)(2,1)}, u32[]{:S(2)}, u32[]{:S(2)}) %all-to-all-start.1) | async-done | bytes 2097184 | tf_op jit(solution)/shard_map/all_to_all | solution.py:271
  72.9 1.5 %copy-done.4 = bf16[7168,128]{1,0:T(8,128)(2,1)S(1)} copy-done((bf16[7168,128]{1,0:T(8,128)(2,1)S(1)}, bf16[7168,128]{1,0:T(8,128)(2,1)}, u32[]{:S(2)}) %copy-start.4) | copy-done | bytes 1835032
  74.4 1.5 %copy-done.5 = bf16[7168,128]{1,0:T(8,128)(2,1)S(1)} copy-done((bf16[7168,128]{1,0:T(8,128)(2,1)S(1)}, bf16[7168,128]{1,0:T(8,128)(2,1)}, u32[]{:S(2)}) %copy-start.5) | copy-done | bytes 1835032
  75.9 1.5 %copy-done.6 = bf16[7168,128]{1,0:T(8,128)(2,1)S(1)} copy-done((bf16[7168,128]{1,0:T(8,128)(2,1)S(1)}, bf16[7168,128]{1,0:T(8,128)(2,1)}, u32[]{:S(2)}) %copy-start.6) | copy-done | bytes 1835032
  77.4 1.5 %copy-done.8 = bf16[7168,128]{1,0:T(8,128)(2,1)S(1)} copy-done((bf16[7168,128]{1,0:T(8,128)(2,1)S(1)}, bf16[7168,128]{1,0:T(8,128)(2,1)}, u32[]{:S(2)}) %copy-start.8) | copy-done | bytes 1835032
  78.9 1.5 %copy-done.10 = bf16[7168,128]{1,0:T(8,128)(2,1)S(1)} copy-done((bf16[7168,128]{1,0:T(8,128)(2,1)S(1)}, bf16[7168,128]{1,0:T(8,128)(2,1)}, u32[]{:S(2)}) %copy-start.10) | copy-done | bytes 1835032
  80.4 1.5 %copy-done.12 = bf16[7168,128]{1,0:T(8,128)(2,1)S(1)} copy-done((bf16[7168,128]{1,0:T(8,128)(2,1)S(1)}, bf16[7168,128]{1,0:T(8,128)(2,1)}, u32[]{:S(2)}) %copy-start.12) | copy-done | bytes 1835032
  81.9 6.2 %shard_map.101 = bf16[64,16,896]{2,1,0:T(8,128)(2,1)S(1)} custom-call(s32[1]{0:T(128)} %bitcast.core_ref, bf16[4,16,32,512]{3,2,1,0:T(8,128)(2,1)} %bitcast.4.x_ref, bf16[7168,128]{1,0:T(8,128)(2,1)S(1)} %copy-done.4, bf16[7168,128]{1,0:T(8,128)(2,1)S(1)} %copy-done.8, bf16[7168,128]{1,0:T(8,128)(2,1)S(1)} %copy-done.5, bf16[7168,128]{1,0:T(8,128)(2,1)S(1)} %copy-done.10, ...), custom_call_target="tpu_custom_call" | custom-call | flops 1409286144 | bytes 12845056 | tf_op jit(solution)/shard_map/pallas_call | solution.py:175
  88.0 1.3 %copy-done.2 = bf16[64,16,896]{2,1,0:T(8,128)(2,1)} copy-done((bf16[64,16,896]{2,1,0:T(8,128)(2,1)}, bf16[64,16,896]{2,1,0:T(8,128)(2,1)S(1)}, u32[]{:S(2)}) %copy-start.2) | copy-done | bytes 1835032
  89.3 5.7 %all-to-all-start.2 = ((bf16[64,16,896]{2,1,0:T(8,128)(2,1)}), bf16[64,16,896]{2,1,0:T(8,128)(2,1)}, u32[]{:S(2)}, u32[]{:S(2)}) async-start(bf16[64,16,896]{2,1,0:T(8,128)(2,1)} %copy-done.2), calls=%async_computation.2 | async-start | bytes 3670016 | tf_op jit(solution)/shard_map/all_to_all | solution.py:282
  95.0 0.9 constant_dynamic-slice_fusion
  96.0 0.2 rev.11
  96.3 0.1 reshape.86
  96.5 24.7 %all-to-all-done.2.parts_ref = bf16[64,16,896]{2,1,0:T(8,128)(2,1)} async-done(((bf16[64,16,896]{2,1,0:T(8,128)(2,1)}), bf16[64,16,896]{2,1,0:T(8,128)(2,1)}, u32[]{:S(2)}, u32[]{:S(2)}) %all-to-all-start.2) | async-done | bytes 1835040 | tf_op jit(solution)/shard_map/all_to_all | solution.py:282
  121.2 1.8 %shard_map.102 = bf16[16,896]{1,0:T(8,128)(2,1)S(1)} custom-call(s32[2]{0:T(128)S(1)} %copy-done.13, bf16[64,16,896]{2,1,0:T(8,128)(2,1)} %all-to-all-done.2.parts_ref, f32[16,896]{1,0:T(8,128)S(1)} %reshape.87.res_ref), custom_call_target="tpu_custom_call" | custom-call | tf_op jit(solution)/shard_map/pallas_call | solution.py:209
  123.0 0.6 reshape.88
  (32 shorter events, 0.4 us)
Async XLA Ops:
  0.0 2.1 %copy-start = (bf16[2,2048,256]{2,1,0:T(8,128)(2,1)S(1)}, bf16[2,2048,256]{2,1,0:T(8,128)(2,1)}, u32[]{:S(2)}) copy-start(bf16[2,2048,256]{2,1,0:T(8,128)(2,1)} %param.11) | copy-start | bytes 6291460
  0.0 28.5 %collective-permute-start = (bf16[224,8192]{1,0:T(8,128)(2,1)}, bf16[224,8192]{1,0:T(8,128)(2,1)}, u32[]{:S(2)}, u32[]{:S(2)}) collective-permute-start(bf16[224,8192]{1,0:T(8,128)(2,1)} %bitcast.32), channel_id=1, source_target_pairs={{0,1},{1,0},{2,3},{3,2},{4,5},{5,4},{6,7},{7,6},{8,9},{9,8},{10,11... | collective-permute-start | bytes 11010056 | tf_op jit(solution)/shard_map/ppermute | solution.py:244
  6.0 9.9 %copy-start.14 = (f32[7168]{0:T(1024)S(1)}, f32[7168]{0:T(1024)}, u32[]{:S(2)}) copy-start(f32[7168]{0:T(1024)} %param.16) | copy-start | bytes 86020
  7.8 20.5 %all-to-all-start = ((bf16[16,2,8704]{2,1,0:T(2,128)(2,1)}), bf16[16,2,8704]{2,1,0:T(2,128)(2,1)S(1)}, u32[]{:S(2)}, u32[]{:S(2)}) async-start(bf16[16,2,8704]{2,1,0:T(2,128)(2,1)} %pad_maximum_fusion), calls=%async_computation | async-start | bytes 1114112 | tf_op jit(solution)/shard_map/all_to_all | solution.py:266
  28.5 2.0 %copy-start.3 = (bf16[8192,224]{0,1:T(8,128)(2,1)S(1)}, bf16[8192,224]{0,1:T(8,128)(2,1)}, u32[]{:S(2)}) copy-start(bf16[8192,224]{0,1:T(8,128)(2,1)} %param.15) | copy-start | bytes 11010052
  35.5 1.3 %copy-start.1 = (bf16[64,32,512]{2,1,0:T(8,128)(2,1)}, bf16[64,32,512]{2,1,0:T(8,128)(2,1)S(1)}, u32[]{:S(2)}) copy-start(bf16[64,32,512]{2,1,0:T(8,128)(2,1)S(1)} %shard_map.100) | copy-start | bytes 6291460
  36.9 36.0 %all-to-all-start.1 = ((bf16[64,32,512]{2,1,0:T(8,128)(2,1)}), bf16[64,32,512]{2,1,0:T(8,128)(2,1)}, u32[]{:S(2)}, u32[]{:S(2)}) async-start(bf16[64,32,512]{2,1,0:T(8,128)(2,1)} %copy-done.1), calls=%async_computation.1 | async-start | bytes 4194304 | tf_op jit(solution)/shard_map/all_to_all | solution.py:271
  44.0 4.1 %collective-permute-start.1 = (bf16[7168,128]{1,0:T(8,128)(2,1)}, bf16[7168,128]{1,0:T(8,128)(2,1)S(1)}, u32[]{:S(2)}, u32[]{:S(2)}) collective-permute-start(bf16[7168,128]{1,0:T(8,128)(2,1)} %go_ref.1), channel_id=1, source_target_pairs={{0,1},{1,0},{2,3},{3,2},{4,5},{5,4},{6,7},{7,6},{8,9},{9,8},{10,11... | collective-permute-start | bytes 5505032 | tf_op jit(solution)/shard_map/ppermute | solution.py:244
  44.1 6.6 %collective-permute-start.2 = (bf16[7168,128]{1,0:T(8,128)(2,1)}, bf16[7168,128]{1,0:T(8,128)(2,1)S(1)}, u32[]{:S(2)}, u32[]{:S(2)}) collective-permute-start(bf16[7168,128]{1,0:T(8,128)(2,1)} %uo_ref.1), channel_id=1, source_target_pairs={{0,1},{1,0},{2,3},{3,2},{4,5},{5,4},{6,7},{7,6},{8,9},{9,8},{10,11... | collective-permute-start | bytes 5505032 | tf_op jit(solution)/shard_map/ppermute | solution.py:244
  44.5 8.7 %collective-permute-start.3 = (bf16[7168,128]{1,0:T(8,128)(2,1)}, bf16[7168,128]{1,0:T(8,128)(2,1)S(1)}, u32[]{:S(2)}, u32[]{:S(2)}) collective-permute-start(bf16[7168,128]{1,0:T(8,128)(2,1)} %do_ref.1), channel_id=1, source_target_pairs={{0,1},{1,0},{2,3},{3,2},{4,5},{5,4},{6,7},{7,6},{8,9},{9,8},{10,11... | collective-permute-start | bytes 5505032 | tf_op jit(solution)/shard_map/ppermute | solution.py:244
  48.0 1.2 %copy-start.7 = (bf16[7168,128]{1,0:T(8,128)(2,1)}, bf16[7168,128]{1,0:T(8,128)(2,1)S(1)}, u32[]{:S(2)}) copy-start(bf16[7168,128]{1,0:T(8,128)(2,1)S(1)} %collective-permute-done.1.gx_ref) | copy-start | bytes 5505028
  50.7 1.2 copy-start.9
  53.3 1.3 %copy-start.11 = (bf16[7168,128]{1,0:T(8,128)(2,1)}, bf16[7168,128]{1,0:T(8,128)(2,1)S(1)}, u32[]{:S(2)}) copy-start(bf16[7168,128]{1,0:T(8,128)(2,1)S(1)} %collective-permute-done.3.dx_ref) | copy-start | bytes 5505028
  72.9 1.5 %copy-start.4 = (bf16[7168,128]{1,0:T(8,128)(2,1)S(1)}, bf16[7168,128]{1,0:T(8,128)(2,1)}, u32[]{:S(2)}) copy-start(bf16[7168,128]{1,0:T(8,128)(2,1)} %go_ref.1) | copy-start | bytes 5505028
  74.4 1.5 %copy-start.5 = (bf16[7168,128]{1,0:T(8,128)(2,1)S(1)}, bf16[7168,128]{1,0:T(8,128)(2,1)}, u32[]{:S(2)}) copy-start(bf16[7168,128]{1,0:T(8,128)(2,1)} %uo_ref.1) | copy-start | bytes 5505028
  75.9 1.5 %copy-start.6 = (bf16[7168,128]{1,0:T(8,128)(2,1)S(1)}, bf16[7168,128]{1,0:T(8,128)(2,1)}, u32[]{:S(2)}) copy-start(bf16[7168,128]{1,0:T(8,128)(2,1)} %do_ref.1) | copy-start | bytes 5505028
  77.4 1.5 %copy-start.8 = (bf16[7168,128]{1,0:T(8,128)(2,1)S(1)}, bf16[7168,128]{1,0:T(8,128)(2,1)}, u32[]{:S(2)}) copy-start(bf16[7168,128]{1,0:T(8,128)(2,1)} %copy-done.7) | copy-start | bytes 5505028
  78.9 1.5 %copy-start.10 = (bf16[7168,128]{1,0:T(8,128)(2,1)S(1)}, bf16[7168,128]{1,0:T(8,128)(2,1)}, u32[]{:S(2)}) copy-start(bf16[7168,128]{1,0:T(8,128)(2,1)} %copy-done.9) | copy-start | bytes 5505028
  80.4 1.5 %copy-start.12 = (bf16[7168,128]{1,0:T(8,128)(2,1)S(1)}, bf16[7168,128]{1,0:T(8,128)(2,1)}, u32[]{:S(2)}) copy-start(bf16[7168,128]{1,0:T(8,128)(2,1)} %copy-done.11) | copy-start | bytes 5505028
  88.0 1.3 %copy-start.2 = (bf16[64,16,896]{2,1,0:T(8,128)(2,1)}, bf16[64,16,896]{2,1,0:T(8,128)(2,1)S(1)}, u32[]{:S(2)}) copy-start(bf16[64,16,896]{2,1,0:T(8,128)(2,1)S(1)} %shard_map.101) | copy-start | bytes 5505028
  89.3 31.9 %copy-start.13 = (s32[2]{0:T(128)S(1)}, s32[2]{0:T(128)}, u32[]{:S(2)}) copy-start(s32[2]{0:T(128)} %lengths_ref.1) | copy-start | bytes 28
  89.3 31.9 %all-to-all-start.2 = ((bf16[64,16,896]{2,1,0:T(8,128)(2,1)}), bf16[64,16,896]{2,1,0:T(8,128)(2,1)}, u32[]{:S(2)}, u32[]{:S(2)}) async-start(bf16[64,16,896]{2,1,0:T(8,128)(2,1)} %copy-done.2), calls=%async_computation.2 | async-start | bytes 3670016 | tf_op jit(solution)/shard_map/all_to_all | solution.py:282

commit v3 on v1

v3 whole, which is shorter than its diff:
```python
import functools

import jax
import jax.numpy as jnp
from jax import lax
from jax.experimental import pallas as pl
from jax.experimental.pallas import tpu as pltpu
from jax.sharding import PartitionSpec as P

BF16 = jnp.bfloat16
F32 = jnp.float32
EPS = 1e-05
VMEM = 40 * 2**20
NT = (((1,), (1,)), ((), ()))


def attend_kernel(lengths_ref, q_ref, k_hbm, v_hbm, hid_ref, out_ref, keys, values, sems):
    slots, span, dim = keys.shape
    heads = q_ref.shape[1] // dim
    chips = out_ref.shape[0]
    copies = []
    for i, (src, dst) in enumerate(((k_hbm, keys), (v_hbm, values))):
        for s in range(slots):
            copy = pltpu.make_async_copy(src.at[s], dst.at[s], sems.at[i, s])
            copy.start()
            copies.append(copy)
    q = q_ref[...].astype(F32)
    q = jnp.concatenate(
        [q[s : s + 1, h * dim : (h + 1) * dim] for s in range(slots) for h in range(heads)], axis=0
    ).astype(BF16)
    hid = hid_ref[...].astype(F32)
    row = lax.broadcasted_iota(jnp.int32, (16, 128), 0)
    tiles = [
        jnp.where(row % slots == 0, hid[0:1, t * 128 : (t + 1) * 128], hid[1:2, t * 128 : (t + 1) * 128])
        for t in range(hid.shape[1] // 128)
    ]
    extra = []
    for p in range(chips):
        first = (p * hid.shape[1] // chips) // 128
        held = jnp.zeros((16, 128), F32)
        for i in range(4):
            held = jnp.where(row // slots == i, tiles[first + i], held)
        extra.append(held.astype(BF16))
    parts, totals = [], []
    position = lax.broadcasted_iota(jnp.int32, (heads, span), 1)
    for s in range(slots):
        copies[s].wait()
        scores = lax.dot_general(
            q[s * heads : (s + 1) * heads, :], keys[s], NT, preferred_element_type=F32
        ) * dim ** (-0.5)
        scores = jnp.where(position < jnp.maximum(lengths_ref[s], 1), scores, -jnp.inf)
        weights = jnp.exp(scores - jnp.max(scores, axis=1, keepdims=True))
        totals.append(jnp.sum(weights, axis=1, keepdims=True))
        parts.append(weights.astype(BF16))
    for s in range(slots):
        copies[slots + s].wait()
        attended = jnp.dot(parts[s], values[s], preferred_element_type=F32)
        parts[s] = (attended / totals[s]).astype(BF16)
    both = jnp.concatenate(parts, axis=0)
    pieces = 16 // slots
    per = heads // pieces
    r = lax.broadcasted_iota(jnp.int32, (16, slots * heads), 0)
    c = lax.broadcasted_iota(jnp.int32, (16, slots * heads), 1)
    rows = []
    for j in range(per):
        take = jnp.where(c == (r % slots) * heads + (r // slots) * per + j, 1.0, 0.0).astype(BF16)
        rows.append(jnp.dot(take, both, preferred_element_type=F32).astype(BF16))
    rows = jnp.concatenate(rows, axis=1)
    for p in range(chips):
        out_ref[p] = jnp.concatenate([rows, extra[p]], axis=1)


def attend(lengths, query, key_cache, value_cache, hidden, chips):
    slots, span, dim = key_cache.shape
    hbm = pl.BlockSpec(memory_space=pl.ANY)
    vmem = pl.BlockSpec(memory_space=pltpu.VMEM)
    lanes = query.shape[1] * slots // 16 + 128
    return pl.pallas_call(
        attend_kernel,
        in_specs=[pl.BlockSpec(memory_space=pltpu.SMEM), vmem, hbm, hbm, vmem],
        out_specs=vmem,
        out_shape=pltpu.HBM((chips, 16, lanes), BF16),
        scratch_shapes=[
            pltpu.VMEM(key_cache.shape, BF16),
            pltpu.VMEM(value_cache.shape, BF16),
            pltpu.SemaphoreType.DMA((2, slots)),
        ],
        compiler_params=pltpu.CompilerParams(vmem_limit_bytes=58 * 2**20),
    )(lengths, query, key_cache, value_cache, hidden)


def project_kernel(
    cols, where_ref, x_hbm, own_hbm, oth_hbm, gain_ref, out_hbm, x_buf, own, oth, block, sems, out_sem
):
    chips, deep, lanes = x_buf.shape
    depth = own.shape[1]
    slots = 2
    pieces = deep // slots
    rows = chips * slots
    cut = 128
    first = pltpu.make_async_copy(x_hbm, x_buf, sems.at[0])
    copies = [
        pltpu.make_async_copy(src.at[span], dst.at[span], sems.at[1 + 2 * i + j])
        for i, (src, dst) in enumerate(((own_hbm, own), (oth_hbm, oth)))
        for j, span in enumerate((pl.ds(0, cut), pl.ds(cut, cols - cut)))
    ]
    first.start()
    copies[0].start()
    copies[1].start()
    r = lax.broadcasted_iota(jnp.int32, (chips * deep, chips * deep), 0)
    c = lax.broadcasted_iota(jnp.int32, (chips * deep, chips * deep), 1)
    order = c == (r % rows) // slots * deep + r // rows * slots + r % slots
    order = jnp.where(order, 1.0, 0.0).astype(BF16)
    first.wait()
    x = jnp.dot(order, x_buf[...].reshape(chips * deep, lanes), preferred_element_type=F32)
    wide = depth // pieces
    chip = where_ref[1]
    lane = lax.broadcasted_iota(jnp.int32, (rows, 128), 1)

    def ahead(tiles, shift):
        moved = [pltpu.roll(t, 128 - shift, 1) for t in tiles]
        return [jnp.where(lane < 128 - shift, a, b) for a, b in zip(moved, moved[1:] + moved[-1:])]

    hids = [x[i * rows : (i + 1) * rows, wide : wide + 128] for i in range(4)]
    hids = [jnp.where(chip % 2 == 0, a, b) for a, b in zip(hids, ahead(hids, 64))]
    hid_a = jnp.concatenate(hids[:2], axis=1)
    hid_b = jnp.concatenate(ahead(hids[1:], cols - 128)[:2], axis=1)
    x = jnp.concatenate([x[i * rows : (i + 1) * rows, :wide] for i in range(pieces)], axis=1).astype(BF16)
    copies[0].wait()
    copies[2].start()
    copies[1].wait()
    copies[3].start()
    sums = [lax.dot_general(x, own[...], NT, preferred_element_type=F32)]
    copies[2].wait()
    copies[3].wait()
    sums.append(lax.dot_general(x, oth[...], NT, preferred_element_type=F32))
    pad = jnp.zeros((rows, 256 - cols), F32)
    swapped = where_ref[0] == 1
    hids = (jnp.where(swapped, hid_b, hid_a), jnp.where(swapped, hid_a, hid_b))
    gains = gain_ref[pl.ds(chip, 1), :]
    sent = []
    for i in range(2):
        projected = jnp.concatenate([sums[i].astype(BF16).astype(F32), pad], axis=1)
        sent.append((hids[i] + projected) * gains[:, 256 * i : 256 * i + 256])
    own_tail, oth_tail = sent[0][:, 128:], sent[1][:, 128:]
    third = jnp.where(lane < cols - 128, own_tail, pltpu.roll(oth_tail, cols - 128, 1))
    rest = pltpu.roll(oth_tail, 128 - (256 - cols), 1)
    turned = pltpu.roll(rest, 64, 1)
    half = rows // 2
    low = lax.broadcasted_iota(jnp.int32, (half, 128), 1) < 64
    even = jnp.where(low, rest[:half], turned[half:])
    odd = jnp.where(low, rest[half:], turned[:half])
    last = jnp.where(chip % 2 == 0, even, odd)
    packed = jnp.concatenate([sent[0][:, :128], sent[1][:, :128], third, last], axis=0).astype(BF16)
    copies = block.shape[0]
    for p in range(copies):
        block[p] = packed
    outs = []
    for p in range(out_hbm.shape[0] // copies):
        out = pltpu.make_async_copy(block, out_hbm.at[pl.ds(p * copies, copies)], out_sem.at[p])
        out.start()
        outs.append(out)
    for out in outs:
        out.wait()


def in_hbm(v):
    return pltpu.with_memory_space_constraint(v, pltpu.HBM)


def project(where, messages, gains, out_own, out_oth, peers):
    cols, depth = out_own.shape
    rows = messages.shape[0] * 2
    packed = rows * 2 * cols // 128
    hbm = pl.BlockSpec(memory_space=pl.ANY)
    vmem = pl.BlockSpec(memory_space=pltpu.VMEM)
    return pl.pallas_call(
        functools.partial(project_kernel, cols),
        in_specs=[pl.BlockSpec(memory_space=pltpu.SMEM), hbm, hbm, hbm, vmem],
        out_specs=hbm,
        out_shape=pltpu.HBM((peers, packed, 128), BF16),
        scratch_shapes=[
            pltpu.VMEM(messages.shape, BF16),
            pltpu.VMEM((cols, depth), BF16),
            pltpu.VMEM((cols, depth), BF16),
            pltpu.VMEM((8, packed, 128), BF16),
            pltpu.SemaphoreType.DMA((5,)),
            pltpu.SemaphoreType.DMA((peers // 8,)),
        ],
        compiler_params=pltpu.CompilerParams(vmem_limit_bytes=VMEM),
        cost_estimate=pl.CostEstimate(
            flops=4 * rows * cols * depth, bytes_accessed=4 * cols * depth, transcendentals=0
        ),
    )(where, messages, in_hbm(out_own), in_hbm(out_oth), gains)


def ffn_kernel(
    chips, cols, width,
    where_ref, x_hbm, go_hbm, gx_hbm, uo_hbm, ux_hbm, do_hbm, dx_hbm, ig_ref, out_hbm,
    x_buf, wide, down, held, out_buf, x_sem, wide_sem, down_sem, out_sem,
):
    groups, _, packed, _ = x_buf.shape
    rows = packed * 128 // (2 * cols)
    total = groups * rows
    units = wide.shape[2]
    quarter = 4
    parts = chips // quarter
    deep = quarter * 2 * cols
    core = where_ref[0]

    spans, _, span = held.shape
    stages = []
    for q in range(parts):
        chip_span, deep_span = pl.ds(q * quarter, quarter), pl.ds(q * deep, deep)
        stages.append(
            [pltpu.make_async_copy(x_hbm.at[:, chip_span], x_buf.at[:, chip_span], x_sem.at[q])]
            + [
                pltpu.make_async_copy(src.at[deep_span], wide.at[i, deep_span], wide_sem.at[i, q])
                for i, src in enumerate((go_hbm, gx_hbm, uo_hbm, ux_hbm))
            ]
        )
    for q in range(parts):
        some = pl.ds(q * deep, deep)
        stages.append(
            [
                pltpu.make_async_copy(src.at[some], down.at[i, some], down_sem.at[i, q])
                for i, src in enumerate((do_hbm, dx_hbm))
            ]
        )

    def begin(k):
        for copy in stages[k]:
            copy.start()

    def arrive(k):
        for copy in stages[k]:
            copy.wait()
        if k + parts < len(stages):
            begin(k + parts)

    for k in range(parts):
        begin(k)

    sums = jnp.zeros((total, 4 * units), F32)
    squares = jnp.zeros((total, 128), F32)
    half = rows // 2
    low = lax.broadcasted_iota(jnp.int32, (groups, half, 128), 2) < 64
    for q in range(parts):
        arrive(q)

        def weights(at, size):
            return jnp.concatenate([wide[i, pl.ds(at, size), :] for i in range(4)], axis=1)

        tiles, stacks = [], []
        for b in range(q * quarter, (q + 1) * quarter):
            own = pl.multiple_of(2 * cols * b + cols * core, 32)
            oth = pl.multiple_of(2 * cols * b + cols * (1 - core), 32)
            tiles += [x_buf[:, b, i * rows : (i + 1) * rows, :].reshape(total, 128) for i in range(3)]
            stacks += [
                weights(own, 128),
                weights(oth, 128),
                weights(pl.multiple_of(own + 128, 32), cols - 128),
                weights(pl.multiple_of(oth + 128, 32), 256 - cols),
            ]
        for b in range(q * quarter, (q + 1) * quarter, 2):
            first, second = (x_buf[:, b + i, 3 * rows :, :].astype(F32) for i in range(2))
            top = jnp.where(low, first, second)
            bottom = jnp.where(low, second, first)
            bottom = pltpu.roll(bottom.reshape(groups * half, 128), 64, 1).reshape(groups, half, 128)
            tiles.append(jnp.concatenate([top, bottom], axis=1).reshape(total, 128).astype(BF16))
            for i in range(2):
                oth = pl.multiple_of(2 * cols * (b + i) + cols * (1 - core) + (384 - cols), 32)
                stacks.append(weights(oth, 2 * cols - 384))
        x = jnp.concatenate(tiles, axis=1)
        sums += jnp.dot(x, jnp.concatenate(stacks, axis=0), preferred_element_type=F32)
        for i, tile in enumerate(tiles):
            res = tile.astype(F32) * ig_ref[q * len(tiles) + i : q * len(tiles) + i + 1, :]
            squares += res * res

    scale = lax.rsqrt(jnp.sum(squares, axis=1, keepdims=True) / width + EPS)
    gate = sums[:, : 2 * units] * scale
    up = sums[:, 2 * units :] * scale
    act = (gate / (1.0 + jnp.exp(-gate)) * up).astype(BF16)

    for b in range(spans):
        if b % (spans // parts) == 0:
            arrive(parts + b // (spans // parts))
        some = slice(b * span, (b + 1) * span)
        w = jnp.concatenate([down[0, some, :], down[1, some, :]], axis=1)
        held[b] = lax.dot_general(act, w, NT, preferred_element_type=F32).astype(BF16)

    r = lax.broadcasted_iota(jnp.int32, (128, 128), 0)
    c = lax.broadcasted_iota(jnp.int32, (128, 128), 1)
    peer, piece, slot = r // 16, (r // 2) % spans, r % 2
    order = jnp.where(c == piece * 16 + peer * 2 + slot, 1.0, 0.0).astype(BF16)
    outs = []
    for g in range(total // 16):
        stack = jnp.concatenate([held[b, g * 16 : (g + 1) * 16, :] for b in range(spans)], axis=0)
        moved = jnp.dot(order, stack, preferred_element_type=F32).astype(BF16)
        some = pl.ds(g * 8, 8)
        out_buf[g * 8 : (g + 1) * 8] = moved.reshape(8, 16, span)
        outs.append(pltpu.make_async_copy(out_buf.at[some], out_hbm.at[some], out_sem.at[g]))
        outs[-1].start()
    for out in outs:
        out.wait()


def feed_forward(where, blocks, gate, up, down, inverse_gain, chips):
    peers, packed, _ = blocks.shape
    groups = peers // chips
    width, units = gate[0].shape
    cols = width // chips // 2
    rows = packed * 128 // (2 * cols)
    total = groups * rows
    spans, parts = 8, 4
    span = width // spans
    hbm = pl.BlockSpec(memory_space=pl.ANY)
    return pl.pallas_call(
        functools.partial(ffn_kernel, chips, cols, width),
        in_specs=[pl.BlockSpec(memory_space=pltpu.SMEM)]
        + [hbm] * 7
        + [pl.BlockSpec(memory_space=pltpu.VMEM)],
        out_specs=hbm,
        out_shape=pltpu.HBM((peers, 16, span), BF16),
        scratch_shapes=[
            pltpu.VMEM((groups, chips, packed, 128), BF16),
            pltpu.VMEM((4, width, units), BF16),
            pltpu.VMEM((2, width, units), BF16),
            pltpu.VMEM((spans, total, span), BF16),
            pltpu.VMEM((peers, 16, span), BF16),
            pltpu.SemaphoreType.DMA((parts,)),
            pltpu.SemaphoreType.DMA((4, parts)),
            pltpu.SemaphoreType.DMA((2, parts)),
            pltpu.SemaphoreType.DMA((total // 16,)),
        ],
        compiler_params=pltpu.CompilerParams(vmem_limit_bytes=VMEM),
        cost_estimate=pl.CostEstimate(
            flops=12 * total * units * width, bytes_accessed=14 * width * units, transcendentals=0
        ),
    )(
        where,
        blocks.reshape(groups, chips, packed, 128),
        *[in_hbm(v) for v in (*gate, *up, *down)],
        inverse_gain,
    )


def final_kernel(lengths_ref, parts_hbm, res_ref, out_ref, parts, sems):
    quarter = parts.shape[0] // 4
    copies = []
    for q in range(4):
        some = pl.ds(q * quarter, quarter)
        copies.append(pltpu.make_async_copy(parts_hbm.at[some], parts.at[some], sems.at[q]))
        copies[q].start()
    total = res_ref[...]
    for q in range(4):
        copies[q].wait()
        for p in range(q * quarter, (q + 1) * quarter):
            total += parts[p].astype(F32)
    row = lax.broadcasted_iota(jnp.int32, total.shape, 0)
    live = jnp.where(row % 2 == 0, lengths_ref[0], lengths_ref[1]) > 0
    out_ref[...] = jnp.where(live, total, 0.0).astype(BF16)


def finish(lengths, parts, res):
    vmem = pl.BlockSpec(memory_space=pltpu.VMEM)
    return pl.pallas_call(
        final_kernel,
        in_specs=[pl.BlockSpec(memory_space=pltpu.SMEM), pl.BlockSpec(memory_space=pl.ANY), vmem],
        out_specs=vmem,
        out_shape=jax.ShapeDtypeStruct(res.shape, BF16),
        scratch_shapes=[pltpu.VMEM(parts.shape, BF16), pltpu.SemaphoreType.DMA((4,))],
        compiler_params=pltpu.CompilerParams(vmem_limit_bytes=16 * 2**20),
    )(lengths, parts, res)


def make_shards(groups, devs):
    chips = devs // 2
    peers = groups * chips
    plane = [[2 * k + c for k in range(chips)] for c in range(2)]
    cube = [[2 * k + c for k in range(peers)] for c in range(2)]
    other = [(i, i ^ 1) for i in range(devs)]

    def shards(
        query,
        key_cache,
        value_cache,
        lengths,
        hidden,
        out_weight,
        ffn_gain,
        gate_weight,
        up_weight,
        down_weight,
    ):
        me = lax.axis_index("dev")
        core = lax.rem(me, 2)
        chip = lax.div(me, 2)
        slots, width = hidden.shape
        cols = width // devs

        def swap(w):
            return lax.ppermute(w, "dev", other)

        out_own = out_weight.T
        out_oth = swap(out_own)
        gate_oth = swap(gate_weight)
        up_oth = swap(up_weight)
        down_oth = swap(down_weight)

        where = jnp.stack([core, chip]).astype(jnp.int32)

        def halves(v):
            v = v.reshape(v.shape[0], chips, 2, cols)
            return jnp.pad(v, ((0, 0), (0, 0), (0, 0), (0, 256 - cols)))

        message = attend(lengths, query, key_cache, value_cache, hidden, chips)
        got = lax.all_to_all(message, "dev", 0, 0, axis_index_groups=plane)
        gain = halves(ffn_gain.reshape(1, width))[0]
        gain = jnp.where(core == 0, gain, gain[:, ::-1])
        block = project(where, got, gain.reshape(chips, 512), out_own, out_oth, peers)
        blocks = lax.all_to_all(block, ("grp", "dev"), 0, 0, axis_index_groups=cube)

        inv = 1.0 / gain
        inv = jnp.concatenate(
            [
                jnp.stack(
                    [
                        inv[:, 0, :128],
                        inv[:, 1, :128],
                        jnp.concatenate([inv[:, 0, 128:cols], inv[:, 1, 128 : 384 - cols]], axis=1),
                    ],
                    axis=1,
                ).reshape(chips // 4, 12, 128),
                inv[:, 1, 384 - cols : cols].reshape(chips // 4, 2, 128),
            ],
            axis=1,
        ).reshape(width // 128, 128)
        partial = feed_forward(
            where,
            blocks,
            (gate_weight, gate_oth),
            (up_weight, up_oth),
            (down_weight, down_oth),
            inv,
            chips,
        )
        parts = lax.all_to_all(partial, ("grp", "dev"), 0, 0, axis_index_groups=cube)

        rows = chips * slots
        mine = lax.dynamic_slice(
            blocks, (lax.axis_index("grp") * chips, 0, 0), (chips,) + blocks.shape[1:]
        )
        full = lax.dynamic_slice(
            mine[:, : 3 * rows].reshape(chips, 3, rows, 128), (0, 0, chip * slots, 0), (chips, 3, slots, 128)
        )
        last = mine[:, 3 * rows :].reshape(chips // 2, 2, rows // 2, 2, 64)
        last = jnp.stack([last[:, 0], last[:, 1, :, ::-1]], axis=1)
        last = last.transpose(0, 1, 3, 2, 4).reshape(chips, rows, 64)
        last = lax.dynamic_slice(last, (0, chip * slots, 0), (chips, slots, 64))
        own = jnp.concatenate([full[:, 0], full[:, 2, :, : cols - 128]], axis=2)
        oth = jnp.concatenate([full[:, 1], full[:, 2, :, cols - 128 :], last], axis=2)
        mine = jnp.stack([jnp.where(core == 0, own, oth), jnp.where(core == 0, oth, own)], axis=2)
        mine = mine.astype(F32).transpose(1, 0, 2, 3).reshape(slots, width) / ffn_gain
        spans = 16 // slots
        mine = mine.reshape(slots, spans, width // spans).transpose(1, 0, 2).reshape(16, width // spans)
        out = finish(lengths, parts, mine)
        return out.reshape(spans, slots, width // spans).transpose(1, 0, 2).reshape(slots, width)

    return shards


def solution(mesh):
    both = ("grp", "dev")
    in_specs = (
        P(both, None),
        P(both, None, None),
        P(both, None, None),
        P(both),
        P(both, None),
        P(None, "dev"),
        P(),
        P(None, both),
        P(None, both),
        P(None, both),
    )
    body = make_shards(mesh.shape["grp"], mesh.shape["dev"])
    return jax.shard_map(body, mesh=mesh, in_specs=in_specs, out_specs=P(both, None), check_vma=False)
```

time: 138 us -> 110 us (0.80)
  matrix products: 22.9 us -> 0 us
  Pallas kernels: 0 us -> 22.9 us
  local copies, waits for them, and re-layouts: 17.1 us -> 1.85 us
  other arithmetic: 9.42 us -> 0.35 us
  waiting for transfers between devices: 64.8 us -> 62.6 us
    dot_general x9 -> x0, matrix products: 22.9 us -> none  [the longest x2 4.85 us: wide(): jnp.dot(x, b, preferred_element_type=F32)]
    pallas_call x0 -> x4, Pallas kernels: none -> 22.9 us  [the longest x1 8.2 us: project(): pl.pallas_call(functools.partial(project_kernel, cols), in_specs=[pl.Bloc...]
    reshape x5 -> x7, local copies, waits for them, and re-layouts: 9.94 us -> 0.97 us  [the longest x1 0.63 us: shards(): out.reshape(spans, slots, width // spans).transpose(1, 0, 2)]
    reduce_sum x2 -> x0, other arithmetic: 5.28 us -> none  [the longest x1 2.98 us: shards(): feed = jnp.sum(parts.astype(F32), axis=0)]
    transpose x1, local copies, waits for them, and re-layouts: 4.08 us -> 0.03 us  [shards(): mine.reshape(slots, spans, width // spans).transpose(1, 0, 2)]
    broadcast_in_dim x2 -> x0, local copies, waits for them, and re-layouts: 1.97 us -> none  [the longest x1 1.57 us: shards(): block = jnp.broadcast_to(sent[None], (peers,) + sent.shape)]
    convert_element_type x2 -> x0, other arithmetic: 1.68 us -> none  [the longest x1 1.6 us: shards(): return jnp.where(live_rows, mine + feed, 0.0).astype(BF16)]
    all_to_all x1, waiting for transfers between devices: 27.5 us -> 26 us  [shards(): blocks = lax.all_to_all(block, ('grp', 'dev'), 0, 0, axis_index_groups=cube)]
  transfers between devices with their start and end apart: 7 -> 7, of which waited for: 3 -> 3; matrix products, arithmetic and copies ran while one was open for 22% -> 1% of each run, Pallas kernels for 0% -> 12%
where the time goes in v3:
time: 110 us; the launch traced here: 109 us
  waiting for transfers between devices  62.6 us (57%)
  Pallas kernels  22.9 us (21%)
  starting transfers between devices  21.4 us (19%)
  local copies, waits for them, and re-layouts  1.85 us (2%)
    all_to_all x1, waiting for transfers between devices, shards(): blocks = lax.all_to_all(block, ('grp', 'dev'), 0, 0, axis_index_groups=cube)  26 us
    all_to_all x1, waiting for transfers between devices, shards(): lax.all_to_all(partial, ('grp', 'dev'), 0, 0, axis_index_groups=cube)  25 us
    all_to_all x1, waiting for transfers between devices, shards(): got = lax.all_to_all(message, 'dev', 0, 0, axis_index_groups=plane)  11.7 us
    pallas_call x1, Pallas kernels, project(): pl.pallas_call(functools.partial(project_kernel, cols), in_specs=[pl.Bloc...  8.2 us
    all_to_all x1, starting transfers between devices, shards(): got = lax.all_to_all(message, 'dev', 0, 0, axis_index_groups=plane)  8.14 us
    pallas_call x1, Pallas kernels, feed_forward(): pl.pallas_call(functools.partial(ffn_kernel, chips, cols, width), in_spec...  7.54 us
    all_to_all x1, starting transfers between devices, shards(): blocks = lax.all_to_all(block, ('grp', 'dev'), 0, 0, axis_index_groups=cube)  6.92 us
    all_to_all x1, starting transfers between devices, shards(): lax.all_to_all(partial, ('grp', 'dev'), 0, 0, axis_index_groups=cube)  5.53 us
  transfers between devices with their start and end apart: 7, of which 3 were waited for; matrix products, arithmetic and copies ran while one was open for 1% of the time, Pallas kernels for 12%

profile of v3, /device:TPU:0, one launch (start us, length us, event | category | flops | bytes accessed | tf_op | source)
XLA Modules:
  0.0 109.4 jit_solution(11546876473744682848)
XLA Ops:
  0.0 0.0 copy-start.1
  0.0 0.0 collective-permute-start
  0.0 5.0 %shard_map.100 = bf16[16,16,1152]{2,1,0:T(8,128)(2,1)} custom-call(s32[2]{0:T(128)} %lengths_ref.3, bf16[2,8192]{1,0:T(2,128)(2,1)} %q_ref.1, bf16[2,2048,256]{2,1,0:T(8,128)(2,1)} %k_hbm.1, bf16[2,2048,256]{2,1,0:T(8,128)(2,1)} %v_hbm.1, bf16[2,7168]{1,0:T(2,128)(2,1)} %hid_ref.1), custom_call_target="tpu_custom_call" | custom-call | tf_op jit(solution)/shard_map/pallas_call | solution.py:78
  5.0 8.1 %all-to-all-start = ((bf16[16,16,1152]{2,1,0:T(8,128)(2,1)}), bf16[16,16,1152]{2,1,0:T(8,128)(2,1)S(1)}, u32[]{:S(2)}, u32[]{:S(2)}) async-start(bf16[16,16,1152]{2,1,0:T(8,128)(2,1)} %shard_map.100), calls=%async_computation | async-start | bytes 1179648 | tf_op jit(solution)/shard_map/all_to_all | solution.py:418
  13.2 0.3 collective-permute-start.1
  13.5 0.3 collective-permute-start.2
  13.8 0.2 collective-permute-start.3
  14.0 0.0 copy-done.1
  14.0 0.1 reshape_reshape.3
  14.1 0.2 rev.6
  14.3 0.1 pad_add_fusion.where_ref
  14.4 11.7 %all-to-all-done.x_hbm = bf16[16,16,1152]{2,1,0:T(8,128)(2,1)S(1)} async-done(((bf16[16,16,1152]{2,1,0:T(8,128)(2,1)}), bf16[16,16,1152]{2,1,0:T(8,128)(2,1)S(1)}, u32[]{:S(2)}, u32[]{:S(2)}) %all-to-all-start) | async-done | bytes 589856 | tf_op jit(solution)/shard_map/all_to_all | solution.py:418
  26.1 0.0 collective-permute-done.oth_hbm
  26.1 8.2 %shard_map.101 = bf16[64,112,128]{2,1,0:T(8,128)(2,1)} custom-call(s32[2]{0:T(128)S(1)} %pad_add_fusion.where_ref, bf16[16,16,1152]{2,1,0:T(8,128)(2,1)S(1)} %all-to-all-done.x_hbm, bf16[224,8192]{1,0:T(8,128)(2,1)} %bitcast.44, bf16[224,8192]{1,0:T(8,128)(2,1)} %collective-permute-done.oth_hbm, f32[16,512]{1,0:T(8,128)S(1)} %bitcast.42), custom_call_target="tpu_custom_call" | custom-call | flops 234881024 | bytes 7340032 | tf_op jit(solution)/shard_map/pallas_call | solution.py:177
  34.3 6.9 %all-to-all-start.1 = ((bf16[64,112,128]{2,1,0:T(8,128)(2,1)}), bf16[64,112,128]{2,1,0:T(8,128)(2,1)S(1)}, u32[]{:S(2)}, u32[]{:S(2)}) async-start(bf16[64,112,128]{2,1,0:T(8,128)(2,1)} %shard_map.101), calls=%async_computation.1 | async-start | bytes 3670016 | tf_op jit(solution)/shard_map/all_to_all | solution.py:422
  41.3 0.1 slice_reduce_fusion
  41.4 0.1 reshape_squeeze.3
  41.5 0.1 pad_maximum_fusion.5
  41.6 0.0 collective-permute-done.1.gx_hbm
  41.6 0.0 collective-permute-done.2.ux_hbm
  41.6 0.0 collective-permute-done.3.dx_hbm
  41.6 26.0 %all-to-all-done.1 = bf16[64,112,128]{2,1,0:T(8,128)(2,1)S(1)} async-done(((bf16[64,112,128]{2,1,0:T(8,128)(2,1)}), bf16[64,112,128]{2,1,0:T(8,128)(2,1)S(1)}, u32[]{:S(2)}, u32[]{:S(2)}) %all-to-all-start.1) | async-done | bytes 1835040 | tf_op jit(solution)/shard_map/all_to_all | solution.py:422
  67.6 7.5 %shard_map.102 = bf16[64,16,896]{2,1,0:T(8,128)(2,1)} custom-call(s32[2]{0:T(128)S(1)} %pad_add_fusion.where_ref, bf16[4,16,112,128]{3,2,1,0:T(8,128)(2,1)S(1)} %bitcast.41, bf16[7168,128]{1,0:T(8,128)(2,1)} %go_hbm.1, bf16[7168,128]{1,0:T(8,128)(2,1)} %collective-permute-done.1.gx_hbm, bf16[7168,128]{1,0:T(8,128)(2,1)} %uo_hbm.1, ...), custom_call_target="tpu_custom_call" | custom-call | flops 1409286144 | bytes 12845056 | tf_op jit(solution)/shard_map/pallas_call | solution.py:318
  75.2 5.5 %all-to-all-start.2 = ((bf16[64,16,896]{2,1,0:T(8,128)(2,1)}), bf16[64,16,896]{2,1,0:T(8,128)(2,1)}, u32[]{:S(2)}, u32[]{:S(2)}) async-start(bf16[64,16,896]{2,1,0:T(8,128)(2,1)} %shard_map.102), calls=%async_computation.2 | async-start | bytes 3670016 | tf_op jit(solution)/shard_map/all_to_all | solution.py:448
  80.7 0.0 copy-start
  80.9 0.1 reshape.193
  81.0 0.1 fusion
  81.2 0.1 constant_dynamic-slice_fusion.4
  81.4 0.1 broadcast_select_fusion.2
  81.5 0.1 copy.32
  81.5 0.1 reshape.201
  81.8 25.0 %all-to-all-done.2.parts_hbm = bf16[64,16,896]{2,1,0:T(8,128)(2,1)} async-done(((bf16[64,16,896]{2,1,0:T(8,128)(2,1)}), bf16[64,16,896]{2,1,0:T(8,128)(2,1)}, u32[]{:S(2)}, u32[]{:S(2)}) %all-to-all-start.2) | async-done | bytes 1835040 | tf_op jit(solution)/shard_map/all_to_all | solution.py:448
  106.7 0.0 copy-done
  106.7 2.1 %shard_map.103 = bf16[16,896]{1,0:T(8,128)(2,1)S(1)} custom-call(s32[2]{0:T(128)S(1)} %copy-done, bf16[64,16,896]{2,1,0:T(8,128)(2,1)} %all-to-all-done.2.parts_hbm, f32[16,896]{1,0:T(8,128)S(1)} %reshape.197.res_ref), custom_call_target="tpu_custom_call" | custom-call | tf_op jit(solution)/shard_map/pallas_call | solution.py:367
  108.8 0.6 reshape.198
  (28 shorter events, 0.4 us)
Async XLA Ops:
  0.0 14.0 %copy-start.1 = (f32[7168]{0:T(1024)S(1)}, f32[7168]{0:T(1024)}, u32[]{:S(2)}) copy-start(f32[7168]{0:T(1024)} %param.16) | copy-start | bytes 86020
  0.0 26.1 %collective-permute-start = (bf16[224,8192]{1,0:T(8,128)(2,1)}, bf16[224,8192]{1,0:T(8,128)(2,1)}, u32[]{:S(2)}, u32[]{:S(2)}) collective-permute-start(bf16[224,8192]{1,0:T(8,128)(2,1)} %bitcast.43), channel_id=1, source_target_pairs={{0,1},{1,0},{2,3},{3,2},{4,5},{5,4},{6,7},{7,6},{8,9},{9,8},{10,11... | collective-permute-start | bytes 11010056 | tf_op jit(solution)/shard_map/ppermute | solution.py:403
  5.0 21.0 %all-to-all-start = ((bf16[16,16,1152]{2,1,0:T(8,128)(2,1)}), bf16[16,16,1152]{2,1,0:T(8,128)(2,1)S(1)}, u32[]{:S(2)}, u32[]{:S(2)}) async-start(bf16[16,16,1152]{2,1,0:T(8,128)(2,1)} %shard_map.100), calls=%async_computation | async-start | bytes 1179648 | tf_op jit(solution)/shard_map/all_to_all | solution.py:418
  13.2 28.4 %collective-permute-start.1 = (bf16[7168,128]{1,0:T(8,128)(2,1)}, bf16[7168,128]{1,0:T(8,128)(2,1)}, u32[]{:S(2)}, u32[]{:S(2)}) collective-permute-start(bf16[7168,128]{1,0:T(8,128)(2,1)} %go_hbm.1), channel_id=1, source_target_pairs={{0,1},{1,0},{2,3},{3,2},{4,5},{5,4},{6,7},{7,6},{8,9},{9,8},{10,11... | collective-permute-start | bytes 5505032 | tf_op jit(solution)/shard_map/ppermute | solution.py:403
  13.5 28.1 %collective-permute-start.2 = (bf16[7168,128]{1,0:T(8,128)(2,1)}, bf16[7168,128]{1,0:T(8,128)(2,1)}, u32[]{:S(2)}, u32[]{:S(2)}) collective-permute-start(bf16[7168,128]{1,0:T(8,128)(2,1)} %uo_hbm.1), channel_id=1, source_target_pairs={{0,1},{1,0},{2,3},{3,2},{4,5},{5,4},{6,7},{7,6},{8,9},{9,8},{10,11... | collective-permute-start | bytes 5505032 | tf_op jit(solution)/shard_map/ppermute | solution.py:403
  13.8 27.8 %collective-permute-start.3 = (bf16[7168,128]{1,0:T(8,128)(2,1)}, bf16[7168,128]{1,0:T(8,128)(2,1)}, u32[]{:S(2)}, u32[]{:S(2)}) collective-permute-start(bf16[7168,128]{1,0:T(8,128)(2,1)} %do_hbm.1), channel_id=1, source_target_pairs={{0,1},{1,0},{2,3},{3,2},{4,5},{5,4},{6,7},{7,6},{8,9},{9,8},{10,11... | collective-permute-start | bytes 5505032 | tf_op jit(solution)/shard_map/ppermute | solution.py:403
  34.3 33.3 %all-to-all-start.1 = ((bf16[64,112,128]{2,1,0:T(8,128)(2,1)}), bf16[64,112,128]{2,1,0:T(8,128)(2,1)S(1)}, u32[]{:S(2)}, u32[]{:S(2)}) async-start(bf16[64,112,128]{2,1,0:T(8,128)(2,1)} %shard_map.101), calls=%async_computation.1 | async-start | bytes 3670016 | tf_op jit(solution)/shard_map/all_to_all | solution.py:422
  75.2 31.5 %all-to-all-start.2 = ((bf16[64,16,896]{2,1,0:T(8,128)(2,1)}), bf16[64,16,896]{2,1,0:T(8,128)(2,1)}, u32[]{:S(2)}, u32[]{:S(2)}) async-start(bf16[64,16,896]{2,1,0:T(8,128)(2,1)} %shard_map.102), calls=%async_computation.2 | async-start | bytes 3670016 | tf_op jit(solution)/shard_map/all_to_all | solution.py:448
  80.7 26.0 %copy-start = (s32[2]{0:T(128)S(1)}, s32[2]{0:T(128)}, u32[]{:S(2)}) copy-start(s32[2]{0:T(128)} %lengths_ref.3) | copy-start | bytes 28

commit v4 on v3

--- a/solution.py
+++ b/solution.py
@@ -14,20 +14,28 @@
 NT = (((1,), (1,)), ((), ()))
 
 
-def attend_kernel(lengths_ref, q_ref, k_hbm, v_hbm, hid_ref, out_ref, keys, values, sems):
+def attend_kernel(lengths_ref, q_hbm, k_hbm, v_hbm, hid_hbm, out_ref, q_ref, hid_ref, keys, values, small_sems, sems):
     slots, span, dim = keys.shape
     heads = q_ref.shape[1] // dim
     chips = out_ref.shape[0]
+    small = [
+        pltpu.make_async_copy(src, dst, small_sems.at[i])
+        for i, (src, dst) in enumerate(((q_hbm, q_ref), (hid_hbm, hid_ref)))
+    ]
+    for copy in small:
+        copy.start()
     copies = []
     for i, (src, dst) in enumerate(((k_hbm, keys), (v_hbm, values))):
         for s in range(slots):
             copy = pltpu.make_async_copy(src.at[s], dst.at[s], sems.at[i, s])
             copy.start()
             copies.append(copy)
+    small[0].wait()
     q = q_ref[...].astype(F32)
     q = jnp.concatenate(
         [q[s : s + 1, h * dim : (h + 1) * dim] for s in range(slots) for h in range(heads)], axis=0
     ).astype(BF16)
+    small[1].wait()
     hid = hid_ref[...].astype(F32)
     row = lax.broadcasted_iota(jnp.int32, (16, 128), 0)
     tiles = [
@@ -41,7 +49,7 @@
         for i in range(4):
             held = jnp.where(row // slots == i, tiles[first + i], held)
         extra.append(held.astype(BF16))
-    parts, totals = [], []
+    parts = []
     position = lax.broadcasted_iota(jnp.int32, (heads, span), 1)
     for s in range(slots):
         copies[s].wait()
@@ -50,12 +58,10 @@
         ) * dim ** (-0.5)
         scores = jnp.where(position < jnp.maximum(lengths_ref[s], 1), scores, -jnp.inf)
         weights = jnp.exp(scores - jnp.max(scores, axis=1, keepdims=True))
-        totals.append(jnp.sum(weights, axis=1, keepdims=True))
-        parts.append(weights.astype(BF16))
+        parts.append((weights * (1.0 / jnp.sum(weights, axis=1, keepdims=True))).astype(BF16))
     for s in range(slots):
         copies[slots + s].wait()
-        attended = jnp.dot(parts[s], values[s], preferred_element_type=F32)
-        parts[s] = (attended / totals[s]).astype(BF16)
+        parts[s] = jnp.dot(parts[s], values[s], preferred_element_type=F32).astype(BF16)
     both = jnp.concatenate(parts, axis=0)
     pieces = 16 // slots
     per = heads // pieces
@@ -77,126 +83,141 @@
     lanes = query.shape[1] * slots // 16 + 128
     return pl.pallas_call(
         attend_kernel,
-        in_specs=[pl.BlockSpec(memory_space=pltpu.SMEM), vmem, hbm, hbm, vmem],
+        in_specs=[pl.BlockSpec(memory_space=pltpu.SMEM), hbm, hbm, hbm, hbm],
         out_specs=vmem,
         out_shape=pltpu.HBM((chips, 16, lanes), BF16),
         scratch_shapes=[
+            pltpu.VMEM(query.shape, BF16),
+            pltpu.VMEM(hidden.shape, BF16),
             pltpu.VMEM(key_cache.shape, BF16),
             pltpu.VMEM(value_cache.shape, BF16),
+            pltpu.SemaphoreType.DMA((2,)),
             pltpu.SemaphoreType.DMA((2, slots)),
         ],
-        compiler_params=pltpu.CompilerParams(vmem_limit_bytes=58 * 2**20),
-    )(lengths, query, key_cache, value_cache, hidden)
+        compiler_params=pltpu.CompilerParams(vmem_limit_bytes=12 * 2**20),
+    )(in_hbm(lengths), *[in_hbm(v) for v in (query, key_cache, value_cache, hidden)])
 
 
 def project_kernel(
-    cols, where_ref, x_hbm, own_hbm, oth_hbm, gain_ref, out_hbm, x_buf, own, oth, block, sems, out_sem
+    steps, cols, x_ref, own_ref, oth_ref, gain_ref, out_hbm, x_rows, hid_rows, acc_own, acc_oth, block, out_sem
 ):
-    chips, deep, lanes = x_buf.shape
-    depth = own.shape[1]
+    step = pl.program_id(0)
+    chips, deep, lanes = x_ref.shape
+    chunk = own_ref.shape[1]
     slots = 2
     pieces = deep // slots
     rows = chips * slots
-    cut = 128
-    first = pltpu.make_async_copy(x_hbm, x_buf, sems.at[0])
-    copies = [
-        pltpu.make_async_copy(src.at[span], dst.at[span], sems.at[1 + 2 * i + j])
-        for i, (src, dst) in enumerate(((own_hbm, own), (oth_hbm, oth)))
-        for j, span in enumerate((pl.ds(0, cut), pl.ds(cut, cols - cut)))
-    ]
-    first.start()
-    copies[0].start()
-    copies[1].start()
-    r = lax.broadcasted_iota(jnp.int32, (chips * deep, chips * deep), 0)
-    c = lax.broadcasted_iota(jnp.int32, (chips * deep, chips * deep), 1)
-    order = c == (r % rows) // slots * deep + r // rows * slots + r % slots
-    order = jnp.where(order, 1.0, 0.0).astype(BF16)
-    first.wait()
-    x = jnp.dot(order, x_buf[...].reshape(chips * deep, lanes), preferred_element_type=F32)
-    wide = depth // pieces
-    chip = where_ref[1]
-    lane = lax.broadcasted_iota(jnp.int32, (rows, 128), 1)
-
-    def ahead(tiles, shift):
-        moved = [pltpu.roll(t, 128 - shift, 1) for t in tiles]
-        return [jnp.where(lane < 128 - shift, a, b) for a, b in zip(moved, moved[1:] + moved[-1:])]
-
-    hids = [x[i * rows : (i + 1) * rows, wide : wide + 128] for i in range(4)]
-    hids = [jnp.where(chip % 2 == 0, a, b) for a, b in zip(hids, ahead(hids, 64))]
-    hid_a = jnp.concatenate(hids[:2], axis=1)
-    hid_b = jnp.concatenate(ahead(hids[1:], cols - 128)[:2], axis=1)
-    x = jnp.concatenate([x[i * rows : (i + 1) * rows, :wide] for i in range(pieces)], axis=1).astype(BF16)
-    copies[0].wait()
-    copies[2].start()
-    copies[1].wait()
-    copies[3].start()
-    sums = [lax.dot_general(x, own[...], NT, preferred_element_type=F32)]
-    copies[2].wait()
-    copies[3].wait()
-    sums.append(lax.dot_general(x, oth[...], NT, preferred_element_type=F32))
-    pad = jnp.zeros((rows, 256 - cols), F32)
-    swapped = where_ref[0] == 1
-    hids = (jnp.where(swapped, hid_b, hid_a), jnp.where(swapped, hid_a, hid_b))
-    gains = gain_ref[pl.ds(chip, 1), :]
-    sent = []
-    for i in range(2):
-        projected = jnp.concatenate([sums[i].astype(BF16).astype(F32), pad], axis=1)
-        sent.append((hids[i] + projected) * gains[:, 256 * i : 256 * i + 256])
-    own_tail, oth_tail = sent[0][:, 128:], sent[1][:, 128:]
-    third = jnp.where(lane < cols - 128, own_tail, pltpu.roll(oth_tail, cols - 128, 1))
-    rest = pltpu.roll(oth_tail, 128 - (256 - cols), 1)
-    turned = pltpu.roll(rest, 64, 1)
-    half = rows // 2
-    low = lax.broadcasted_iota(jnp.int32, (half, 128), 1) < 64
-    even = jnp.where(low, rest[:half], turned[half:])
-    odd = jnp.where(low, rest[half:], turned[:half])
-    last = jnp.where(chip % 2 == 0, even, odd)
-    packed = jnp.concatenate([sent[0][:, :128], sent[1][:, :128], third, last], axis=0).astype(BF16)
-    copies = block.shape[0]
-    for p in range(copies):
-        block[p] = packed
-    outs = []
-    for p in range(out_hbm.shape[0] // copies):
-        out = pltpu.make_async_copy(block, out_hbm.at[pl.ds(p * copies, copies)], out_sem.at[p])
-        out.start()
-        outs.append(out)
-    for out in outs:
-        out.wait()
+    wide = x_rows.shape[1] // pieces
+
+    @pl.when(step == 0)
+    def _():
+        r = lax.broadcasted_iota(jnp.int32, (chips * deep, chips * deep), 0)
+        c = lax.broadcasted_iota(jnp.int32, (chips * deep, chips * deep), 1)
+        order = c == (r % rows) // slots * deep + r // rows * slots + r % slots
+        order = jnp.where(order, 1.0, 0.0).astype(BF16)
+        x = jnp.dot(order, x_ref[...].reshape(chips * deep, lanes), preferred_element_type=F32)
+        for i in range(pieces):
+            x_rows[:, i * wide : (i + 1) * wide] = x[i * rows : (i + 1) * rows, :wide].astype(BF16)
+        for i in range(4):
+            hid_rows[i] = x[i * rows : (i + 1) * rows, wide:]
+
+    x = x_rows[:, pl.ds(pl.multiple_of(step * chunk, chunk), chunk)]
+    for acc, w in ((acc_own, own_ref), (acc_oth, oth_ref)):
+        part = lax.dot_general(x, w[...], NT, preferred_element_type=F32)
+
+        @pl.when(step == 0)
+        def _():
+            acc[...] = part
+
+        @pl.when(step > 0)
+        def _():
+            acc[...] += part
+
+    @pl.when(step == steps - 1)
+    def _():
+        me = lax.axis_index("dev")
+        core, chip = me % 2, me // 2
+        lane = lax.broadcasted_iota(jnp.int32, (rows, 128), 1)
+
+        def ahead(tiles, shift):
+            moved = [pltpu.roll(t, 128 - shift, 1) for t in tiles]
+            return [jnp.where(lane < 128 - shift, a, b) for a, b in zip(moved, moved[1:] + moved[-1:])]
+
+        def halves(tiles):
+            tiles = [jnp.where(chip % 2 == 0, a, b) for a, b in zip(tiles, ahead(tiles, 64))]
+            first = jnp.concatenate(tiles[:2], axis=1)
+            second = jnp.concatenate(ahead(tiles[1:], cols - 128)[:2], axis=1)
+            return jnp.where(core == 0, first, second), jnp.where(core == 0, second, first)
+
+        hids = halves([hid_rows[i] for i in range(4)])
+        start = 7 * (chip // 2) + 3 * (chip % 2)
+        gains = halves([jnp.broadcast_to(gain_ref[pl.ds(start + i, 1), :], (rows, 128)) for i in range(4)])
+        pad = jnp.zeros((rows, 256 - cols), F32)
+        sent = []
+        for acc, hid, gain in zip((acc_own, acc_oth), hids, gains):
+            projected = jnp.concatenate([acc[...].astype(BF16).astype(F32), pad], axis=1)
+            sent.append((hid + projected) * gain)
+        own_tail, oth_tail = sent[0][:, 128:], sent[1][:, 128:]
+        third = jnp.where(lane < cols - 128, own_tail, pltpu.roll(oth_tail, cols - 128, 1))
+        rest = pltpu.roll(oth_tail, 128 - (256 - cols), 1)
+        turned = pltpu.roll(rest, 64, 1)
+        half = rows // 2
+        low = lax.broadcasted_iota(jnp.int32, (half, 128), 1) < 64
+        even = jnp.where(low, rest[:half], turned[half:])
+        odd = jnp.where(low, rest[half:], turned[:half])
+        last = jnp.where(chip % 2 == 0, even, odd)
+        packed = jnp.concatenate([sent[0][:, :128], sent[1][:, :128], third, last], axis=0).astype(BF16)
+        copies = block.shape[0]
+        for p in range(copies):
+            block[p] = packed
+        outs = []
+        for p in range(out_hbm.shape[0] // copies):
+            out = pltpu.make_async_copy(block, out_hbm.at[pl.ds(p * copies, copies)], out_sem.at[p])
+            out.start()
+            outs.append(out)
+        for out in outs:
+            out.wait()
 
 
 def in_hbm(v):
     return pltpu.with_memory_space_constraint(v, pltpu.HBM)
 
 
-def project(where, messages, gains, out_own, out_oth, peers):
+def project(messages, gain, out_own, out_oth, peers):
     cols, depth = out_own.shape
     rows = messages.shape[0] * 2
     packed = rows * 2 * cols // 128
-    hbm = pl.BlockSpec(memory_space=pl.ANY)
-    vmem = pl.BlockSpec(memory_space=pltpu.VMEM)
+    steps = 1
+    chunk = depth // steps
     return pl.pallas_call(
-        functools.partial(project_kernel, cols),
-        in_specs=[pl.BlockSpec(memory_space=pltpu.SMEM), hbm, hbm, hbm, vmem],
-        out_specs=hbm,
+        functools.partial(project_kernel, steps, cols),
+        grid=(steps,),
+        in_specs=[
+            pl.BlockSpec(messages.shape, lambda k: (0, 0, 0)),
+            pl.BlockSpec((cols, chunk), lambda k: (0, k)),
+            pl.BlockSpec((cols, chunk), lambda k: (0, k)),
+            pl.BlockSpec(gain.shape, lambda k: (0, 0)),
+        ],
+        out_specs=pl.BlockSpec(memory_space=pl.ANY),
         out_shape=pltpu.HBM((peers, packed, 128), BF16),
         scratch_shapes=[
-            pltpu.VMEM(messages.shape, BF16),
-            pltpu.VMEM((cols, depth), BF16),
-            pltpu.VMEM((cols, depth), BF16),
+            pltpu.VMEM((rows, depth), BF16),
+            pltpu.VMEM((4, rows, 128), F32),
+            pltpu.VMEM((rows, cols), F32),
+            pltpu.VMEM((rows, cols), F32),
             pltpu.VMEM((8, packed, 128), BF16),
-            pltpu.SemaphoreType.DMA((5,)),
             pltpu.SemaphoreType.DMA((peers // 8,)),
         ],
-        compiler_params=pltpu.CompilerParams(vmem_limit_bytes=VMEM),
+        compiler_params=pltpu.CompilerParams(vmem_limit_bytes=24 * 2**20),
         cost_estimate=pl.CostEstimate(
             flops=4 * rows * cols * depth, bytes_accessed=4 * cols * depth, transcendentals=0
         ),
-    )(where, messages, in_hbm(out_own), in_hbm(out_oth), gains)
+    )(messages, out_own, out_oth, in_hbm(gain))
 
 
 def ffn_kernel(
     chips, cols, width,
-    where_ref, x_hbm, go_hbm, gx_hbm, uo_hbm, ux_hbm, do_hbm, dx_hbm, ig_ref, out_hbm,
+    x_hbm, go_hbm, gx_hbm, uo_hbm, ux_hbm, do_hbm, dx_hbm, ig_ref, out_hbm,
     x_buf, wide, down, held, out_buf, x_sem, wide_sem, down_sem, out_sem,
 ):
     groups, _, packed, _ = x_buf.shape
@@ -206,7 +227,7 @@
     quarter = 4
     parts = chips // quarter
     deep = quarter * 2 * cols
-    core = where_ref[0]
+    core = lax.axis_index("dev") % 2
 
     spans, _, span = held.shape
     stages = []
@@ -305,7 +326,7 @@
         out.wait()
 
 
-def feed_forward(where, blocks, gate, up, down, inverse_gain, chips):
+def feed_forward(blocks, gate, up, down, inverse_gain, chips):
     peers, packed, _ = blocks.shape
     groups = peers // chips
     width, units = gate[0].shape
@@ -317,8 +338,7 @@
     hbm = pl.BlockSpec(memory_space=pl.ANY)
     return pl.pallas_call(
         functools.partial(ffn_kernel, chips, cols, width),
-        in_specs=[pl.BlockSpec(memory_space=pltpu.SMEM)]
-        + [hbm] * 7
+        in_specs=[hbm] * 7
         + [pl.BlockSpec(memory_space=pltpu.VMEM)],
         out_specs=hbm,
         out_shape=pltpu.HBM((peers, 16, span), BF16),
@@ -338,38 +358,48 @@
             flops=12 * total * units * width, bytes_accessed=14 * width * units, transcendentals=0
         ),
     )(
-        where,
         blocks.reshape(groups, chips, packed, 128),
         *[in_hbm(v) for v in (*gate, *up, *down)],
         inverse_gain,
     )
 
 
-def final_kernel(lengths_ref, parts_hbm, res_ref, out_ref, parts, sems):
+def final_kernel(lengths_ref, parts_hbm, res_hbm, out_ref, parts, res, res_sem, sems):
     quarter = parts.shape[0] // 4
     copies = []
     for q in range(4):
         some = pl.ds(q * quarter, quarter)
         copies.append(pltpu.make_async_copy(parts_hbm.at[some], parts.at[some], sems.at[q]))
         copies[q].start()
-    total = res_ref[...]
+    copy = pltpu.make_async_copy(res_hbm, res, res_sem)
+    copy.start()
+    copy.wait()
+    total = res[...]
     for q in range(4):
         copies[q].wait()
         for p in range(q * quarter, (q + 1) * quarter):
             total += parts[p].astype(F32)
     row = lax.broadcasted_iota(jnp.int32, total.shape, 0)
     live = jnp.where(row % 2 == 0, lengths_ref[0], lengths_ref[1]) > 0
-    out_ref[...] = jnp.where(live, total, 0.0).astype(BF16)
+    total = jnp.where(live, total, 0.0)
+    span = total.shape[1]
+    for b in range(total.shape[0] // 2):
+        out_ref[:, b * span : (b + 1) * span] = total[2 * b : 2 * b + 2].astype(BF16)
 
 
 def finish(lengths, parts, res):
     vmem = pl.BlockSpec(memory_space=pltpu.VMEM)
     return pl.pallas_call(
         final_kernel,
-        in_specs=[pl.BlockSpec(memory_space=pltpu.SMEM), pl.BlockSpec(memory_space=pl.ANY), vmem],
+        in_specs=[pl.BlockSpec(memory_space=pltpu.SMEM)] + [pl.BlockSpec(memory_space=pl.ANY)] * 2,
         out_specs=vmem,
-        out_shape=jax.ShapeDtypeStruct(res.shape, BF16),
-        scratch_shapes=[pltpu.VMEM(parts.shape, BF16), pltpu.SemaphoreType.DMA((4,))],
+        out_shape=jax.ShapeDtypeStruct((2, res.size // 2), BF16),
+        scratch_shapes=[
+            pltpu.VMEM(parts.shape, BF16),
+            pltpu.VMEM(res.shape, F32),
+            pltpu.SemaphoreType.DMA,
+            pltpu.SemaphoreType.DMA((4,)),
+        ],
         compiler_params=pltpu.CompilerParams(vmem_limit_bytes=16 * 2**20),
     )(lengths, parts, res)
 
@@ -404,24 +434,19 @@
 
         out_own = out_weight.T
         out_oth = swap(out_own)
+        message = attend(lengths, query, key_cache, value_cache, hidden, chips)
+        got = lax.all_to_all(message, "dev", 0, 0, axis_index_groups=plane)
+        block = project(got, ffn_gain.reshape(width // 128, 128), out_own, out_oth, peers)
+        blocks = lax.all_to_all(block, ("grp", "dev"), 0, 0, axis_index_groups=cube)
+
+        gate_weight, up_weight, down_weight, gains, _ = lax.optimization_barrier(
+            (gate_weight, up_weight, down_weight, ffn_gain, block)
+        )
         gate_oth = swap(gate_weight)
         up_oth = swap(up_weight)
         down_oth = swap(down_weight)
-
-        where = jnp.stack([core, chip]).astype(jnp.int32)
-
-        def halves(v):
-            v = v.reshape(v.shape[0], chips, 2, cols)
-            return jnp.pad(v, ((0, 0), (0, 0), (0, 0), (0, 256 - cols)))
-
-        message = attend(lengths, query, key_cache, value_cache, hidden, chips)
-        got = lax.all_to_all(message, "dev", 0, 0, axis_index_groups=plane)
-        gain = halves(ffn_gain.reshape(1, width))[0]
-        gain = jnp.where(core == 0, gain, gain[:, ::-1])
-        block = project(where, got, gain.reshape(chips, 512), out_own, out_oth, peers)
-        blocks = lax.all_to_all(block, ("grp", "dev"), 0, 0, axis_index_groups=cube)
-
-        inv = 1.0 / gain
+        inv = 1.0 / gains.reshape(chips, 2, cols)
+        inv = jnp.where(core == 0, inv, inv[:, ::-1])
         inv = jnp.concatenate(
             [
                 jnp.stack(
@@ -437,7 +462,6 @@
             axis=1,
         ).reshape(width // 128, 128)
         partial = feed_forward(
-            where,
             blocks,
             (gate_weight, gate_oth),
             (up_weight, up_oth),
@@ -464,8 +488,7 @@
         mine = mine.astype(F32).transpose(1, 0, 2, 3).reshape(slots, width) / ffn_gain
         spans = 16 // slots
         mine = mine.reshape(slots, spans, width // spans).transpose(1, 0, 2).reshape(16, width // spans)
-        out = finish(lengths, parts, mine)
-        return out.reshape(spans, slots, width // spans).transpose(1, 0, 2).reshape(slots, width)
+        return finish(lengths, parts, mine)
 
     return shards
 

time: 110 us -> 109 us (level)
  blocking collectives: 0 us -> 20.7 us
  waiting for transfers between devices: 62.6 us -> 52.2 us
  starting transfers between devices: 21.4 us -> 13 us
  Pallas kernels: 22.9 us -> 20.2 us
    all_to_all x0 -> x1, blocking collectives: none -> 20.7 us  [shards(): got = lax.all_to_all(message, 'dev', 0, 0, axis_index_groups=plane)]
    all_to_all x1 -> x0, waiting for transfers between devices: 11.7 us -> none  [shards(): got = lax.all_to_all(message, 'dev', 0, 0, axis_index_groups=plane)]
    all_to_all x1 -> x0, starting transfers between devices: 8.14 us -> none  [shards(): got = lax.all_to_all(message, 'dev', 0, 0, axis_index_groups=plane)]
    pallas_call x1, Pallas kernels: 8.2 us -> 4.66 us  [project(): pl.pallas_call(functools.partial(project_kernel, steps, cols), grid=(step...]
  transfers between devices with their start and end apart: 7 -> 6, of which waited for: 3 -> 2; matrix products, arithmetic and copies ran while one was open for 1% -> 1% of each run, Pallas kernels for 12% -> 5%
where the time goes in v4:
time: 109 us; the launch traced here: 108 us
  waiting for transfers between devices  52.2 us (48%)
  blocking collectives  20.7 us (19%)
  Pallas kernels  20.2 us (19%)
  starting transfers between devices  13 us (12%)
  local copies, waits for them, and re-layouts  1.21 us (1%)
    all_to_all x1, waiting for transfers between devices, shards(): blocks = lax.all_to_all(block, ('grp', 'dev'), 0, 0, axis_index_groups=cube)  26.8 us
    all_to_all x1, waiting for transfers between devices, shards(): lax.all_to_all(partial, ('grp', 'dev'), 0, 0, axis_index_groups=cube)  25.4 us
    all_to_all x1, blocking collectives, shards(): got = lax.all_to_all(message, 'dev', 0, 0, axis_index_groups=plane)  20.7 us
    pallas_call x1, Pallas kernels, feed_forward(): pl.pallas_call(functools.partial(ffn_kernel, chips, cols, width), in_spec...  6.97 us
    all_to_all x1, starting transfers between devices, shards(): blocks = lax.all_to_all(block, ('grp', 'dev'), 0, 0, axis_index_groups=cube)  6.78 us
    pallas_call x1, Pallas kernels, attend(): pl.pallas_call(attend_kernel, in_specs=[pl.BlockSpec(memory_space=pltpu.S...  5.91 us
    all_to_all x1, starting transfers between devices, shards(): lax.all_to_all(partial, ('grp', 'dev'), 0, 0, axis_index_groups=cube)  5.54 us
    pallas_call x1, Pallas kernels, project(): pl.pallas_call(functools.partial(project_kernel, steps, cols), grid=(step...  4.66 us
  transfers between devices with their start and end apart: 6, of which 2 were waited for; matrix products, arithmetic and copies ran while one was open for 1% of the time, Pallas kernels for 5%

profile of v4, /device:TPU:0, one launch (start us, length us, event | category | flops | bytes accessed | tf_op | source)
XLA Modules:
  0.0 108.0 jit_solution(18201034269955964923)
XLA Ops:
  0.0 0.0 copy-start
  0.0 0.0 collective-permute-start
  0.0 5.9 %shard_map.100 = bf16[16,16,1152]{2,1,0:T(8,128)(2,1)} custom-call(s32[2]{0:T(128)} %lengths_ref.3, bf16[2,8192]{1,0:T(2,128)(2,1)} %q_hbm.1, bf16[2,2048,256]{2,1,0:T(8,128)(2,1)} %k_hbm.1, bf16[2,2048,256]{2,1,0:T(8,128)(2,1)} %v_hbm.1, bf16[2,7168]{1,0:T(2,128)(2,1)} %hid_hbm.1), custom_call_target="tpu_custom_call" | custom-call | tf_op jit(solution)/shard_map/pallas_call | solution.py:84
  5.9 20.7 %all_to_all.15.x_ref = bf16[16,16,1152]{2,1,0:T(8,128)(2,1)S(1)} all-to-all(bf16[16,16,1152]{2,1,0:T(8,128)(2,1)} %shard_map.100), channel_id=1, replica_groups={{0,2,4,6,8,10,12,14,16,18,20,22,24,26,28,30},{1,3,5,7,9,11,13,15,17,19,..., dimensions={0} | all-to-all | bytes 1179648 | tf_op jit(solution)/shard_map/all_to_all | solution.py:438
  26.7 0.0 collective-permute-done.oth_ref
  26.7 0.0 copy-done
  26.7 4.7 %shard_map.101 = bf16[64,112,128]{2,1,0:T(8,128)(2,1)} custom-call(bf16[16,16,1152]{2,1,0:T(8,128)(2,1)S(1)} %all_to_all.15.x_ref, bf16[224,8192]{1,0:T(8,128)(2,1)S(1)} %bitcast.32, bf16[224,8192]{1,0:T(8,128)(2,1)S(1)} %collective-permute-done.oth_ref, f32[56,128]{1,0:T(8,128)} %bitcast.36), custom_call_target="tpu_custom_call" | custom-call | flops 234881024 | bytes 7340032 | tf_op jit(solution)/shard_map/pallas_call | solution.py:192
  31.3 0.0 copy-start.2
  31.3 0.1 collective-permute-start.1
  31.4 0.5 collective-permute-start.2
  31.9 0.1 collective-permute-start.3
  32.0 6.8 %all-to-all-start.1 = ((bf16[64,112,128]{2,1,0:T(8,128)(2,1)}), bf16[64,112,128]{2,1,0:T(8,128)(2,1)S(1)}, u32[]{:S(2)}, u32[]{:S(2)}) async-start(bf16[64,112,128]{2,1,0:T(8,128)(2,1)} %shard_map.101), calls=%async_computation.1 | async-start | bytes 3670016 | tf_op jit(solution)/shard_map/all_to_all | solution.py:440
  38.8 0.0 copy-done.2
  38.8 0.1 reshape.187
  38.9 0.2 reverse.3
  39.2 0.1 slice_reduce_fusion
  39.3 0.1 reshape_squeeze.3
  39.4 0.1 pad_maximum_fusion.5
  39.5 26.8 %all-to-all-done.1 = bf16[64,112,128]{2,1,0:T(8,128)(2,1)S(1)} async-done(((bf16[64,112,128]{2,1,0:T(8,128)(2,1)}), bf16[64,112,128]{2,1,0:T(8,128)(2,1)S(1)}, u32[]{:S(2)}, u32[]{:S(2)}) %all-to-all-start.1) | async-done | bytes 1835040 | tf_op jit(solution)/shard_map/all_to_all | solution.py:440
  66.3 0.0 collective-permute-done.1.gx_hbm
  66.3 0.0 collective-permute-done.2.ux_hbm
  66.3 0.0 collective-permute-done.3.dx_hbm
  66.3 7.0 %shard_map.102 = bf16[64,16,896]{2,1,0:T(8,128)(2,1)} custom-call(bf16[4,16,112,128]{3,2,1,0:T(8,128)(2,1)S(1)} %bitcast.30, bf16[7168,128]{1,0:T(8,128)(2,1)} %go_hbm, bf16[7168,128]{1,0:T(8,128)(2,1)} %collective-permute-done.1.gx_hbm, bf16[7168,128]{1,0:T(8,128)(2,1)} %uo_hbm, bf16[7168,128]{1,0:T(8,128)(2,1)} %collective-permute-done.2.ux_hbm, ...), custom_call_target="tpu_custom_call" | custom-call | flops 1409286144 | bytes 12845056 | tf_op jit(solution)/shard_map/pallas_call | solution.py:339
  73.3 5.5 %all-to-all-start.2 = ((bf16[64,16,896]{2,1,0:T(8,128)(2,1)}), bf16[64,16,896]{2,1,0:T(8,128)(2,1)}, u32[]{:S(2)}, u32[]{:S(2)}) async-start(bf16[64,16,896]{2,1,0:T(8,128)(2,1)} %shard_map.102), calls=%async_computation.2 | async-start | bytes 3670016 | tf_op jit(solution)/shard_map/all_to_all | solution.py:472
  78.9 0.0 copy-start.1
  79.0 0.1 reshape.191
  79.1 0.1 fusion
  79.4 0.1 constant_dynamic-slice_fusion.4
  79.5 0.1 broadcast_select_fusion.1
  79.6 0.1 copy.29
  79.7 0.1 reshape.197
  79.9 25.4 %all-to-all-done.2.parts_hbm = bf16[64,16,896]{2,1,0:T(8,128)(2,1)} async-done(((bf16[64,16,896]{2,1,0:T(8,128)(2,1)}), bf16[64,16,896]{2,1,0:T(8,128)(2,1)}, u32[]{:S(2)}, u32[]{:S(2)}) %all-to-all-start.2) | async-done | bytes 1835040 | tf_op jit(solution)/shard_map/all_to_all | solution.py:472
  105.3 0.0 copy-done.1
  105.3 2.7 %shard_map.103 = bf16[2,7168]{1,0:T(2,128)(2,1)} custom-call(s32[2]{0:T(128)S(1)} %copy-done.1, bf16[64,16,896]{2,1,0:T(8,128)(2,1)} %all-to-all-done.2.parts_hbm, f32[16,896]{1,0:T(8,128)S(1)} %reshape.195.res_hbm), custom_call_target="tpu_custom_call" | custom-call | tf_op jit(solution)/shard_map/pallas_call | solution.py:392
  (26 shorter events, 0.4 us)
Async XLA Ops:
  0.0 26.7 %copy-start = (bf16[8192,224]{0,1:T(8,128)(2,1)S(1)}, bf16[8192,224]{0,1:T(8,128)(2,1)}, u32[]{:S(2)}) copy-start(bf16[8192,224]{0,1:T(8,128)(2,1)} %param.15) | copy-start | bytes 11010052
  0.0 26.7 %collective-permute-start = (bf16[224,8192]{1,0:T(8,128)(2,1)}, bf16[224,8192]{1,0:T(8,128)(2,1)S(1)}, u32[]{:S(2)}, u32[]{:S(2)}) collective-permute-start(bf16[224,8192]{1,0:T(8,128)(2,1)} %bitcast.31), channel_id=1, source_target_pairs={{0,1},{1,0},{2,3},{3,2},{4,5},{5,4},{6,7},{7,6},{8,9},{9,8},{10,11... | collective-permute-start | bytes 11010056 | tf_op jit(solution)/shard_map/ppermute | solution.py:433
  31.3 7.5 %copy-start.2 = (f32[7168]{0:T(1024)S(1)}, f32[7168]{0:T(1024)}, u32[]{:S(2)}) copy-start(f32[7168]{0:T(1024)} %param.16) | copy-start | bytes 86020
  31.3 35.0 %collective-permute-start.1 = (bf16[7168,128]{1,0:T(8,128)(2,1)}, bf16[7168,128]{1,0:T(8,128)(2,1)}, u32[]{:S(2)}, u32[]{:S(2)}) collective-permute-start(bf16[7168,128]{1,0:T(8,128)(2,1)} %go_hbm), channel_id=1, source_target_pairs={{0,1},{1,0},{2,3},{3,2},{4,5},{5,4},{6,7},{7,6},{8,9},{9,8},{10,11... | collective-permute-start | bytes 5505032 | tf_op jit(solution)/shard_map/ppermute | solution.py:433
  31.4 34.9 %collective-permute-start.2 = (bf16[7168,128]{1,0:T(8,128)(2,1)}, bf16[7168,128]{1,0:T(8,128)(2,1)}, u32[]{:S(2)}, u32[]{:S(2)}) collective-permute-start(bf16[7168,128]{1,0:T(8,128)(2,1)} %uo_hbm), channel_id=1, source_target_pairs={{0,1},{1,0},{2,3},{3,2},{4,5},{5,4},{6,7},{7,6},{8,9},{9,8},{10,11... | collective-permute-start | bytes 5505032 | tf_op jit(solution)/shard_map/ppermute | solution.py:433
  31.9 34.4 %collective-permute-start.3 = (bf16[7168,128]{1,0:T(8,128)(2,1)}, bf16[7168,128]{1,0:T(8,128)(2,1)}, u32[]{:S(2)}, u32[]{:S(2)}) collective-permute-start(bf16[7168,128]{1,0:T(8,128)(2,1)} %do_hbm), channel_id=1, source_target_pairs={{0,1},{1,0},{2,3},{3,2},{4,5},{5,4},{6,7},{7,6},{8,9},{9,8},{10,11... | collective-permute-start | bytes 5505032 | tf_op jit(solution)/shard_map/ppermute | solution.py:433
  32.0 34.3 %all-to-all-start.1 = ((bf16[64,112,128]{2,1,0:T(8,128)(2,1)}), bf16[64,112,128]{2,1,0:T(8,128)(2,1)S(1)}, u32[]{:S(2)}, u32[]{:S(2)}) async-start(bf16[64,112,128]{2,1,0:T(8,128)(2,1)} %shard_map.101), calls=%async_computation.1 | async-start | bytes 3670016 | tf_op jit(solution)/shard_map/all_to_all | solution.py:440
  73.3 32.0 %all-to-all-start.2 = ((bf16[64,16,896]{2,1,0:T(8,128)(2,1)}), bf16[64,16,896]{2,1,0:T(8,128)(2,1)}, u32[]{:S(2)}, u32[]{:S(2)}) async-start(bf16[64,16,896]{2,1,0:T(8,128)(2,1)} %shard_map.102), calls=%async_computation.2 | async-start | bytes 3670016 | tf_op jit(solution)/shard_map/all_to_all | solution.py:472
  78.9 26.4 %copy-start.1 = (s32[2]{0:T(128)S(1)}, s32[2]{0:T(128)}, u32[]{:S(2)}) copy-start(s32[2]{0:T(128)} %lengths_ref.3) | copy-start | bytes 28

commit v5 on v4

v5 whole, which is shorter than its diff:
```python
import functools

import jax
import jax.numpy as jnp
from jax import lax
from jax.experimental import pallas as pl
from jax.experimental.pallas import tpu as pltpu
from jax.sharding import PartitionSpec as P

BF16 = jnp.bfloat16
F32 = jnp.float32
EPS = 1e-05
VMEM = 32 * 2**20
HOPS = 4
NT = (((1,), (1,)), ((), ()))


def attend_kernel(lengths_ref, q_hbm, k_hbm, v_hbm, hid_hbm, token_hbm, out_ref, q_ref, hid_ref, keys, values, small_sems, sems):
    slots, span, dim = keys.shape
    heads = q_ref.shape[1] // dim
    chips = out_ref.shape[0]
    small = [
        pltpu.make_async_copy(src, dst, small_sems.at[i])
        for i, (src, dst) in enumerate(((q_hbm, q_ref), (hid_hbm, hid_ref)))
    ]
    for copy in small:
        copy.start()
    copies = []
    for i, (src, dst) in enumerate(((k_hbm, keys), (v_hbm, values))):
        for s in range(slots):
            copy = pltpu.make_async_copy(src.at[s], dst.at[s], sems.at[i, s])
            copy.start()
            copies.append(copy)
    small[0].wait()
    q = q_ref[...].astype(F32)
    q = jnp.concatenate(
        [q[s : s + 1, h * dim : (h + 1) * dim] for s in range(slots) for h in range(heads)], axis=0
    ).astype(BF16)
    small[1].wait()
    hid = hid_ref[...].astype(F32)
    row = lax.broadcasted_iota(jnp.int32, (16, 128), 0)
    tiles = [
        jnp.where(row % slots == 0, hid[0:1, t * 128 : (t + 1) * 128], hid[1:2, t * 128 : (t + 1) * 128])
        for t in range(hid.shape[1] // 128)
    ]
    extra = []
    for p in range(chips):
        first = (p * hid.shape[1] // chips) // 128
        held = jnp.zeros((16, 128), F32)
        for i in range(4):
            held = jnp.where(row // slots == i, tiles[first + i], held)
        extra.append(held.astype(BF16))
    parts = []
    position = lax.broadcasted_iota(jnp.int32, (heads, span), 1)
    for s in range(slots):
        copies[s].wait()
        scores = lax.dot_general(
            q[s * heads : (s + 1) * heads, :], keys[s], NT, preferred_element_type=F32
        ) * dim ** (-0.5)
        scores = jnp.where(position < jnp.maximum(lengths_ref[s], 1), scores, -jnp.inf)
        weights = jnp.exp(scores - jnp.max(scores, axis=1, keepdims=True))
        parts.append((weights * (1.0 / jnp.sum(weights, axis=1, keepdims=True))).astype(BF16))
    for s in range(slots):
        copies[slots + s].wait()
        parts[s] = jnp.dot(parts[s], values[s], preferred_element_type=F32).astype(BF16)
    both = jnp.concatenate(parts, axis=0)
    pieces = 16 // slots
    per = heads // pieces
    r = lax.broadcasted_iota(jnp.int32, (16, slots * heads), 0)
    c = lax.broadcasted_iota(jnp.int32, (16, slots * heads), 1)
    rows = []
    for j in range(per):
        take = jnp.where(c == (r % slots) * heads + (r // slots) * per + j, 1.0, 0.0).astype(BF16)
        rows.append(jnp.dot(take, both, preferred_element_type=F32).astype(BF16))
    rows = jnp.concatenate(rows, axis=1)
    for p in range(chips):
        out_ref[p] = jnp.concatenate([rows, extra[p]], axis=1)


def attend(lengths, query, key_cache, value_cache, hidden, token, chips):
    slots, span, dim = key_cache.shape
    hbm = pl.BlockSpec(memory_space=pl.ANY)
    vmem = pl.BlockSpec(memory_space=pltpu.VMEM)
    lanes = query.shape[1] * slots // 16 + 128
    return pl.pallas_call(
        attend_kernel,
        in_specs=[pl.BlockSpec(memory_space=pltpu.SMEM)] + [hbm] * 5,
        out_specs=vmem,
        out_shape=pltpu.HBM((chips, 16, lanes), BF16),
        scratch_shapes=[
            pltpu.VMEM(query.shape, BF16),
            pltpu.VMEM(hidden.shape, BF16),
            pltpu.VMEM(key_cache.shape, BF16),
            pltpu.VMEM(value_cache.shape, BF16),
            pltpu.SemaphoreType.DMA((2,)),
            pltpu.SemaphoreType.DMA((2, slots)),
        ],
        compiler_params=pltpu.CompilerParams(vmem_limit_bytes=12 * 2**20),
    )(in_hbm(lengths), *[in_hbm(v) for v in (query, key_cache, value_cache, hidden)], token)


def project_kernel(
    steps, cols, x_ref, own_ref, oth_ref, gain_ref, *refs
):
    _, _, _, out_hbm, res_ref, x_rows, hid_rows, acc_own, acc_oth, block, out_sem = refs
    step = pl.program_id(0)
    chips, deep, lanes = x_ref.shape
    chunk = own_ref.shape[1]
    slots = 2
    pieces = deep // slots
    rows = chips * slots
    wide = x_rows.shape[1] // pieces

    @pl.when(step == 0)
    def _():
        r = lax.broadcasted_iota(jnp.int32, (chips * deep, chips * deep), 0)
        c = lax.broadcasted_iota(jnp.int32, (chips * deep, chips * deep), 1)
        order = c == (r % rows) // slots * deep + r // rows * slots + r % slots
        order = jnp.where(order, 1.0, 0.0).astype(BF16)
        x = jnp.dot(order, x_ref[...].reshape(chips * deep, lanes), preferred_element_type=F32)
        for i in range(pieces):
            x_rows[:, i * wide : (i + 1) * wide] = x[i * rows : (i + 1) * rows, :wide].astype(BF16)
        for i in range(4):
            hid_rows[i] = x[i * rows : (i + 1) * rows, wide:]

    x = x_rows[:, pl.ds(pl.multiple_of(step * chunk, chunk), chunk)]
    for acc, w in ((acc_own, own_ref), (acc_oth, oth_ref)):
        part = lax.dot_general(x, w[...], NT, preferred_element_type=F32)

        @pl.when(step == 0)
        def _():
            acc[...] = part

        @pl.when(step > 0)
        def _():
            acc[...] += part

    @pl.when(step == steps - 1)
    def _():
        me = lax.axis_index("dev")
        core, chip = me % 2, me // 2
        lane = lax.broadcasted_iota(jnp.int32, (rows, 128), 1)

        def ahead(tiles, shift):
            moved = [pltpu.roll(t, 128 - shift, 1) for t in tiles]
            return [jnp.where(lane < 128 - shift, a, b) for a, b in zip(moved, moved[1:] + moved[-1:])]

        def halves(tiles):
            tiles = [jnp.where(chip % 2 == 0, a, b) for a, b in zip(tiles, ahead(tiles, 64))]
            first = jnp.concatenate(tiles[:2], axis=1)
            second = jnp.concatenate(ahead(tiles[1:], cols - 128)[:2], axis=1)
            return jnp.where(core == 0, first, second), jnp.where(core == 0, second, first)

        hids = halves([hid_rows[i] for i in range(4)])
        start = 7 * (chip // 2) + 3 * (chip % 2)
        gains = halves([jnp.broadcast_to(gain_ref[pl.ds(start + i, 1), :], (rows, 128)) for i in range(4)])
        pad = jnp.zeros((rows, 256 - cols), F32)
        held, sent = [], []
        for acc, hid, gain in zip((acc_own, acc_oth), hids, gains):
            projected = jnp.concatenate([acc[...].astype(BF16).astype(F32), pad], axis=1)
            held.append(hid + projected)
            sent.append(held[-1] * gain)

        first = jnp.where(core == 0, held[0], held[1])
        second = jnp.where(core == 0, held[1], held[0])
        near, far = pltpu.roll(second[:, :128], cols - 128, 1), pltpu.roll(second[:, 128:], cols - 128, 1)
        tiles = [
            first[:, :128],
            jnp.where(lane < cols - 128, first[:, 128:], near),
            jnp.where(lane < cols - 128, near, far),
            jnp.where(lane < 64, far, 0.0),
        ]
        moved = [pltpu.roll(t, 64, 1) for t in tiles]
        for i in range(4):
            before = moved[i - 1] if i else jnp.zeros((rows, 128), F32)
            res_ref[i] = jnp.where(chip % 2 == 0, tiles[i], jnp.where(lane < 64, before, moved[i]))
        own_tail, oth_tail = sent[0][:, 128:], sent[1][:, 128:]
        third = jnp.where(lane < cols - 128, own_tail, pltpu.roll(oth_tail, cols - 128, 1))
        rest = pltpu.roll(oth_tail, 128 - (256 - cols), 1)
        turned = pltpu.roll(rest, 64, 1)
        half = rows // 2
        low = lax.broadcasted_iota(jnp.int32, (half, 128), 1) < 64
        even = jnp.where(low, rest[:half], turned[half:])
        odd = jnp.where(low, rest[half:], turned[:half])
        last = jnp.where(chip % 2 == 0, even, odd)
        packed = jnp.concatenate([sent[0][:, :128], sent[1][:, :128], third, last], axis=0).astype(BF16)
        copies = block.shape[0]
        for p in range(copies):
            block[p] = packed
        outs = []
        for p in range(out_hbm.shape[0] // copies):
            out = pltpu.make_async_copy(block, out_hbm.at[pl.ds(p * copies, copies)], out_sem.at[p])
            out.start()
            outs.append(out)
        for out in outs:
            out.wait()


def in_hbm(v):
    return pltpu.with_memory_space_constraint(v, pltpu.HBM)


def project(messages, gain, out_own, out_oth, arrived, peers):
    cols, depth = out_own.shape
    rows = messages.shape[0] * 2
    packed = rows * 2 * cols // 128
    steps = 1
    chunk = depth // steps
    return pl.pallas_call(
        functools.partial(project_kernel, steps, cols),
        grid=(steps,),
        in_specs=[
            pl.BlockSpec(messages.shape, lambda k: (0, 0, 0)),
            pl.BlockSpec((cols, chunk), lambda k: (0, k)),
            pl.BlockSpec((cols, chunk), lambda k: (0, k)),
            pl.BlockSpec(gain.shape, lambda k: (0, 0)),
        ]
        + [pl.BlockSpec(memory_space=pl.ANY)] * 3,
        out_specs=[
            pl.BlockSpec(memory_space=pl.ANY),
            pl.BlockSpec((4, rows, 128), lambda k: (0, 0, 0)),
        ],
        out_shape=[pltpu.HBM((peers, packed, 128), BF16), pltpu.HBM((4, rows, 128), F32)],
        scratch_shapes=[
            pltpu.VMEM((rows, depth), BF16),
            pltpu.VMEM((4, rows, 128), F32),
            pltpu.VMEM((rows, cols), F32),
            pltpu.VMEM((rows, cols), F32),
            pltpu.VMEM((8, packed, 128), BF16),
            pltpu.SemaphoreType.DMA((peers // 8,)),
        ],
        compiler_params=pltpu.CompilerParams(vmem_limit_bytes=24 * 2**20),
        cost_estimate=pl.CostEstimate(
            flops=4 * rows * cols * depth, bytes_accessed=4 * cols * depth, transcendentals=0
        ),
    )(messages, out_own, out_oth, in_hbm(gain), *arrived)


def ffn_kernel(
    chips, cols, width,
    x_buf, go_ref, gx_ref, uo_ref, ux_ref, do_ref, dx_ref, gain_ref, res_ref, out_hbm, held, out_buf, out_sem,
):
    groups, _, packed, _ = x_buf.shape
    rows = packed * 128 // (2 * cols)
    total = groups * rows
    units = go_ref.shape[1]
    quarter = 4
    parts = chips // quarter
    me = lax.axis_index("dev")
    core, chip = me % 2, me // 2
    spans, span = 8, width // 8
    per = span // 128
    sums = jnp.zeros((total, 4 * units), F32)
    squares = jnp.zeros((total, 128), F32)
    half = rows // 2
    low = lax.broadcasted_iota(jnp.int32, (groups, half, 128), 2) < 64
    lane = lax.broadcasted_iota(jnp.int32, (1, 128), 1)

    def ahead(tiles, shift):
        moved = [pltpu.roll(t, 128 - shift, 1) for t in tiles]
        return [jnp.where(lane < 128 - shift, a, b) for a, b in zip(moved, moved[1:] + moved[-1:])]

    def inverse(b):
        start = 7 * (b // 2) + 3 * (b % 2)
        tiles = [gain_ref[start + i : start + i + 1, :] for i in range(4)]
        if b % 2:
            tiles = ahead(tiles, 64)
        first, last = tiles[:2], ahead(tiles[1:], cols - 128)[:2]
        own = [jnp.where(core == 0, p, q) for p, q in zip(first, last)]
        oth = [jnp.where(core == 0, q, p) for p, q in zip(first, last)]
        third = jnp.where(lane < cols - 128, own[1], pltpu.roll(oth[1], cols - 128, 1))
        return [1.0 / own[0], 1.0 / oth[0], 1.0 / third], pltpu.roll(oth[1], 128 - (256 - cols), 1)

    for q in range(parts):

        def weights(at, size):
            return jnp.concatenate([w[pl.ds(at, size), :] for w in (go_ref, gx_ref, uo_ref, ux_ref)], axis=1)

        tiles, stacks, inverses, rests = [], [], [], {}
        for b in range(q * quarter, (q + 1) * quarter):
            own = pl.multiple_of(2 * cols * b + cols * core, 32)
            oth = pl.multiple_of(2 * cols * b + cols * (1 - core), 32)
            tiles += [x_buf[:, b, i * rows : (i + 1) * rows, :].reshape(total, 128) for i in range(3)]
            stacks += [
                weights(own, 128),
                weights(oth, 128),
                weights(pl.multiple_of(own + 128, 32), cols - 128),
                weights(pl.multiple_of(oth + 128, 32), 256 - cols),
            ]
            inv, rests[b] = inverse(b)
            inverses += inv
        for b in range(q * quarter, (q + 1) * quarter, 2):
            first, second = (x_buf[:, b + i, 3 * rows :, :].astype(F32) for i in range(2))
            top = jnp.where(low, first, second)
            bottom = jnp.where(low, second, first)
            bottom = pltpu.roll(bottom.reshape(groups * half, 128), 64, 1).reshape(groups, half, 128)
            tiles.append(jnp.concatenate([top, bottom], axis=1).reshape(total, 128).astype(BF16))
            inverses.append(1.0 / jnp.where(lane < 64, rests[b], pltpu.roll(rests[b + 1], 64, 1)))
            for i in range(2):
                oth = pl.multiple_of(2 * cols * (b + i) + cols * (1 - core) + (384 - cols), 32)
                stacks.append(weights(oth, 2 * cols - 384))
        x = jnp.concatenate(tiles, axis=1)
        sums += jnp.dot(x, jnp.concatenate(stacks, axis=0), preferred_element_type=F32)
        for tile, inv in zip(tiles, inverses):
            res = tile.astype(F32) * inv
            squares += res * res

    scale = lax.rsqrt(jnp.sum(squares, axis=1, keepdims=True) / width + EPS)
    gate = sums[:, : 2 * units] * scale
    up = sums[:, 2 * units :] * scale
    act = (gate / (1.0 + jnp.exp(-gate)) * up).astype(BF16)

    for b in range(spans):
        some = slice(b * span, (b + 1) * span)
        w = jnp.concatenate([do_ref[some, :], dx_ref[some, :]], axis=1)
        product = lax.dot_general(act, w, NT, preferred_element_type=F32).astype(BF16)
        for t in range(per):
            held[b * per + t] = product[:, t * 128 : (t + 1) * 128]
    mine = pl.multiple_of(rows * lax.axis_index("grp"), rows)
    start = 7 * (chip // 2) + 3 * (chip % 2)
    for i in range(4):
        at = (pl.ds(start + i, 1), pl.ds(mine, rows))
        held[at] = (held[at].astype(F32) + res_ref[i : i + 1]).astype(BF16)

    r = lax.broadcasted_iota(jnp.int32, (128, 128), 0)
    c = lax.broadcasted_iota(jnp.int32, (128, 128), 1)
    peer, piece, slot = r // 16, (r // 2) % spans, r % 2
    order = jnp.where(c == piece * 16 + peer * 2 + slot, 1.0, 0.0).astype(BF16)
    outs = []
    for g in range(total // 16):
        stack = jnp.concatenate(
            [
                jnp.concatenate([held[b * per + t, g * 16 : (g + 1) * 16, :] for t in range(per)], axis=1)
                for b in range(spans)
            ],
            axis=0,
        )
        moved = jnp.dot(order, stack, preferred_element_type=F32).astype(BF16)
        some = pl.ds(g * 8, 8)
        out_buf[g * 8 : (g + 1) * 8] = moved.reshape(8, 16, span)
        outs.append(pltpu.make_async_copy(out_buf.at[some], out_hbm.at[some], out_sem.at[g]))
        outs[-1].start()
    for out in outs:
        out.wait()


def feed_forward(blocks, gate, up, down, gain, residual, chips):
    peers, packed, _ = blocks.shape
    groups = peers // chips
    width, units = gate[0].shape
    cols = width // chips // 2
    rows = packed * 128 // (2 * cols)
    total = groups * rows
    spans = 8
    span = width // spans
    vmem = pl.BlockSpec(memory_space=pltpu.VMEM)
    return pl.pallas_call(
        functools.partial(ffn_kernel, chips, cols, width),
        in_specs=[vmem] * 9,
        out_specs=pl.BlockSpec(memory_space=pl.ANY),
        out_shape=pltpu.HBM((peers, 16, span), BF16),
        scratch_shapes=[
            pltpu.VMEM((width // 128, total, 128), BF16),
            pltpu.VMEM((peers, 16, span), BF16),
            pltpu.SemaphoreType.DMA((total // 16,)),
        ],
        compiler_params=pltpu.CompilerParams(vmem_limit_bytes=28 * 2**20),
        cost_estimate=pl.CostEstimate(
            flops=12 * total * units * width, bytes_accessed=14 * width * units, transcendentals=0
        ),
    )(
        blocks.reshape(groups, chips, packed, 128),
        *gate,
        *up,
        *down,
        gain,
        residual,
    )


def final_kernel(lengths_ref, parts_hbm, out_ref, parts, sems):
    quarter = parts.shape[0] // 4
    copies = []
    for q in range(4):
        some = pl.ds(q * quarter, quarter)
        copies.append(pltpu.make_async_copy(parts_hbm.at[some], parts.at[some], sems.at[q]))
        copies[q].start()
    total = jnp.zeros(parts.shape[1:], F32)
    for q in range(4):
        copies[q].wait()
        for p in range(q * quarter, (q + 1) * quarter):
            total += parts[p].astype(F32)
    row = lax.broadcasted_iota(jnp.int32, total.shape, 0)
    live = jnp.where(row % 2 == 0, lengths_ref[0], lengths_ref[1]) > 0
    total = jnp.where(live, total, 0.0)
    span = total.shape[1]
    for b in range(total.shape[0] // 2):
        out_ref[:, b * span : (b + 1) * span] = total[2 * b : 2 * b + 2].astype(BF16)


def finish(lengths, parts):
    _, rows, span = parts.shape
    return pl.pallas_call(
        final_kernel,
        in_specs=[pl.BlockSpec(memory_space=pltpu.SMEM), pl.BlockSpec(memory_space=pl.ANY)],
        out_specs=pl.BlockSpec(memory_space=pltpu.VMEM),
        out_shape=jax.ShapeDtypeStruct((2, rows * span // 2), BF16),
        scratch_shapes=[pltpu.VMEM(parts.shape, BF16), pltpu.SemaphoreType.DMA((4,))],
        compiler_params=pltpu.CompilerParams(vmem_limit_bytes=16 * 2**20),
    )(in_hbm(lengths), parts)


def make_shards(groups, devs):
    chips = devs // 2
    peers = groups * chips
    plane = [[2 * k + c for k in range(chips)] for c in range(2)]
    cube = [[2 * k + c for k in range(peers)] for c in range(2)]
    other = [(i, i ^ 1) for i in range(devs)]
    links = [[(i, i ^ 2) for i in range(1, devs, 2)]] * HOPS

    def shards(
        query,
        key_cache,
        value_cache,
        lengths,
        hidden,
        out_weight,
        ffn_gain,
        gate_weight,
        up_weight,
        down_weight,
    ):
        slots, width = hidden.shape

        def swap(w):
            return lax.ppermute(w, "dev", other)

        out_own = out_weight.T
        out_oth = swap(out_own)
        gate = (gate_weight, swap(gate_weight))
        up = (up_weight, swap(up_weight))
        down = (down_weight, swap(down_weight))
        token = lengths
        for link in links:
            token = lax.ppermute(token, "dev", link)
        message = attend(lengths, query, key_cache, value_cache, hidden, token, chips)
        got = lax.all_to_all(message, "dev", 0, 0, axis_index_groups=plane)
        gain = ffn_gain.reshape(width // 128, 128)
        block, residual = project(got, gain, out_own, out_oth, (gate[1], up[1], down[1]), peers)

        both = ("grp", "dev")
        blocks = lax.all_to_all(block, both, 0, 0, axis_index_groups=cube)
        partial = feed_forward(blocks, gate, up, down, gain, residual, chips)
        parts = lax.all_to_all(partial, both, 0, 0, axis_index_groups=cube)
        return finish(lengths, parts)

    return shards


def solution(mesh):
    both = ("grp", "dev")
    in_specs = (
        P(both, None),
        P(both, None, None),
        P(both, None, None),
        P(both),
        P(both, None),
        P(None, "dev"),
        P(),
        P(None, both),
        P(None, both),
        P(None, both),
    )
    body = make_shards(mesh.shape["grp"], mesh.shape["dev"])
    return jax.shard_map(body, mesh=mesh, in_specs=in_specs, out_specs=P(both, None), check_vma=False)
```

time: 109 us -> 102 us (0.936)
  the two profiles are of different devices: /device:TPU:0 before, /device:TPU:1 now
where the time goes in v5:
time: 102 us
  blocking collectives  63.5 us (62%)
  Pallas kernels  17.9 us (18%)
  starting transfers between devices  15.7 us (15%)
  waiting for transfers between devices  3.78 us (4%)
    all_to_all x1, blocking collectives, shards(): blocks = lax.all_to_all(block, both, 0, 0, axis_index_groups=cube)  24.2 us
    all_to_all x1, blocking collectives, shards(): parts = lax.all_to_all(partial, both, 0, 0, axis_index_groups=cube)  22.1 us
    all_to_all x1, blocking collectives, shards(): got = lax.all_to_all(message, 'dev', 0, 0, axis_index_groups=plane)  17.2 us
    ppermute x4, starting transfers between devices, shards(): token = lax.ppermute(token, 'dev', link)  13.8 us
    pallas_call x1, Pallas kernels, attend(): pl.pallas_call(attend_kernel, in_specs=[pl.BlockSpec(memory_space=pltpu.S...  5.47 us
    pallas_call x1, Pallas kernels, project(): pl.pallas_call(functools.partial(project_kernel, steps, cols), grid=(step...  5.45 us
    pallas_call x1, Pallas kernels, feed_forward(): pl.pallas_call(functools.partial(ffn_kernel, chips, cols, width), in_spec...  4.32 us
    ppermute x4, waiting for transfers between devices, shards(): token = lax.ppermute(token, 'dev', link)  3.77 us
  transfers between devices with their start and end apart: 8, of which 4 were waited for; matrix products, arithmetic and copies ran while one was open for 0% of the time, Pallas kernels for 5%

profile of v5, /device:TPU:1, one launch (start us, length us, event | category | flops | bytes accessed | tf_op | source)
XLA Modules:
  0.0 101.9 jit_solution(18160493401443280877)
XLA Ops:
  0.0 0.0 copy-start
  0.0 1.4 %collective-permute-start.4 = (bf16[224,8192]{1,0:T(8,128)(2,1)}, bf16[224,8192]{1,0:T(8,128)(2,1)S(1)}, u32[]{:S(2)}, u32[]{:S(2)}) collective-permute-start(bf16[224,8192]{1,0:T(8,128)(2,1)} %bitcast.4), channel_id=1, source_target_pairs={{0,1},{1,0},{2,3},{3,2},{4,5},{5,4},{6,7},{7,6},{8,9},{9,8},{10,11... | collective-permute-start | bytes 11010056 | tf_op jit(solution)/shard_map/ppermute | solution.py:436
  1.4 0.0 collective-permute-start.5
  1.4 0.5 collective-permute-start.6
  1.9 0.0 collective-permute-start.7
  1.9 3.7 %collective-permute-start = (s32[2]{0:T(128)}, s32[2]{0:T(128)S(1)}, u32[]{:S(2)}, u32[]{:S(2)}) collective-permute-start(s32[2]{0:T(128)} %lengths_ref.3), channel_id=1, source_target_pairs={{1,3},{3,1},{5,7},{7,5},{9,11},{11,9},{13,15},{15,13},{17,19},{19,... | collective-permute-start | bytes 32 | tf_op jit(solution)/shard_map/ppermute | solution.py:445
  5.6 1.0 %collective-permute-done = s32[2]{0:T(128)S(1)} collective-permute-done((s32[2]{0:T(128)}, s32[2]{0:T(128)S(1)}, u32[]{:S(2)}, u32[]{:S(2)}) %collective-permute-start) | collective-permute-done | bytes 40 | tf_op jit(solution)/shard_map/ppermute | solution.py:445
  6.7 3.4 %collective-permute-start.1 = (s32[2]{0:T(128)S(1)}, s32[2]{0:T(128)S(1)}, u32[]{:S(2)}, u32[]{:S(2)}) collective-permute-start(s32[2]{0:T(128)S(1)} %collective-permute-done), channel_id=1, source_target_pairs={{1,3},{3,1},{5,7},{7,5},{9,11},{11,9},{13,15},{15,13},{17,19},{19,... | collective-permute-start | bytes 32 | tf_op jit(solution)/shard_map/ppermute | solution.py:445
  10.0 0.9 collective-permute-done.1
  11.0 3.4 %collective-permute-start.2 = (s32[2]{0:T(128)S(1)}, s32[2]{0:T(128)S(1)}, u32[]{:S(2)}, u32[]{:S(2)}) collective-permute-start(s32[2]{0:T(128)S(1)} %collective-permute-done.1), channel_id=1, source_target_pairs={{1,3},{3,1},{5,7},{7,5},{9,11},{11,9},{13,15},{15,13},{17,19},{19,... | collective-permute-start | bytes 32 | tf_op jit(solution)/shard_map/ppermute | solution.py:445
  14.3 0.9 collective-permute-done.2
  15.2 3.4 %collective-permute-start.3 = (s32[2]{0:T(128)S(1)}, s32[2]{0:T(128)S(1)}, u32[]{:S(2)}, u32[]{:S(2)}) collective-permute-start(s32[2]{0:T(128)S(1)} %collective-permute-done.2), channel_id=1, source_target_pairs={{1,3},{3,1},{5,7},{7,5},{9,11},{11,9},{13,15},{15,13},{17,19},{19,... | collective-permute-start | bytes 32 | tf_op jit(solution)/shard_map/ppermute | solution.py:445
  18.6 0.9 collective-permute-done.3.token_hbm
  19.5 5.5 %shard_map.100 = bf16[16,16,1152]{2,1,0:T(8,128)(2,1)} custom-call(s32[2]{0:T(128)} %lengths_ref.3, bf16[2,8192]{1,0:T(2,128)(2,1)} %q_hbm.1, bf16[2,2048,256]{2,1,0:T(8,128)(2,1)} %k_hbm.1, bf16[2,2048,256]{2,1,0:T(8,128)(2,1)} %v_hbm.1, bf16[2,7168]{1,0:T(2,128)(2,1)} %hid_hbm.1, s32[2]{0:T(128)S(1)} %collective-permute-done.3.token_hbm), custom_call_target="tpu_custom_call" | custom-call | tf_op jit(solution)/shard_map/pallas_call | solution.py:85
  25.0 17.2 %all_to_all.15.x_ref = bf16[16,16,1152]{2,1,0:T(8,128)(2,1)S(1)} all-to-all(bf16[16,16,1152]{2,1,0:T(8,128)(2,1)} %shard_map.100), channel_id=1, replica_groups={{0,2,4,6,8,10,12,14,16,18,20,22,24,26,28,30},{1,3,5,7,9,11,13,15,17,19,..., dimensions={0} | all-to-all | bytes 1179648 | tf_op jit(solution)/shard_map/all_to_all | solution.py:447
  42.2 0.0 collective-permute-done.5.refs_0_.gx_ref
  42.2 0.0 collective-permute-done.6.refs_1_.ux_ref
  42.2 0.0 collective-permute-done.7.refs_2_.dx_ref
  42.2 0.0 collective-permute-done.4.oth_ref
  42.2 0.0 copy-done
  42.2 0.0 copy-start.3
  42.3 0.0 copy-start.4
  42.3 5.4 %shard_map.101 = (bf16[64,112,128]{2,1,0:T(8,128)(2,1)}, f32[4,32,128]{2,1,0:T(8,128)}) custom-call(bf16[16,16,1152]{2,1,0:T(8,128)(2,1)S(1)} %all_to_all.15.x_ref, bf16[224,8192]{1,0:T(8,128)(2,1)S(1)} %bitcast.5, bf16[224,8192]{1,0:T(8,128)(2,1)S(1)} %collective-permute-done.4.oth_ref, f32[56,128]{1,0:T(8,128)} %bitcast.6, ...), custom_call_target="tpu_custom_call" | custom-call | flops 234881024 | bytes 7340032 | tf_op jit(solution)/shard_map/pallas_call | solution.py:209
  47.7 0.0 copy-start.1
  47.7 0.0 copy-start.2
  47.7 24.2 %all_to_all.16 = bf16[64,112,128]{2,1,0:T(8,128)(2,1)S(1)} all-to-all(bf16[64,112,128]{2,1,0:T(8,128)(2,1)} %get-tuple-element.7), channel_id=1, replica_groups={{0,2,4,6,8,10,12,14,16,18,20,22,24,26,28,30,32,34,36,38,40,42,44,46,48,..., dimensions={0} | all-to-all | bytes 3670016 | tf_op jit(solution)/shard_map/all_to_all | solution.py:452
  71.9 0.0 copy-done.3
  71.9 0.0 copy-done.4
  71.9 0.0 copy-done.1
  71.9 0.0 copy-done.2
  72.0 0.0 copy-start.5
  72.0 0.8 copy-done.5
  72.8 4.3 %shard_map.102 = bf16[64,16,896]{2,1,0:T(8,128)(2,1)} custom-call(bf16[4,16,112,128]{3,2,1,0:T(8,128)(2,1)S(1)} %bitcast.3, bf16[7168,128]{1,0:T(8,128)(2,1)S(1)} %copy-done.1, bf16[7168,128]{1,0:T(8,128)(2,1)S(1)} %collective-permute-done.5.refs_0_.gx_ref, bf16[7168,128]{1,0:T(8,128)(2,1)S(1)} %copy-done.2, ...), custom_call_target="tpu_custom_call" | custom-call | flops 1409286144 | bytes 12845056 | tf_op jit(solution)/shard_map/pallas_call | solution.py:357
  77.1 22.1 %all_to_all.17.parts_hbm = bf16[64,16,896]{2,1,0:T(8,128)(2,1)S(1)} all-to-all(bf16[64,16,896]{2,1,0:T(8,128)(2,1)} %shard_map.102), channel_id=1, replica_groups={{0,2,4,6,8,10,12,14,16,18,20,22,24,26,28,30,32,34,36,38,40,42,44,46,48,..., dimensions={0} | all-to-all | bytes 3670016 | tf_op jit(solution)/shard_map/all_to_all | solution.py:454
  99.3 2.6 %shard_map.103 = bf16[2,7168]{1,0:T(2,128)(2,1)} custom-call(s32[2]{0:T(128)} %lengths_ref.3, bf16[64,16,896]{2,1,0:T(8,128)(2,1)S(1)} %all_to_all.17.parts_hbm), custom_call_target="tpu_custom_call" | custom-call | tf_op jit(solution)/shard_map/pallas_call | solution.py:403
Async XLA Ops:
  0.0 42.2 %copy-start = (bf16[8192,224]{0,1:T(8,128)(2,1)S(1)}, bf16[8192,224]{0,1:T(8,128)(2,1)}, u32[]{:S(2)}) copy-start(bf16[8192,224]{0,1:T(8,128)(2,1)} %param.15) | copy-start | bytes 11010052
  0.0 42.2 %collective-permute-start.4 = (bf16[224,8192]{1,0:T(8,128)(2,1)}, bf16[224,8192]{1,0:T(8,128)(2,1)S(1)}, u32[]{:S(2)}, u32[]{:S(2)}) collective-permute-start(bf16[224,8192]{1,0:T(8,128)(2,1)} %bitcast.4), channel_id=1, source_target_pairs={{0,1},{1,0},{2,3},{3,2},{4,5},{5,4},{6,7},{7,6},{8,9},{9,8},{10,11... | collective-permute-start | bytes 11010056 | tf_op jit(solution)/shard_map/ppermute | solution.py:436
  1.4 40.8 %collective-permute-start.5 = (bf16[7168,128]{1,0:T(8,128)(2,1)}, bf16[7168,128]{1,0:T(8,128)(2,1)S(1)}, u32[]{:S(2)}, u32[]{:S(2)}) collective-permute-start(bf16[7168,128]{1,0:T(8,128)(2,1)} %go_ref.1), channel_id=1, source_target_pairs={{0,1},{1,0},{2,3},{3,2},{4,5},{5,4},{6,7},{7,6},{8,9},{9,8},{10,11... | collective-permute-start | bytes 5505032 | tf_op jit(solution)/shard_map/ppermute | solution.py:436
  1.4 40.8 %collective-permute-start.6 = (bf16[7168,128]{1,0:T(8,128)(2,1)}, bf16[7168,128]{1,0:T(8,128)(2,1)S(1)}, u32[]{:S(2)}, u32[]{:S(2)}) collective-permute-start(bf16[7168,128]{1,0:T(8,128)(2,1)} %uo_ref.1), channel_id=1, source_target_pairs={{0,1},{1,0},{2,3},{3,2},{4,5},{5,4},{6,7},{7,6},{8,9},{9,8},{10,11... | collective-permute-start | bytes 5505032 | tf_op jit(solution)/shard_map/ppermute | solution.py:436
  1.9 40.3 %collective-permute-start.7 = (bf16[7168,128]{1,0:T(8,128)(2,1)}, bf16[7168,128]{1,0:T(8,128)(2,1)S(1)}, u32[]{:S(2)}, u32[]{:S(2)}) collective-permute-start(bf16[7168,128]{1,0:T(8,128)(2,1)} %do_ref.1), channel_id=1, source_target_pairs={{0,1},{1,0},{2,3},{3,2},{4,5},{5,4},{6,7},{7,6},{8,9},{9,8},{10,11... | collective-permute-start | bytes 5505032 | tf_op jit(solution)/shard_map/ppermute | solution.py:436
  1.9 4.7 %collective-permute-start = (s32[2]{0:T(128)}, s32[2]{0:T(128)S(1)}, u32[]{:S(2)}, u32[]{:S(2)}) collective-permute-start(s32[2]{0:T(128)} %lengths_ref.3), channel_id=1, source_target_pairs={{1,3},{3,1},{5,7},{7,5},{9,11},{11,9},{13,15},{15,13},{17,19},{19,... | collective-permute-start | bytes 32 | tf_op jit(solution)/shard_map/ppermute | solution.py:445
  6.7 4.3 %collective-permute-start.1 = (s32[2]{0:T(128)S(1)}, s32[2]{0:T(128)S(1)}, u32[]{:S(2)}, u32[]{:S(2)}) collective-permute-start(s32[2]{0:T(128)S(1)} %collective-permute-done), channel_id=1, source_target_pairs={{1,3},{3,1},{5,7},{7,5},{9,11},{11,9},{13,15},{15,13},{17,19},{19,... | collective-permute-start | bytes 32 | tf_op jit(solution)/shard_map/ppermute | solution.py:445
  11.0 4.3 %collective-permute-start.2 = (s32[2]{0:T(128)S(1)}, s32[2]{0:T(128)S(1)}, u32[]{:S(2)}, u32[]{:S(2)}) collective-permute-start(s32[2]{0:T(128)S(1)} %collective-permute-done.1), channel_id=1, source_target_pairs={{1,3},{3,1},{5,7},{7,5},{9,11},{11,9},{13,15},{15,13},{17,19},{19,... | collective-permute-start | bytes 32 | tf_op jit(solution)/shard_map/ppermute | solution.py:445
  15.2 4.3 %collective-permute-start.3 = (s32[2]{0:T(128)S(1)}, s32[2]{0:T(128)S(1)}, u32[]{:S(2)}, u32[]{:S(2)}) collective-permute-start(s32[2]{0:T(128)S(1)} %collective-permute-done.2), channel_id=1, source_target_pairs={{1,3},{3,1},{5,7},{7,5},{9,11},{11,9},{13,15},{15,13},{17,19},{19,... | collective-permute-start | bytes 32 | tf_op jit(solution)/shard_map/ppermute | solution.py:445
  42.2 29.7 %copy-start.3 = (bf16[7168,128]{1,0:T(8,128)(2,1)S(1)}, bf16[7168,128]{1,0:T(8,128)(2,1)}, u32[]{:S(2)}) copy-start(bf16[7168,128]{1,0:T(8,128)(2,1)} %do_ref.1) | copy-start | bytes 5505028
  42.3 29.7 %copy-start.4 = (f32[7168]{0:T(1024)S(1)}, f32[7168]{0:T(1024)}, u32[]{:S(2)}) copy-start(f32[7168]{0:T(1024)} %param.16) | copy-start | bytes 86020
  47.7 24.2 %copy-start.1 = (bf16[7168,128]{1,0:T(8,128)(2,1)S(1)}, bf16[7168,128]{1,0:T(8,128)(2,1)}, u32[]{:S(2)}) copy-start(bf16[7168,128]{1,0:T(8,128)(2,1)} %go_ref.1) | copy-start | bytes 5505028
  47.7 24.2 %copy-start.2 = (bf16[7168,128]{1,0:T(8,128)(2,1)S(1)}, bf16[7168,128]{1,0:T(8,128)(2,1)}, u32[]{:S(2)}) copy-start(bf16[7168,128]{1,0:T(8,128)(2,1)} %uo_ref.1) | copy-start | bytes 5505028
  72.0 0.8 copy-start.5

commit v6 on v5

--- a/solution.py
+++ b/solution.py
@@ -11,7 +11,6 @@
 F32 = jnp.float32
 EPS = 1e-05
 VMEM = 32 * 2**20
-HOPS = 4
 NT = (((1,), (1,)), ((), ()))
 
 
@@ -52,16 +51,18 @@
         extra.append(held.astype(BF16))
     parts = []
     position = lax.broadcasted_iota(jnp.int32, (heads, span), 1)
+    for copy in copies[:slots]:
+        copy.wait()
     for s in range(slots):
-        copies[s].wait()
         scores = lax.dot_general(
             q[s * heads : (s + 1) * heads, :], keys[s], NT, preferred_element_type=F32
         ) * dim ** (-0.5)
         scores = jnp.where(position < jnp.maximum(lengths_ref[s], 1), scores, -jnp.inf)
         weights = jnp.exp(scores - jnp.max(scores, axis=1, keepdims=True))
         parts.append((weights * (1.0 / jnp.sum(weights, axis=1, keepdims=True))).astype(BF16))
+    for copy in copies[slots:]:
+        copy.wait()
     for s in range(slots):
-        copies[slots + s].wait()
         parts[s] = jnp.dot(parts[s], values[s], preferred_element_type=F32).astype(BF16)
     both = jnp.concatenate(parts, axis=0)
     pieces = 16 // slots
@@ -238,7 +239,8 @@
 
 def ffn_kernel(
     chips, cols, width,
-    x_buf, go_ref, gx_ref, uo_ref, ux_ref, do_ref, dx_ref, gain_ref, res_ref, out_hbm, held, out_buf, out_sem,
+    x_buf, go_ref, gx_ref, uo_ref, ux_ref, do_ref, dx_ref, gain_ref, res_hbm, out_hbm,
+    held, out_buf, res_ref, res_sem, out_sem,
 ):
     groups, _, packed, _ = x_buf.shape
     rows = packed * 128 // (2 * cols)
@@ -248,6 +250,8 @@
     parts = chips // quarter
     me = lax.axis_index("dev")
     core, chip = me % 2, me // 2
+    res_copy = pltpu.make_async_copy(res_hbm, res_ref, res_sem)
+    res_copy.start()
     spans, span = 8, width // 8
     per = span // 128
     sums = jnp.zeros((total, 4 * units), F32)
@@ -316,6 +320,7 @@
         product = lax.dot_general(act, w, NT, preferred_element_type=F32).astype(BF16)
         for t in range(per):
             held[b * per + t] = product[:, t * 128 : (t + 1) * 128]
+    res_copy.wait()
     mine = pl.multiple_of(rows * lax.axis_index("grp"), rows)
     start = 7 * (chip // 2) + 3 * (chip % 2)
     for i in range(4):
@@ -356,12 +361,14 @@
     vmem = pl.BlockSpec(memory_space=pltpu.VMEM)
     return pl.pallas_call(
         functools.partial(ffn_kernel, chips, cols, width),
-        in_specs=[vmem] * 9,
+        in_specs=[vmem] * 8 + [pl.BlockSpec(memory_space=pl.ANY)],
         out_specs=pl.BlockSpec(memory_space=pl.ANY),
         out_shape=pltpu.HBM((peers, 16, span), BF16),
         scratch_shapes=[
             pltpu.VMEM((width // 128, total, 128), BF16),
             pltpu.VMEM((peers, 16, span), BF16),
+            pltpu.VMEM(residual.shape, F32),
+            pltpu.SemaphoreType.DMA,
             pltpu.SemaphoreType.DMA((total // 16,)),
         ],
         compiler_params=pltpu.CompilerParams(vmem_limit_bytes=28 * 2**20),
@@ -374,22 +381,14 @@
         *up,
         *down,
         gain,
-        residual,
+        in_hbm(residual),
     )
 
 
-def final_kernel(lengths_ref, parts_hbm, out_ref, parts, sems):
-    quarter = parts.shape[0] // 4
-    copies = []
-    for q in range(4):
-        some = pl.ds(q * quarter, quarter)
-        copies.append(pltpu.make_async_copy(parts_hbm.at[some], parts.at[some], sems.at[q]))
-        copies[q].start()
-    total = jnp.zeros(parts.shape[1:], F32)
-    for q in range(4):
-        copies[q].wait()
-        for p in range(q * quarter, (q + 1) * quarter):
-            total += parts[p].astype(F32)
+def final_kernel(lengths_ref, parts_ref, out_ref):
+    total = jnp.zeros(parts_ref.shape[1:], F32)
+    for p in range(parts_ref.shape[0]):
+        total += parts_ref[p].astype(F32)
     row = lax.broadcasted_iota(jnp.int32, total.shape, 0)
     live = jnp.where(row % 2 == 0, lengths_ref[0], lengths_ref[1]) > 0
     total = jnp.where(live, total, 0.0)
@@ -402,10 +401,9 @@
     _, rows, span = parts.shape
     return pl.pallas_call(
         final_kernel,
-        in_specs=[pl.BlockSpec(memory_space=pltpu.SMEM), pl.BlockSpec(memory_space=pl.ANY)],
+        in_specs=[pl.BlockSpec(memory_space=pltpu.SMEM), pl.BlockSpec(memory_space=pltpu.VMEM)],
         out_specs=pl.BlockSpec(memory_space=pltpu.VMEM),
         out_shape=jax.ShapeDtypeStruct((2, rows * span // 2), BF16),
-        scratch_shapes=[pltpu.VMEM(parts.shape, BF16), pltpu.SemaphoreType.DMA((4,))],
         compiler_params=pltpu.CompilerParams(vmem_limit_bytes=16 * 2**20),
     )(in_hbm(lengths), parts)
 
@@ -416,7 +414,11 @@
     plane = [[2 * k + c for k in range(chips)] for c in range(2)]
     cube = [[2 * k + c for k in range(peers)] for c in range(2)]
     other = [(i, i ^ 1) for i in range(devs)]
-    links = [[(i, i ^ 2) for i in range(1, devs, 2)]] * HOPS
+    both = ("grp", "dev")
+    near = [(i, i ^ 2) for i in range(1, groups * devs, 2)]
+    far = [
+        (x * devs + i, (x + groups // 2) % groups * devs + (i + devs // 2 + 4) % devs) for x in range(groups) for i in range(1, devs, 2)
+    ]
 
     def shards(
         query,
@@ -441,14 +443,13 @@
         up = (up_weight, swap(up_weight))
         down = (down_weight, swap(down_weight))
         token = lengths
-        for link in links:
-            token = lax.ppermute(token, "dev", link)
+        for link in (far, near):
+            token = lax.ppermute(token, both, link)
         message = attend(lengths, query, key_cache, value_cache, hidden, token, chips)
         got = lax.all_to_all(message, "dev", 0, 0, axis_index_groups=plane)
         gain = ffn_gain.reshape(width // 128, 128)
         block, residual = project(got, gain, out_own, out_oth, (gate[1], up[1], down[1]), peers)
 
-        both = ("grp", "dev")
         blocks = lax.all_to_all(block, both, 0, 0, axis_index_groups=cube)
         partial = feed_forward(blocks, gate, up, down, gain, residual, chips)
         parts = lax.all_to_all(partial, both, 0, 0, axis_index_groups=cube)

time: 102 us -> 99 us (0.971)
  waiting for transfers between devices: 3.78 us -> 2.47 us
  Pallas kernels: 17.9 us -> 16.8 us
    ppermute x4 -> x2, waiting for transfers between devices: 3.77 us -> 2.46 us  [shards(): token = lax.ppermute(token, both, link)]
    pallas_call x1, Pallas kernels: 2.64 us -> 1.52 us  [finish(): pl.pallas_call(final_kernel, in_specs=[pl.BlockSpec(memory_space=pltpu.SM...]
    ppermute x4 -> x2, starting transfers between devices: 13.8 us -> 13.4 us  [shards(): token = lax.ppermute(token, both, link)]
  transfers between devices with their start and end apart: 8 -> 6, of which waited for: 4 -> 2; matrix products, arithmetic and copies ran while one was open for 0% -> 0% of each run, Pallas kernels for 5% -> 5%
where the time goes in v6:
time: 99 us; the launch traced here: 98.5 us
  blocking collectives  63.8 us (64%)
  Pallas kernels  16.8 us (17%)
  starting transfers between devices  15.3 us (15%)
  waiting for transfers between devices  2.47 us (2%)
    all_to_all x1, blocking collectives, shards(): blocks = lax.all_to_all(block, both, 0, 0, axis_index_groups=cube)  24.2 us
    all_to_all x1, blocking collectives, shards(): parts = lax.all_to_all(partial, both, 0, 0, axis_index_groups=cube)  23.1 us
    all_to_all x1, blocking collectives, shards(): got = lax.all_to_all(message, 'dev', 0, 0, axis_index_groups=plane)  16.5 us
    ppermute x2, starting transfers between devices, shards(): token = lax.ppermute(token, both, link)  13.4 us
    pallas_call x1, Pallas kernels, project(): pl.pallas_call(functools.partial(project_kernel, steps, cols), grid=(step...  5.43 us
    pallas_call x1, Pallas kernels, feed_forward(): pl.pallas_call(functools.partial(ffn_kernel, chips, cols, width), in_spec...  5 us
    pallas_call x1, Pallas kernels, attend(): pl.pallas_call(attend_kernel, in_specs=[pl.BlockSpec(memory_space=pltpu.S...  4.85 us
    ppermute x2, waiting for transfers between devices, shards(): token = lax.ppermute(token, both, link)  2.46 us
  transfers between devices with their start and end apart: 6, of which 2 were waited for; matrix products, arithmetic and copies ran while one was open for 0% of the time, Pallas kernels for 5%

profile of v6, /device:TPU:1, one launch (start us, length us, event | category | flops | bytes accessed | tf_op | source)
XLA Modules:
  0.0 98.5 jit_solution(14823108849779346616)
XLA Ops:
  0.0 0.0 copy-start
  0.0 1.4 %collective-permute-start.2 = (bf16[224,8192]{1,0:T(8,128)(2,1)}, bf16[224,8192]{1,0:T(8,128)(2,1)S(1)}, u32[]{:S(2)}, u32[]{:S(2)}) collective-permute-start(bf16[224,8192]{1,0:T(8,128)(2,1)} %bitcast.4), channel_id=1, source_target_pairs={{0,1},{1,0},{2,3},{3,2},{4,5},{5,4},{6,7},{7,6},{8,9},{9,8},{10,11... | collective-permute-start | bytes 11010056 | tf_op jit(solution)/shard_map/ppermute | solution.py:438
  1.4 0.0 collective-permute-start.3
  1.4 0.5 collective-permute-start.4
  1.9 0.0 collective-permute-start.5
  1.9 10.7 %collective-permute-start = (s32[2]{0:T(128)}, s32[2]{0:T(128)S(1)}, u32[]{:S(2)}, u32[]{:S(2)}) collective-permute-start(s32[2]{0:T(128)} %lengths_ref.3), channel_id=1, source_target_pairs={{1,85},{3,87},{5,89},{7,91},{9,93},{11,95},{13,65},{15,67},{17,69}... | collective-permute-start | bytes 32 | tf_op jit(solution)/shard_map/ppermute | solution.py:447
  12.7 0.8 collective-permute-done
  13.5 2.6 %collective-permute-start.1 = (s32[2]{0:T(128)S(1)}, s32[2]{0:T(128)S(1)}, u32[]{:S(2)}, u32[]{:S(2)}) collective-permute-start(s32[2]{0:T(128)S(1)} %collective-permute-done), channel_id=1, source_target_pairs={{1,3},{3,1},{5,7},{7,5},{9,11},{11,9},{13,15},{15,13},{17,19},{19,... | collective-permute-start | bytes 32 | tf_op jit(solution)/shard_map/ppermute | solution.py:447
  16.2 1.6 %collective-permute-done.1.token_hbm = s32[2]{0:T(128)S(1)} collective-permute-done((s32[2]{0:T(128)S(1)}, s32[2]{0:T(128)S(1)}, u32[]{:S(2)}, u32[]{:S(2)}) %collective-permute-start.1) | collective-permute-done | bytes 40 | tf_op jit(solution)/shard_map/ppermute | solution.py:447
  17.8 4.9 %shard_map.100 = bf16[16,16,1152]{2,1,0:T(8,128)(2,1)} custom-call(s32[2]{0:T(128)} %lengths_ref.3, bf16[2,8192]{1,0:T(2,128)(2,1)} %q_hbm.1, bf16[2,2048,256]{2,1,0:T(8,128)(2,1)} %k_hbm.1, bf16[2,2048,256]{2,1,0:T(8,128)(2,1)} %v_hbm.1, bf16[2,7168]{1,0:T(2,128)(2,1)} %hid_hbm.1, s32[2]{0:T(128)S(1)} %collective-permute-done.1.token_hbm), custom_call_target="tpu_custom_call" | custom-call | tf_op jit(solution)/shard_map/pallas_call | solution.py:86
  22.7 16.5 %all_to_all.15.x_ref = bf16[16,16,1152]{2,1,0:T(8,128)(2,1)S(1)} all-to-all(bf16[16,16,1152]{2,1,0:T(8,128)(2,1)} %shard_map.100), channel_id=1, replica_groups={{0,2,4,6,8,10,12,14,16,18,20,22,24,26,28,30},{1,3,5,7,9,11,13,15,17,19,..., dimensions={0} | all-to-all | bytes 1179648 | tf_op jit(solution)/shard_map/all_to_all | solution.py:449
  39.2 0.0 collective-permute-done.3.refs_0_.gx_ref
  39.2 0.0 collective-permute-done.4.refs_1_.ux_ref
  39.2 0.0 collective-permute-done.5.refs_2_.dx_ref
  39.2 0.0 collective-permute-done.2.oth_ref
  39.2 0.0 copy-done
  39.2 0.0 copy-start.3
  39.2 0.0 copy-start.4
  39.2 5.4 %shard_map.101 = (bf16[64,112,128]{2,1,0:T(8,128)(2,1)}, f32[4,32,128]{2,1,0:T(8,128)}) custom-call(bf16[16,16,1152]{2,1,0:T(8,128)(2,1)S(1)} %all_to_all.15.x_ref, bf16[224,8192]{1,0:T(8,128)(2,1)S(1)} %bitcast.5, bf16[224,8192]{1,0:T(8,128)(2,1)S(1)} %collective-permute-done.2.oth_ref, f32[56,128]{1,0:T(8,128)} %bitcast.6, ...), custom_call_target="tpu_custom_call" | custom-call | flops 234881024 | bytes 7340032 | tf_op jit(solution)/shard_map/pallas_call | solution.py:210
  44.7 0.0 copy-start.1
  44.7 0.0 copy-start.2
  44.7 24.2 %all_to_all.16 = bf16[64,112,128]{2,1,0:T(8,128)(2,1)S(1)} all-to-all(bf16[64,112,128]{2,1,0:T(8,128)(2,1)} %get-tuple-element.7), channel_id=1, replica_groups={{0,2,4,6,8,10,12,14,16,18,20,22,24,26,28,30,32,34,36,38,40,42,44,46,48,..., dimensions={0} | all-to-all | bytes 3670016 | tf_op jit(solution)/shard_map/all_to_all | solution.py:453
  68.9 0.0 copy-done.3
  68.9 0.0 copy-done.4
  68.9 0.0 copy-done.1
  68.9 0.0 copy-done.2
  68.9 5.0 %shard_map.102 = bf16[64,16,896]{2,1,0:T(8,128)(2,1)} custom-call(bf16[4,16,112,128]{3,2,1,0:T(8,128)(2,1)S(1)} %bitcast.3, bf16[7168,128]{1,0:T(8,128)(2,1)S(1)} %copy-done.1, bf16[7168,128]{1,0:T(8,128)(2,1)S(1)} %collective-permute-done.3.refs_0_.gx_ref, bf16[7168,128]{1,0:T(8,128)(2,1)S(1)} %copy-done.2, ...), custom_call_target="tpu_custom_call" | custom-call | flops 1409286144 | bytes 12845056 | tf_op jit(solution)/shard_map/pallas_call | solution.py:362
  73.9 23.1 %all_to_all.17.parts_ref = bf16[64,16,896]{2,1,0:T(8,128)(2,1)S(1)} all-to-all(bf16[64,16,896]{2,1,0:T(8,128)(2,1)} %shard_map.102), channel_id=1, replica_groups={{0,2,4,6,8,10,12,14,16,18,20,22,24,26,28,30,32,34,36,38,40,42,44,46,48,..., dimensions={0} | all-to-all | bytes 3670016 | tf_op jit(solution)/shard_map/all_to_all | solution.py:455
  97.0 1.5 %shard_map.103 = bf16[2,7168]{1,0:T(2,128)(2,1)} custom-call(s32[2]{0:T(128)} %lengths_ref.3, bf16[64,16,896]{2,1,0:T(8,128)(2,1)S(1)} %all_to_all.17.parts_ref), custom_call_target="tpu_custom_call" | custom-call | tf_op jit(solution)/shard_map/pallas_call | solution.py:402
Async XLA Ops:
  0.0 39.2 %copy-start = (bf16[8192,224]{0,1:T(8,128)(2,1)S(1)}, bf16[8192,224]{0,1:T(8,128)(2,1)}, u32[]{:S(2)}) copy-start(bf16[8192,224]{0,1:T(8,128)(2,1)} %param.15) | copy-start | bytes 11010052
  0.0 39.2 %collective-permute-start.2 = (bf16[224,8192]{1,0:T(8,128)(2,1)}, bf16[224,8192]{1,0:T(8,128)(2,1)S(1)}, u32[]{:S(2)}, u32[]{:S(2)}) collective-permute-start(bf16[224,8192]{1,0:T(8,128)(2,1)} %bitcast.4), channel_id=1, source_target_pairs={{0,1},{1,0},{2,3},{3,2},{4,5},{5,4},{6,7},{7,6},{8,9},{9,8},{10,11... | collective-permute-start | bytes 11010056 | tf_op jit(solution)/shard_map/ppermute | solution.py:438
  1.4 37.8 %collective-permute-start.3 = (bf16[7168,128]{1,0:T(8,128)(2,1)}, bf16[7168,128]{1,0:T(8,128)(2,1)S(1)}, u32[]{:S(2)}, u32[]{:S(2)}) collective-permute-start(bf16[7168,128]{1,0:T(8,128)(2,1)} %go_ref.1), channel_id=1, source_target_pairs={{0,1},{1,0},{2,3},{3,2},{4,5},{5,4},{6,7},{7,6},{8,9},{9,8},{10,11... | collective-permute-start | bytes 5505032 | tf_op jit(solution)/shard_map/ppermute | solution.py:438
  1.4 37.7 %collective-permute-start.4 = (bf16[7168,128]{1,0:T(8,128)(2,1)}, bf16[7168,128]{1,0:T(8,128)(2,1)S(1)}, u32[]{:S(2)}, u32[]{:S(2)}) collective-permute-start(bf16[7168,128]{1,0:T(8,128)(2,1)} %uo_ref.1), channel_id=1, source_target_pairs={{0,1},{1,0},{2,3},{3,2},{4,5},{5,4},{6,7},{7,6},{8,9},{9,8},{10,11... | collective-permute-start | bytes 5505032 | tf_op jit(solution)/shard_map/ppermute | solution.py:438
  1.9 37.2 %collective-permute-start.5 = (bf16[7168,128]{1,0:T(8,128)(2,1)}, bf16[7168,128]{1,0:T(8,128)(2,1)S(1)}, u32[]{:S(2)}, u32[]{:S(2)}) collective-permute-start(bf16[7168,128]{1,0:T(8,128)(2,1)} %do_ref.1), channel_id=1, source_target_pairs={{0,1},{1,0},{2,3},{3,2},{4,5},{5,4},{6,7},{7,6},{8,9},{9,8},{10,11... | collective-permute-start | bytes 5505032 | tf_op jit(solution)/shard_map/ppermute | solution.py:438
  1.9 11.6 %collective-permute-start = (s32[2]{0:T(128)}, s32[2]{0:T(128)S(1)}, u32[]{:S(2)}, u32[]{:S(2)}) collective-permute-start(s32[2]{0:T(128)} %lengths_ref.3), channel_id=1, source_target_pairs={{1,85},{3,87},{5,89},{7,91},{9,93},{11,95},{13,65},{15,67},{17,69}... | collective-permute-start | bytes 32 | tf_op jit(solution)/shard_map/ppermute | solution.py:447
  13.5 4.3 %collective-permute-start.1 = (s32[2]{0:T(128)S(1)}, s32[2]{0:T(128)S(1)}, u32[]{:S(2)}, u32[]{:S(2)}) collective-permute-start(s32[2]{0:T(128)S(1)} %collective-permute-done), channel_id=1, source_target_pairs={{1,3},{3,1},{5,7},{7,5},{9,11},{11,9},{13,15},{15,13},{17,19},{19,... | collective-permute-start | bytes 32 | tf_op jit(solution)/shard_map/ppermute | solution.py:447
  39.2 29.7 %copy-start.3 = (bf16[7168,128]{1,0:T(8,128)(2,1)S(1)}, bf16[7168,128]{1,0:T(8,128)(2,1)}, u32[]{:S(2)}) copy-start(bf16[7168,128]{1,0:T(8,128)(2,1)} %do_ref.1) | copy-start | bytes 5505028
  39.2 29.7 %copy-start.4 = (f32[7168]{0:T(1024)S(1)}, f32[7168]{0:T(1024)}, u32[]{:S(2)}) copy-start(f32[7168]{0:T(1024)} %param.16) | copy-start | bytes 86020
  44.7 24.2 %copy-start.1 = (bf16[7168,128]{1,0:T(8,128)(2,1)S(1)}, bf16[7168,128]{1,0:T(8,128)(2,1)}, u32[]{:S(2)}) copy-start(bf16[7168,128]{1,0:T(8,128)(2,1)} %go_ref.1) | copy-start | bytes 5505028
  44.7 24.2 %copy-start.2 = (bf16[7168,128]{1,0:T(8,128)(2,1)S(1)}, bf16[7168,128]{1,0:T(8,128)(2,1)}, u32[]{:S(2)}) copy-start(bf16[7168,128]{1,0:T(8,128)(2,1)} %uo_ref.1) | copy-start | bytes 5505028

commit v7 on v6

--- a/solution.py
+++ b/solution.py
@@ -53,17 +53,17 @@
     position = lax.broadcasted_iota(jnp.int32, (heads, span), 1)
     for copy in copies[:slots]:
         copy.wait()
-    for s in range(slots):
-        scores = lax.dot_general(
-            q[s * heads : (s + 1) * heads, :], keys[s], NT, preferred_element_type=F32
-        ) * dim ** (-0.5)
-        scores = jnp.where(position < jnp.maximum(lengths_ref[s], 1), scores, -jnp.inf)
-        weights = jnp.exp(scores - jnp.max(scores, axis=1, keepdims=True))
-        parts.append((weights * (1.0 / jnp.sum(weights, axis=1, keepdims=True))).astype(BF16))
+    scores = [
+        lax.dot_general(q[s * heads : (s + 1) * heads, :], keys[s], NT, preferred_element_type=F32)
+        for s in range(slots)
+    ]
     for copy in copies[slots:]:
         copy.wait()
     for s in range(slots):
-        parts[s] = jnp.dot(parts[s], values[s], preferred_element_type=F32).astype(BF16)
+        score = jnp.where(position < jnp.maximum(lengths_ref[s], 1), scores[s] * dim ** (-0.5), -jnp.inf)
+        weights = jnp.exp(score - jnp.max(score, axis=1, keepdims=True))
+        probs = (weights * (1.0 / jnp.sum(weights, axis=1, keepdims=True))).astype(BF16)
+        parts.append(jnp.dot(probs, values[s], preferred_element_type=F32).astype(BF16))
     both = jnp.concatenate(parts, axis=0)
     pieces = 16 // slots
     per = heads // pieces
@@ -100,101 +100,82 @@
     )(in_hbm(lengths), *[in_hbm(v) for v in (query, key_cache, value_cache, hidden)], token)
 
 
-def project_kernel(
-    steps, cols, x_ref, own_ref, oth_ref, gain_ref, *refs
-):
-    _, _, _, out_hbm, res_ref, x_rows, hid_rows, acc_own, acc_oth, block, out_sem = refs
-    step = pl.program_id(0)
+def project_kernel(cols, x_ref, own, oth, gain_hbm, *refs):
+    out_hbm, res_hbm, gain_ref, res_ref, block, gain_sem, res_sem, out_sem = refs[-8:]
+    gain_copy = pltpu.make_async_copy(gain_hbm, gain_ref, gain_sem)
+    gain_copy.start()
     chips, deep, lanes = x_ref.shape
-    chunk = own_ref.shape[1]
     slots = 2
     pieces = deep // slots
     rows = chips * slots
-    wide = x_rows.shape[1] // pieces
-
-    @pl.when(step == 0)
-    def _():
-        r = lax.broadcasted_iota(jnp.int32, (chips * deep, chips * deep), 0)
-        c = lax.broadcasted_iota(jnp.int32, (chips * deep, chips * deep), 1)
-        order = c == (r % rows) // slots * deep + r // rows * slots + r % slots
-        order = jnp.where(order, 1.0, 0.0).astype(BF16)
-        x = jnp.dot(order, x_ref[...].reshape(chips * deep, lanes), preferred_element_type=F32)
-        for i in range(pieces):
-            x_rows[:, i * wide : (i + 1) * wide] = x[i * rows : (i + 1) * rows, :wide].astype(BF16)
-        for i in range(4):
-            hid_rows[i] = x[i * rows : (i + 1) * rows, wide:]
-
-    x = x_rows[:, pl.ds(pl.multiple_of(step * chunk, chunk), chunk)]
-    for acc, w in ((acc_own, own_ref), (acc_oth, oth_ref)):
-        part = lax.dot_general(x, w[...], NT, preferred_element_type=F32)
-
-        @pl.when(step == 0)
-        def _():
-            acc[...] = part
-
-        @pl.when(step > 0)
-        def _():
-            acc[...] += part
-
-    @pl.when(step == steps - 1)
-    def _():
-        me = lax.axis_index("dev")
-        core, chip = me % 2, me // 2
-        lane = lax.broadcasted_iota(jnp.int32, (rows, 128), 1)
-
-        def ahead(tiles, shift):
-            moved = [pltpu.roll(t, 128 - shift, 1) for t in tiles]
-            return [jnp.where(lane < 128 - shift, a, b) for a, b in zip(moved, moved[1:] + moved[-1:])]
-
-        def halves(tiles):
-            tiles = [jnp.where(chip % 2 == 0, a, b) for a, b in zip(tiles, ahead(tiles, 64))]
-            first = jnp.concatenate(tiles[:2], axis=1)
-            second = jnp.concatenate(ahead(tiles[1:], cols - 128)[:2], axis=1)
-            return jnp.where(core == 0, first, second), jnp.where(core == 0, second, first)
-
-        hids = halves([hid_rows[i] for i in range(4)])
-        start = 7 * (chip // 2) + 3 * (chip % 2)
-        gains = halves([jnp.broadcast_to(gain_ref[pl.ds(start + i, 1), :], (rows, 128)) for i in range(4)])
-        pad = jnp.zeros((rows, 256 - cols), F32)
-        held, sent = [], []
-        for acc, hid, gain in zip((acc_own, acc_oth), hids, gains):
-            projected = jnp.concatenate([acc[...].astype(BF16).astype(F32), pad], axis=1)
-            held.append(hid + projected)
-            sent.append(held[-1] * gain)
-
-        first = jnp.where(core == 0, held[0], held[1])
-        second = jnp.where(core == 0, held[1], held[0])
-        near, far = pltpu.roll(second[:, :128], cols - 128, 1), pltpu.roll(second[:, 128:], cols - 128, 1)
-        tiles = [
-            first[:, :128],
-            jnp.where(lane < cols - 128, first[:, 128:], near),
-            jnp.where(lane < cols - 128, near, far),
-            jnp.where(lane < 64, far, 0.0),
-        ]
-        moved = [pltpu.roll(t, 64, 1) for t in tiles]
-        for i in range(4):
-            before = moved[i - 1] if i else jnp.zeros((rows, 128), F32)
-            res_ref[i] = jnp.where(chip % 2 == 0, tiles[i], jnp.where(lane < 64, before, moved[i]))
-        own_tail, oth_tail = sent[0][:, 128:], sent[1][:, 128:]
-        third = jnp.where(lane < cols - 128, own_tail, pltpu.roll(oth_tail, cols - 128, 1))
-        rest = pltpu.roll(oth_tail, 128 - (256 - cols), 1)
-        turned = pltpu.roll(rest, 64, 1)
-        half = rows // 2
-        low = lax.broadcasted_iota(jnp.int32, (half, 128), 1) < 64
-        even = jnp.where(low, rest[:half], turned[half:])
-        odd = jnp.where(low, rest[half:], turned[:half])
-        last = jnp.where(chip % 2 == 0, even, odd)
-        packed = jnp.concatenate([sent[0][:, :128], sent[1][:, :128], third, last], axis=0).astype(BF16)
-        copies = block.shape[0]
-        for p in range(copies):
-            block[p] = packed
-        outs = []
-        for p in range(out_hbm.shape[0] // copies):
-            out = pltpu.make_async_copy(block, out_hbm.at[pl.ds(p * copies, copies)], out_sem.at[p])
-            out.start()
-            outs.append(out)
-        for out in outs:
-            out.wait()
+    wide = own.shape[1] // pieces
+    r = lax.broadcasted_iota(jnp.int32, (chips * deep, chips * deep), 0)
+    c = lax.broadcasted_iota(jnp.int32, (chips * deep, chips * deep), 1)
+    order = c == (r % rows) // slots * deep + r // rows * slots + r % slots
+    order = jnp.where(order, 1.0, 0.0).astype(BF16)
+    x = jnp.dot(order, x_ref[...].reshape(chips * deep, lanes), preferred_element_type=F32)
+    hid_rows = [x[i * rows : (i + 1) * rows, wide:] for i in range(4)]
+    x = jnp.concatenate([x[i * rows : (i + 1) * rows, :wide] for i in range(pieces)], axis=1).astype(BF16)
+    sums = [lax.dot_general(x, w[...], NT, preferred_element_type=F32) for w in (own, oth)]
+    me = lax.axis_index("dev")
+    core, chip = me % 2, me // 2
+    lane = lax.broadcasted_iota(jnp.int32, (rows, 128), 1)
+
+    def ahead(tiles, shift):
+        moved = [pltpu.roll(t, 128 - shift, 1) for t in tiles]
+        return [jnp.where(lane < 128 - shift, a, b) for a, b in zip(moved, moved[1:] + moved[-1:])]
+
+    def halves(tiles):
+        tiles = [jnp.where(chip % 2 == 0, a, b) for a, b in zip(tiles, ahead(tiles, 64))]
+        first = jnp.concatenate(tiles[:2], axis=1)
+        second = jnp.concatenate(ahead(tiles[1:], cols - 128)[:2], axis=1)
+        return jnp.where(core == 0, first, second), jnp.where(core == 0, second, first)
+
+    hids = halves(hid_rows)
+    start = 7 * (chip // 2) + 3 * (chip % 2)
+    gain_copy.wait()
+    gains = halves([jnp.broadcast_to(gain_ref[pl.ds(start + i, 1), :], (rows, 128)) for i in range(4)])
+    pad = jnp.zeros((rows, 256 - cols), F32)
+    held, sent = [], []
+    for acc, hid, gain in zip(sums, hids, gains):
+        projected = jnp.concatenate([acc.astype(BF16).astype(F32), pad], axis=1)
+        held.append(hid + projected)
+        sent.append(held[-1] * gain)
+
+    first = jnp.where(core == 0, held[0], held[1])
+    second = jnp.where(core == 0, held[1], held[0])
+    near, far = pltpu.roll(second[:, :128], cols - 128, 1), pltpu.roll(second[:, 128:], cols - 128, 1)
+    tiles = [
+        first[:, :128],
+        jnp.where(lane < cols - 128, first[:, 128:], near),
+        jnp.where(lane < cols - 128, near, far),
+        jnp.where(lane < 64, far, 0.0),
+    ]
+    moved = [pltpu.roll(t, 64, 1) for t in tiles]
+    for i in range(4):
+        before = moved[i - 1] if i else jnp.zeros((rows, 128), F32)
+        res_ref[i] = jnp.where(chip % 2 == 0, tiles[i], jnp.where(lane < 64, before, moved[i]))
+    own_tail, oth_tail = sent[0][:, 128:], sent[1][:, 128:]
+    third = jnp.where(lane < cols - 128, own_tail, pltpu.roll(oth_tail, cols - 128, 1))
+    rest = pltpu.roll(oth_tail, 128 - (256 - cols), 1)
+    turned = pltpu.roll(rest, 64, 1)
+    half = rows // 2
+    low = lax.broadcasted_iota(jnp.int32, (half, 128), 1) < 64
+    even = jnp.where(low, rest[:half], turned[half:])
+    odd = jnp.where(low, rest[half:], turned[:half])
+    last = jnp.where(chip % 2 == 0, even, odd)
+    packed = jnp.concatenate([sent[0][:, :128], sent[1][:, :128], third, last], axis=0).astype(BF16)
+    many = block.shape[0]
+    for p in range(many):
+        block[p] = packed
+    outs = [pltpu.make_async_copy(res_ref, res_hbm, res_sem)]
+    outs[0].start()
+    for p in range(out_hbm.shape[0] // many):
+        out = pltpu.make_async_copy(block, out_hbm.at[pl.ds(p * many, many)], out_sem.at[p])
+        out.start()
+        outs.append(out)
+    for out in outs:
+        out.wait()
 
 
 def in_hbm(v):
@@ -205,29 +186,18 @@
     cols, depth = out_own.shape
     rows = messages.shape[0] * 2
     packed = rows * 2 * cols // 128
-    steps = 1
-    chunk = depth // steps
+    hbm = pl.BlockSpec(memory_space=pl.ANY)
     return pl.pallas_call(
-        functools.partial(project_kernel, steps, cols),
-        grid=(steps,),
-        in_specs=[
-            pl.BlockSpec(messages.shape, lambda k: (0, 0, 0)),
-            pl.BlockSpec((cols, chunk), lambda k: (0, k)),
-            pl.BlockSpec((cols, chunk), lambda k: (0, k)),
-            pl.BlockSpec(gain.shape, lambda k: (0, 0)),
-        ]
-        + [pl.BlockSpec(memory_space=pl.ANY)] * 3,
-        out_specs=[
-            pl.BlockSpec(memory_space=pl.ANY),
-            pl.BlockSpec((4, rows, 128), lambda k: (0, 0, 0)),
-        ],
+        functools.partial(project_kernel, cols),
+        in_specs=[pl.BlockSpec(memory_space=pltpu.VMEM)] * 3 + [hbm] * (1 + len(arrived)),
+        out_specs=[hbm, hbm],
         out_shape=[pltpu.HBM((peers, packed, 128), BF16), pltpu.HBM((4, rows, 128), F32)],
         scratch_shapes=[
-            pltpu.VMEM((rows, depth), BF16),
+            pltpu.VMEM(gain.shape, F32),
             pltpu.VMEM((4, rows, 128), F32),
-            pltpu.VMEM((rows, cols), F32),
-            pltpu.VMEM((rows, cols), F32),
             pltpu.VMEM((8, packed, 128), BF16),
+            pltpu.SemaphoreType.DMA,
+            pltpu.SemaphoreType.DMA,
             pltpu.SemaphoreType.DMA((peers // 8,)),
         ],
         compiler_params=pltpu.CompilerParams(vmem_limit_bytes=24 * 2**20),
@@ -309,6 +279,7 @@
             res = tile.astype(F32) * inv
             squares += res * res
 
+    res_copy.wait()
     scale = lax.rsqrt(jnp.sum(squares, axis=1, keepdims=True) / width + EPS)
     gate = sums[:, : 2 * units] * scale
     up = sums[:, 2 * units :] * scale
@@ -320,7 +291,6 @@
         product = lax.dot_general(act, w, NT, preferred_element_type=F32).astype(BF16)
         for t in range(per):
             held[b * per + t] = product[:, t * 128 : (t + 1) * 128]
-    res_copy.wait()
     mine = pl.multiple_of(rows * lax.axis_index("grp"), rows)
     start = 7 * (chip // 2) + 3 * (chip % 2)
     for i in range(4):

time: 99 us -> 98 us (0.990)
  Pallas kernels: 16.8 us -> 15.8 us
where the time goes in v7:
time: 98 us; the launch traced here: 97.5 us
  blocking collectives  63.7 us (65%)
  Pallas kernels  15.8 us (16%)
  starting transfers between devices  15.3 us (16%)
  waiting for transfers between devices  2.47 us (3%)
    all_to_all x1, blocking collectives, shards(): blocks = lax.all_to_all(block, both, 0, 0, axis_index_groups=cube)  24.2 us
    all_to_all x1, blocking collectives, shards(): parts = lax.all_to_all(partial, both, 0, 0, axis_index_groups=cube)  22.8 us
    all_to_all x1, blocking collectives, shards(): got = lax.all_to_all(message, 'dev', 0, 0, axis_index_groups=plane)  16.7 us
    ppermute x2, starting transfers between devices, shards(): token = lax.ppermute(token, both, link)  13.4 us
    pallas_call x1, Pallas kernels, feed_forward(): pl.pallas_call(functools.partial(ffn_kernel, chips, cols, width), in_spec...  4.81 us
    pallas_call x1, Pallas kernels, attend(): pl.pallas_call(attend_kernel, in_specs=[pl.BlockSpec(memory_space=pltpu.S...  4.76 us
    pallas_call x1, Pallas kernels, project(): pl.pallas_call(functools.partial(project_kernel, cols), in_specs=[pl.Bloc...  4.72 us
    ppermute x2, waiting for transfers between devices, shards(): token = lax.ppermute(token, both, link)  2.46 us
  transfers between devices with their start and end apart: 6, of which 2 were waited for; matrix products, arithmetic and copies ran while one was open for 0% of the time, Pallas kernels for 5%

profile of v7, /device:TPU:1, one launch (start us, length us, event | category | flops | bytes accessed | tf_op | source)
XLA Modules:
  0.0 97.5 jit_solution(3185986121556644140)
XLA Ops:
  0.0 0.0 copy-start
  0.0 1.4 %collective-permute-start.2 = (bf16[224,8192]{1,0:T(8,128)(2,1)}, bf16[224,8192]{1,0:T(8,128)(2,1)S(1)}, u32[]{:S(2)}, u32[]{:S(2)}) collective-permute-start(bf16[224,8192]{1,0:T(8,128)(2,1)} %bitcast.4), channel_id=1, source_target_pairs={{0,1},{1,0},{2,3},{3,2},{4,5},{5,4},{6,7},{7,6},{8,9},{9,8},{10,11... | collective-permute-start | bytes 11010056 | tf_op jit(solution)/shard_map/ppermute | solution.py:408
  1.4 0.0 collective-permute-start.3
  1.4 0.5 collective-permute-start.4
  1.9 0.0 collective-permute-start.5
  1.9 10.7 %collective-permute-start = (s32[2]{0:T(128)}, s32[2]{0:T(128)S(1)}, u32[]{:S(2)}, u32[]{:S(2)}) collective-permute-start(s32[2]{0:T(128)} %lengths_ref.3), channel_id=1, source_target_pairs={{1,85},{3,87},{5,89},{7,91},{9,93},{11,95},{13,65},{15,67},{17,69}... | collective-permute-start | bytes 32 | tf_op jit(solution)/shard_map/ppermute | solution.py:417
  12.7 0.8 collective-permute-done
  13.5 2.6 %collective-permute-start.1 = (s32[2]{0:T(128)S(1)}, s32[2]{0:T(128)S(1)}, u32[]{:S(2)}, u32[]{:S(2)}) collective-permute-start(s32[2]{0:T(128)S(1)} %collective-permute-done), channel_id=1, source_target_pairs={{1,3},{3,1},{5,7},{7,5},{9,11},{11,9},{13,15},{15,13},{17,19},{19,... | collective-permute-start | bytes 32 | tf_op jit(solution)/shard_map/ppermute | solution.py:417
  16.2 1.6 %collective-permute-done.1.token_hbm = s32[2]{0:T(128)S(1)} collective-permute-done((s32[2]{0:T(128)S(1)}, s32[2]{0:T(128)S(1)}, u32[]{:S(2)}, u32[]{:S(2)}) %collective-permute-start.1) | collective-permute-done | bytes 40 | tf_op jit(solution)/shard_map/ppermute | solution.py:417
  17.8 4.8 %shard_map.100 = bf16[16,16,1152]{2,1,0:T(8,128)(2,1)} custom-call(s32[2]{0:T(128)} %lengths_ref.3, bf16[2,8192]{1,0:T(2,128)(2,1)} %q_hbm.1, bf16[2,2048,256]{2,1,0:T(8,128)(2,1)} %k_hbm.1, bf16[2,2048,256]{2,1,0:T(8,128)(2,1)} %v_hbm.1, bf16[2,7168]{1,0:T(2,128)(2,1)} %hid_hbm.1, s32[2]{0:T(128)S(1)} %collective-permute-done.1.token_hbm), custom_call_target="tpu_custom_call" | custom-call | tf_op jit(solution)/shard_map/pallas_call | solution.py:86
  22.6 16.7 %all_to_all.15.x_ref = bf16[16,16,1152]{2,1,0:T(8,128)(2,1)S(1)} all-to-all(bf16[16,16,1152]{2,1,0:T(8,128)(2,1)} %shard_map.100), channel_id=1, replica_groups={{0,2,4,6,8,10,12,14,16,18,20,22,24,26,28,30},{1,3,5,7,9,11,13,15,17,19,..., dimensions={0} | all-to-all | bytes 1179648 | tf_op jit(solution)/shard_map/all_to_all | solution.py:419
  39.3 0.0 collective-permute-done.3.refs_0_.gx_ref
  39.3 0.0 collective-permute-done.4.refs_1_.ux_ref
  39.3 0.0 collective-permute-done.5.refs_2_.dx_ref
  39.3 0.0 collective-permute-done.2.oth
  39.3 0.0 copy-done
  39.3 0.0 copy-start.3
  39.3 0.0 copy-start.4
  39.3 4.7 %shard_map.101 = (bf16[64,112,128]{2,1,0:T(8,128)(2,1)}, f32[4,32,128]{2,1,0:T(8,128)}) custom-call(bf16[16,16,1152]{2,1,0:T(8,128)(2,1)S(1)} %all_to_all.15.x_ref, bf16[224,8192]{1,0:T(8,128)(2,1)S(1)} %bitcast.5, bf16[224,8192]{1,0:T(8,128)(2,1)S(1)} %collective-permute-done.2.oth, f32[56,128]{1,0:T(8,128)} %bitcast.6, ...), custom_call_target="tpu_custom_call" | custom-call | flops 234881024 | bytes 7340032 | tf_op jit(solution)/shard_map/pallas_call | solution.py:190
  44.0 0.0 copy-start.1
  44.1 0.0 copy-start.2
  44.1 24.2 %all_to_all.16 = bf16[64,112,128]{2,1,0:T(8,128)(2,1)S(1)} all-to-all(bf16[64,112,128]{2,1,0:T(8,128)(2,1)} %get-tuple-element.7), channel_id=1, replica_groups={{0,2,4,6,8,10,12,14,16,18,20,22,24,26,28,30,32,34,36,38,40,42,44,46,48,..., dimensions={0} | all-to-all | bytes 3670016 | tf_op jit(solution)/shard_map/all_to_all | solution.py:423
  68.2 0.0 copy-done.3
  68.2 0.0 copy-done.4
  68.3 0.0 copy-done.1
  68.3 0.0 copy-done.2
  68.3 4.8 %shard_map.102 = bf16[64,16,896]{2,1,0:T(8,128)(2,1)} custom-call(bf16[4,16,112,128]{3,2,1,0:T(8,128)(2,1)S(1)} %bitcast.3, bf16[7168,128]{1,0:T(8,128)(2,1)S(1)} %copy-done.1, bf16[7168,128]{1,0:T(8,128)(2,1)S(1)} %collective-permute-done.3.refs_0_.gx_ref, bf16[7168,128]{1,0:T(8,128)(2,1)S(1)} %copy-done.2, ...), custom_call_target="tpu_custom_call" | custom-call | flops 1409286144 | bytes 12845056 | tf_op jit(solution)/shard_map/pallas_call | solution.py:332
  73.1 22.8 %all_to_all.17.parts_ref = bf16[64,16,896]{2,1,0:T(8,128)(2,1)S(1)} all-to-all(bf16[64,16,896]{2,1,0:T(8,128)(2,1)} %shard_map.102), channel_id=1, replica_groups={{0,2,4,6,8,10,12,14,16,18,20,22,24,26,28,30,32,34,36,38,40,42,44,46,48,..., dimensions={0} | all-to-all | bytes 3670016 | tf_op jit(solution)/shard_map/all_to_all | solution.py:425
  95.9 1.5 %shard_map.103 = bf16[2,7168]{1,0:T(2,128)(2,1)} custom-call(s32[2]{0:T(128)} %lengths_ref.3, bf16[64,16,896]{2,1,0:T(8,128)(2,1)S(1)} %all_to_all.17.parts_ref), custom_call_target="tpu_custom_call" | custom-call | tf_op jit(solution)/shard_map/pallas_call | solution.py:372
Async XLA Ops:
  0.0 39.3 %copy-start = (bf16[8192,224]{0,1:T(8,128)(2,1)S(1)}, bf16[8192,224]{0,1:T(8,128)(2,1)}, u32[]{:S(2)}) copy-start(bf16[8192,224]{0,1:T(8,128)(2,1)} %param.15) | copy-start | bytes 11010052
  0.0 39.3 %collective-permute-start.2 = (bf16[224,8192]{1,0:T(8,128)(2,1)}, bf16[224,8192]{1,0:T(8,128)(2,1)S(1)}, u32[]{:S(2)}, u32[]{:S(2)}) collective-permute-start(bf16[224,8192]{1,0:T(8,128)(2,1)} %bitcast.4), channel_id=1, source_target_pairs={{0,1},{1,0},{2,3},{3,2},{4,5},{5,4},{6,7},{7,6},{8,9},{9,8},{10,11... | collective-permute-start | bytes 11010056 | tf_op jit(solution)/shard_map/ppermute | solution.py:408
  1.4 37.8 %collective-permute-start.3 = (bf16[7168,128]{1,0:T(8,128)(2,1)}, bf16[7168,128]{1,0:T(8,128)(2,1)S(1)}, u32[]{:S(2)}, u32[]{:S(2)}) collective-permute-start(bf16[7168,128]{1,0:T(8,128)(2,1)} %go_ref.1), channel_id=1, source_target_pairs={{0,1},{1,0},{2,3},{3,2},{4,5},{5,4},{6,7},{7,6},{8,9},{9,8},{10,11... | collective-permute-start | bytes 5505032 | tf_op jit(solution)/shard_map/ppermute | solution.py:408
  1.4 37.8 %collective-permute-start.4 = (bf16[7168,128]{1,0:T(8,128)(2,1)}, bf16[7168,128]{1,0:T(8,128)(2,1)S(1)}, u32[]{:S(2)}, u32[]{:S(2)}) collective-permute-start(bf16[7168,128]{1,0:T(8,128)(2,1)} %uo_ref.1), channel_id=1, source_target_pairs={{0,1},{1,0},{2,3},{3,2},{4,5},{5,4},{6,7},{7,6},{8,9},{9,8},{10,11... | collective-permute-start | bytes 5505032 | tf_op jit(solution)/shard_map/ppermute | solution.py:408
  1.9 37.3 %collective-permute-start.5 = (bf16[7168,128]{1,0:T(8,128)(2,1)}, bf16[7168,128]{1,0:T(8,128)(2,1)S(1)}, u32[]{:S(2)}, u32[]{:S(2)}) collective-permute-start(bf16[7168,128]{1,0:T(8,128)(2,1)} %do_ref.1), channel_id=1, source_target_pairs={{0,1},{1,0},{2,3},{3,2},{4,5},{5,4},{6,7},{7,6},{8,9},{9,8},{10,11... | collective-permute-start | bytes 5505032 | tf_op jit(solution)/shard_map/ppermute | solution.py:408
  1.9 11.6 %collective-permute-start = (s32[2]{0:T(128)}, s32[2]{0:T(128)S(1)}, u32[]{:S(2)}, u32[]{:S(2)}) collective-permute-start(s32[2]{0:T(128)} %lengths_ref.3), channel_id=1, source_target_pairs={{1,85},{3,87},{5,89},{7,91},{9,93},{11,95},{13,65},{15,67},{17,69}... | collective-permute-start | bytes 32 | tf_op jit(solution)/shard_map/ppermute | solution.py:417
  13.5 4.3 %collective-permute-start.1 = (s32[2]{0:T(128)S(1)}, s32[2]{0:T(128)S(1)}, u32[]{:S(2)}, u32[]{:S(2)}) collective-permute-start(s32[2]{0:T(128)S(1)} %collective-permute-done), channel_id=1, source_target_pairs={{1,3},{3,1},{5,7},{7,5},{9,11},{11,9},{13,15},{15,13},{17,19},{19,... | collective-permute-start | bytes 32 | tf_op jit(solution)/shard_map/ppermute | solution.py:417
  39.3 29.0 %copy-start.3 = (bf16[7168,128]{1,0:T(8,128)(2,1)S(1)}, bf16[7168,128]{1,0:T(8,128)(2,1)}, u32[]{:S(2)}) copy-start(bf16[7168,128]{1,0:T(8,128)(2,1)} %do_ref.1) | copy-start | bytes 5505028
  39.3 28.9 %copy-start.4 = (f32[7168]{0:T(1024)S(1)}, f32[7168]{0:T(1024)}, u32[]{:S(2)}) copy-start(f32[7168]{0:T(1024)} %param.16) | copy-start | bytes 86020
  44.0 24.2 %copy-start.1 = (bf16[7168,128]{1,0:T(8,128)(2,1)S(1)}, bf16[7168,128]{1,0:T(8,128)(2,1)}, u32[]{:S(2)}) copy-start(bf16[7168,128]{1,0:T(8,128)(2,1)} %go_ref.1) | copy-start | bytes 5505028
  44.1 24.2 %copy-start.2 = (bf16[7168,128]{1,0:T(8,128)(2,1)S(1)}, bf16[7168,128]{1,0:T(8,128)(2,1)}, u32[]{:S(2)}) copy-start(bf16[7168,128]{1,0:T(8,128)(2,1)} %uo_ref.1) | copy-start | bytes 5505028

commit v8 on v7

--- a/solution.py
+++ b/solution.py
@@ -87,7 +87,7 @@
         attend_kernel,
         in_specs=[pl.BlockSpec(memory_space=pltpu.SMEM)] + [hbm] * 5,
         out_specs=vmem,
-        out_shape=pltpu.HBM((chips, 16, lanes), BF16),
+        out_shape=jax.ShapeDtypeStruct((chips, 16, lanes), BF16),
         scratch_shapes=[
             pltpu.VMEM(query.shape, BF16),
             pltpu.VMEM(hidden.shape, BF16),
@@ -101,7 +101,7 @@
 
 
 def project_kernel(cols, x_ref, own, oth, gain_hbm, *refs):
-    out_hbm, res_hbm, gain_ref, res_ref, block, gain_sem, res_sem, out_sem = refs[-8:]
+    out_ref, res_ref, gain_ref, gain_sem = refs[-4:]
     gain_copy = pltpu.make_async_copy(gain_hbm, gain_ref, gain_sem)
     gain_copy.start()
     chips, deep, lanes = x_ref.shape
@@ -165,17 +165,8 @@
     odd = jnp.where(low, rest[half:], turned[:half])
     last = jnp.where(chip % 2 == 0, even, odd)
     packed = jnp.concatenate([sent[0][:, :128], sent[1][:, :128], third, last], axis=0).astype(BF16)
-    many = block.shape[0]
-    for p in range(many):
-        block[p] = packed
-    outs = [pltpu.make_async_copy(res_ref, res_hbm, res_sem)]
-    outs[0].start()
-    for p in range(out_hbm.shape[0] // many):
-        out = pltpu.make_async_copy(block, out_hbm.at[pl.ds(p * many, many)], out_sem.at[p])
-        out.start()
-        outs.append(out)
-    for out in outs:
-        out.wait()
+    for p in range(out_ref.shape[0]):
+        out_ref[p] = packed
 
 
 def in_hbm(v):
@@ -190,15 +181,14 @@
     return pl.pallas_call(
         functools.partial(project_kernel, cols),
         in_specs=[pl.BlockSpec(memory_space=pltpu.VMEM)] * 3 + [hbm] * (1 + len(arrived)),
-        out_specs=[hbm, hbm],
-        out_shape=[pltpu.HBM((peers, packed, 128), BF16), pltpu.HBM((4, rows, 128), F32)],
+        out_specs=[pl.BlockSpec(memory_space=pltpu.VMEM)] * 2,
+        out_shape=[
+            jax.ShapeDtypeStruct((peers, packed, 128), BF16),
+            jax.ShapeDtypeStruct((4, rows, 128), F32),
+        ],
         scratch_shapes=[
             pltpu.VMEM(gain.shape, F32),
-            pltpu.VMEM((4, rows, 128), F32),
-            pltpu.VMEM((8, packed, 128), BF16),
             pltpu.SemaphoreType.DMA,
-            pltpu.SemaphoreType.DMA,
-            pltpu.SemaphoreType.DMA((peers // 8,)),
         ],
         compiler_params=pltpu.CompilerParams(vmem_limit_bytes=24 * 2**20),
         cost_estimate=pl.CostEstimate(
@@ -209,8 +199,7 @@
 
 def ffn_kernel(
     chips, cols, width,
-    x_buf, go_ref, gx_ref, uo_ref, ux_ref, do_ref, dx_ref, gain_ref, res_hbm, out_hbm,
-    held, out_buf, res_ref, res_sem, out_sem,
+    x_buf, go_ref, gx_ref, uo_ref, ux_ref, do_ref, dx_ref, gain_ref, res_ref, out_ref, held,
 ):
     groups, _, packed, _ = x_buf.shape
     rows = packed * 128 // (2 * cols)
@@ -220,8 +209,6 @@
     parts = chips // quarter
     me = lax.axis_index("dev")
     core, chip = me % 2, me // 2
-    res_copy = pltpu.make_async_copy(res_hbm, res_ref, res_sem)
-    res_copy.start()
     spans, span = 8, width // 8
     per = span // 128
     sums = jnp.zeros((total, 4 * units), F32)
@@ -279,7 +266,6 @@
             res = tile.astype(F32) * inv
             squares += res * res
 
-    res_copy.wait()
     scale = lax.rsqrt(jnp.sum(squares, axis=1, keepdims=True) / width + EPS)
     gate = sums[:, : 2 * units] * scale
     up = sums[:, 2 * units :] * scale
@@ -301,7 +287,6 @@
     c = lax.broadcasted_iota(jnp.int32, (128, 128), 1)
     peer, piece, slot = r // 16, (r // 2) % spans, r % 2
     order = jnp.where(c == piece * 16 + peer * 2 + slot, 1.0, 0.0).astype(BF16)
-    outs = []
     for g in range(total // 16):
         stack = jnp.concatenate(
             [
@@ -311,12 +296,7 @@
             axis=0,
         )
         moved = jnp.dot(order, stack, preferred_element_type=F32).astype(BF16)
-        some = pl.ds(g * 8, 8)
-        out_buf[g * 8 : (g + 1) * 8] = moved.reshape(8, 16, span)
-        outs.append(pltpu.make_async_copy(out_buf.at[some], out_hbm.at[some], out_sem.at[g]))
-        outs[-1].start()
-    for out in outs:
-        out.wait()
+        out_ref[g * 8 : (g + 1) * 8] = moved.reshape(8, 16, span)
 
 
 def feed_forward(blocks, gate, up, down, gain, residual, chips):
@@ -331,15 +311,11 @@
     vmem = pl.BlockSpec(memory_space=pltpu.VMEM)
     return pl.pallas_call(
         functools.partial(ffn_kernel, chips, cols, width),
-        in_specs=[vmem] * 8 + [pl.BlockSpec(memory_space=pl.ANY)],
-        out_specs=pl.BlockSpec(memory_space=pl.ANY),
-        out_shape=pltpu.HBM((peers, 16, span), BF16),
+        in_specs=[vmem] * 9,
+        out_specs=vmem,
+        out_shape=jax.ShapeDtypeStruct((peers, 16, span), BF16),
         scratch_shapes=[
             pltpu.VMEM((width // 128, total, 128), BF16),
-            pltpu.VMEM((peers, 16, span), BF16),
-            pltpu.VMEM(residual.shape, F32),
-            pltpu.SemaphoreType.DMA,
-            pltpu.SemaphoreType.DMA((total // 16,)),
         ],
         compiler_params=pltpu.CompilerParams(vmem_limit_bytes=28 * 2**20),
         cost_estimate=pl.CostEstimate(
@@ -351,7 +327,7 @@
         *up,
         *down,
         gain,
-        in_hbm(residual),
+        residual,
     )
 
 

time: 98 us -> 92.9 us (0.948)
  Pallas kernels: 15.8 us -> 12.3 us
  blocking collectives: 63.7 us -> 62.4 us
    pallas_call x1, Pallas kernels: 4.81 us -> 3.46 us  [feed_forward(): pl.pallas_call(functools.partial(ffn_kernel, chips, cols, width), in_spec...]
    pallas_call x1, Pallas kernels: 4.72 us -> 3.39 us  [project(): pl.pallas_call(functools.partial(project_kernel, cols), in_specs=[pl.Bloc...]
  transfers between devices with their start and end apart: 6 -> 6, of which waited for: 2 -> 2; matrix products, arithmetic and copies ran while one was open for 0% -> 0% of each run, Pallas kernels for 5% -> 4%
where the time goes in v8:
time: 92.9 us; the launch traced here: 92.6 us
  blocking collectives  62.4 us (67%)
  starting transfers between devices  15.3 us (16%)
  Pallas kernels  12.3 us (13%)
  waiting for transfers between devices  2.47 us (3%)
    all_to_all x1, blocking collectives, shards(): blocks = lax.all_to_all(block, both, 0, 0, axis_index_groups=cube)  24 us
    all_to_all x1, blocking collectives, shards(): parts = lax.all_to_all(partial, both, 0, 0, axis_index_groups=cube)  21.9 us
    all_to_all x1, blocking collectives, shards(): got = lax.all_to_all(message, 'dev', 0, 0, axis_index_groups=plane)  16.5 us
    ppermute x2, starting transfers between devices, shards(): token = lax.ppermute(token, both, link)  13.4 us
    pallas_call x1, Pallas kernels, attend(): pl.pallas_call(attend_kernel, in_specs=[pl.BlockSpec(memory_space=pltpu.S...  3.96 us
    pallas_call x1, Pallas kernels, feed_forward(): pl.pallas_call(functools.partial(ffn_kernel, chips, cols, width), in_spec...  3.46 us
    pallas_call x1, Pallas kernels, project(): pl.pallas_call(functools.partial(project_kernel, cols), in_specs=[pl.Bloc...  3.39 us
    ppermute x2, waiting for transfers between devices, shards(): token = lax.ppermute(token, both, link)  2.46 us
  transfers between devices with their start and end apart: 6, of which 2 were waited for; matrix products, arithmetic and copies ran while one was open for 0% of the time, Pallas kernels for 4%

profile of v8, /device:TPU:1, one launch (start us, length us, event | category | flops | bytes accessed | tf_op | source)
XLA Modules:
  0.0 92.6 jit_solution(6856052706006146914)
XLA Ops:
  0.0 0.0 copy-start
  0.0 1.4 %collective-permute-start.2 = (bf16[224,8192]{1,0:T(8,128)(2,1)}, bf16[224,8192]{1,0:T(8,128)(2,1)S(1)}, u32[]{:S(2)}, u32[]{:S(2)}) collective-permute-start(bf16[224,8192]{1,0:T(8,128)(2,1)} %bitcast.4), channel_id=1, source_target_pairs={{0,1},{1,0},{2,3},{3,2},{4,5},{5,4},{6,7},{7,6},{8,9},{9,8},{10,11... | collective-permute-start | bytes 11010056 | tf_op jit(solution)/shard_map/ppermute | solution.py:384
  1.4 0.0 collective-permute-start.3
  1.4 0.5 collective-permute-start.4
  1.9 0.0 collective-permute-start.5
  1.9 10.7 %collective-permute-start = (s32[2]{0:T(128)}, s32[2]{0:T(128)S(1)}, u32[]{:S(2)}, u32[]{:S(2)}) collective-permute-start(s32[2]{0:T(128)} %lengths_ref.3), channel_id=1, source_target_pairs={{1,85},{3,87},{5,89},{7,91},{9,93},{11,95},{13,65},{15,67},{17,69}... | collective-permute-start | bytes 32 | tf_op jit(solution)/shard_map/ppermute | solution.py:393
  12.7 0.8 collective-permute-done
  13.5 2.6 %collective-permute-start.1 = (s32[2]{0:T(128)S(1)}, s32[2]{0:T(128)S(1)}, u32[]{:S(2)}, u32[]{:S(2)}) collective-permute-start(s32[2]{0:T(128)S(1)} %collective-permute-done), channel_id=1, source_target_pairs={{1,3},{3,1},{5,7},{7,5},{9,11},{11,9},{13,15},{15,13},{17,19},{19,... | collective-permute-start | bytes 32 | tf_op jit(solution)/shard_map/ppermute | solution.py:393
  16.2 1.6 %collective-permute-done.1.token_hbm = s32[2]{0:T(128)S(1)} collective-permute-done((s32[2]{0:T(128)S(1)}, s32[2]{0:T(128)S(1)}, u32[]{:S(2)}, u32[]{:S(2)}) %collective-permute-start.1) | collective-permute-done | bytes 40 | tf_op jit(solution)/shard_map/ppermute | solution.py:393
  17.8 4.0 %shard_map.100 = bf16[16,16,1152]{2,1,0:T(8,128)(2,1)S(1)} custom-call(s32[2]{0:T(128)} %lengths_ref.3, bf16[2,8192]{1,0:T(2,128)(2,1)} %q_hbm.1, bf16[2,2048,256]{2,1,0:T(8,128)(2,1)} %k_hbm.1, bf16[2,2048,256]{2,1,0:T(8,128)(2,1)} %v_hbm.1, bf16[2,7168]{1,0:T(2,128)(2,1)} %hid_hbm.1, s32[2]{0:T(128)S(1)} %collective-permute-done.1.token_hbm), custom_call_target="tpu_custom_call" | custom-call | tf_op jit(solution)/shard_map/pallas_call | solution.py:86
  21.8 16.5 %all_to_all.15.x_ref = bf16[16,16,1152]{2,1,0:T(8,128)(2,1)S(1)} all-to-all(bf16[16,16,1152]{2,1,0:T(8,128)(2,1)S(1)} %shard_map.100), channel_id=1, replica_groups={{0,2,4,6,8,10,12,14,16,18,20,22,24,26,28,30},{1,3,5,7,9,11,13,15,17,19,..., dimensions={0} | all-to-all | bytes 1179648 | tf_op jit(solution)/shard_map/all_to_all | solution.py:395
  38.3 0.0 collective-permute-done.3.refs_0_.gx_ref
  38.3 0.0 collective-permute-done.4.refs_1_.ux_ref
  38.3 0.0 collective-permute-done.5.refs_2_.dx_ref
  38.3 0.0 collective-permute-done.2.oth
  38.3 0.0 copy-done
  38.3 0.0 copy-start.3
  38.3 0.0 copy-start.4
  38.3 3.4 %shard_map.101 = (bf16[64,112,128]{2,1,0:T(8,128)(2,1)S(1)}, f32[4,32,128]{2,1,0:T(8,128)S(1)}) custom-call(bf16[16,16,1152]{2,1,0:T(8,128)(2,1)S(1)} %all_to_all.15.x_ref, bf16[224,8192]{1,0:T(8,128)(2,1)S(1)} %bitcast.5, bf16[224,8192]{1,0:T(8,128)(2,1)S(1)} %collective-permute-done.2.oth, f32[56,128]{1,0:T(8,128)} %bitcast.6, ...), custom_call_target="tpu_custom_call" | custom-call | flops 234881024 | bytes 7340032 | tf_op jit(solution)/shard_map/pallas_call | solution.py:181
  41.7 0.0 copy-start.1
  41.7 0.0 copy-start.2
  41.7 24.0 %all_to_all.16 = bf16[64,112,128]{2,1,0:T(8,128)(2,1)S(1)} all-to-all(bf16[64,112,128]{2,1,0:T(8,128)(2,1)S(1)} %get-tuple-element.7), channel_id=1, replica_groups={{0,2,4,6,8,10,12,14,16,18,20,22,24,26,28,30,32,34,36,38,40,42,44,46,48,..., dimensions={0} | all-to-all | bytes 3670016 | tf_op jit(solution)/shard_map/all_to_all | solution.py:399
  65.7 0.0 copy-done.3
  65.7 0.0 copy-done.4
  65.7 0.0 copy-done.1
  65.7 0.0 copy-done.2
  65.7 3.5 %shard_map.102 = bf16[64,16,896]{2,1,0:T(8,128)(2,1)S(1)} custom-call(bf16[4,16,112,128]{3,2,1,0:T(8,128)(2,1)S(1)} %bitcast.3, bf16[7168,128]{1,0:T(8,128)(2,1)S(1)} %copy-done.1, bf16[7168,128]{1,0:T(8,128)(2,1)S(1)} %collective-permute-done.3.refs_0_.gx_ref, bf16[7168,128]{1,0:T(8,128)(2,1)S(1)} %copy-done.2, ...), custom_call_target="tpu_custom_call" | custom-call | flops 1409286144 | bytes 12845056 | tf_op jit(solution)/shard_map/pallas_call | solution.py:312
  69.2 21.9 %all_to_all.17.parts_ref = bf16[64,16,896]{2,1,0:T(8,128)(2,1)S(1)} all-to-all(bf16[64,16,896]{2,1,0:T(8,128)(2,1)S(1)} %shard_map.102), channel_id=1, replica_groups={{0,2,4,6,8,10,12,14,16,18,20,22,24,26,28,30,32,34,36,38,40,42,44,46,48,..., dimensions={0} | all-to-all | bytes 3670016 | tf_op jit(solution)/shard_map/all_to_all | solution.py:401
  91.1 1.5 %shard_map.103 = bf16[2,7168]{1,0:T(2,128)(2,1)} custom-call(s32[2]{0:T(128)} %lengths_ref.3, bf16[64,16,896]{2,1,0:T(8,128)(2,1)S(1)} %all_to_all.17.parts_ref), custom_call_target="tpu_custom_call" | custom-call | tf_op jit(solution)/shard_map/pallas_call | solution.py:348
Async XLA Ops:
  0.0 38.3 %copy-start = (bf16[8192,224]{0,1:T(8,128)(2,1)S(1)}, bf16[8192,224]{0,1:T(8,128)(2,1)}, u32[]{:S(2)}) copy-start(bf16[8192,224]{0,1:T(8,128)(2,1)} %param.15) | copy-start | bytes 11010052
  0.0 38.3 %collective-permute-start.2 = (bf16[224,8192]{1,0:T(8,128)(2,1)}, bf16[224,8192]{1,0:T(8,128)(2,1)S(1)}, u32[]{:S(2)}, u32[]{:S(2)}) collective-permute-start(bf16[224,8192]{1,0:T(8,128)(2,1)} %bitcast.4), channel_id=1, source_target_pairs={{0,1},{1,0},{2,3},{3,2},{4,5},{5,4},{6,7},{7,6},{8,9},{9,8},{10,11... | collective-permute-start | bytes 11010056 | tf_op jit(solution)/shard_map/ppermute | solution.py:384
  1.4 36.8 %collective-permute-start.3 = (bf16[7168,128]{1,0:T(8,128)(2,1)}, bf16[7168,128]{1,0:T(8,128)(2,1)S(1)}, u32[]{:S(2)}, u32[]{:S(2)}) collective-permute-start(bf16[7168,128]{1,0:T(8,128)(2,1)} %go_ref.1), channel_id=1, source_target_pairs={{0,1},{1,0},{2,3},{3,2},{4,5},{5,4},{6,7},{7,6},{8,9},{9,8},{10,11... | collective-permute-start | bytes 5505032 | tf_op jit(solution)/shard_map/ppermute | solution.py:384
  1.4 36.8 %collective-permute-start.4 = (bf16[7168,128]{1,0:T(8,128)(2,1)}, bf16[7168,128]{1,0:T(8,128)(2,1)S(1)}, u32[]{:S(2)}, u32[]{:S(2)}) collective-permute-start(bf16[7168,128]{1,0:T(8,128)(2,1)} %uo_ref.1), channel_id=1, source_target_pairs={{0,1},{1,0},{2,3},{3,2},{4,5},{5,4},{6,7},{7,6},{8,9},{9,8},{10,11... | collective-permute-start | bytes 5505032 | tf_op jit(solution)/shard_map/ppermute | solution.py:384
  1.9 36.3 %collective-permute-start.5 = (bf16[7168,128]{1,0:T(8,128)(2,1)}, bf16[7168,128]{1,0:T(8,128)(2,1)S(1)}, u32[]{:S(2)}, u32[]{:S(2)}) collective-permute-start(bf16[7168,128]{1,0:T(8,128)(2,1)} %do_ref.1), channel_id=1, source_target_pairs={{0,1},{1,0},{2,3},{3,2},{4,5},{5,4},{6,7},{7,6},{8,9},{9,8},{10,11... | collective-permute-start | bytes 5505032 | tf_op jit(solution)/shard_map/ppermute | solution.py:384
  1.9 11.6 %collective-permute-start = (s32[2]{0:T(128)}, s32[2]{0:T(128)S(1)}, u32[]{:S(2)}, u32[]{:S(2)}) collective-permute-start(s32[2]{0:T(128)} %lengths_ref.3), channel_id=1, source_target_pairs={{1,85},{3,87},{5,89},{7,91},{9,93},{11,95},{13,65},{15,67},{17,69}... | collective-permute-start | bytes 32 | tf_op jit(solution)/shard_map/ppermute | solution.py:393
  13.5 4.3 %collective-permute-start.1 = (s32[2]{0:T(128)S(1)}, s32[2]{0:T(128)S(1)}, u32[]{:S(2)}, u32[]{:S(2)}) collective-permute-start(s32[2]{0:T(128)S(1)} %collective-permute-done), channel_id=1, source_target_pairs={{1,3},{3,1},{5,7},{7,5},{9,11},{11,9},{13,15},{15,13},{17,19},{19,... | collective-permute-start | bytes 32 | tf_op jit(solution)/shard_map/ppermute | solution.py:393
  38.3 27.4 %copy-start.3 = (bf16[7168,128]{1,0:T(8,128)(2,1)S(1)}, bf16[7168,128]{1,0:T(8,128)(2,1)}, u32[]{:S(2)}) copy-start(bf16[7168,128]{1,0:T(8,128)(2,1)} %do_ref.1) | copy-start | bytes 5505028
  38.3 27.4 %copy-start.4 = (f32[7168]{0:T(1024)S(1)}, f32[7168]{0:T(1024)}, u32[]{:S(2)}) copy-start(f32[7168]{0:T(1024)} %param.16) | copy-start | bytes 86020
  41.7 24.0 %copy-start.1 = (bf16[7168,128]{1,0:T(8,128)(2,1)S(1)}, bf16[7168,128]{1,0:T(8,128)(2,1)}, u32[]{:S(2)}) copy-start(bf16[7168,128]{1,0:T(8,128)(2,1)} %go_ref.1) | copy-start | bytes 5505028
  41.7 24.0 %copy-start.2 = (bf16[7168,128]{1,0:T(8,128)(2,1)S(1)}, bf16[7168,128]{1,0:T(8,128)(2,1)}, u32[]{:S(2)}) copy-start(bf16[7168,128]{1,0:T(8,128)(2,1)} %uo_ref.1) | copy-start | bytes 5505028

commit v9 on v8

--- a/solution.py
+++ b/solution.py
@@ -100,10 +100,8 @@
     )(in_hbm(lengths), *[in_hbm(v) for v in (query, key_cache, value_cache, hidden)], token)
 
 
-def project_kernel(cols, x_ref, own, oth, gain_hbm, *refs):
-    out_ref, res_ref, gain_ref, gain_sem = refs[-4:]
-    gain_copy = pltpu.make_async_copy(gain_hbm, gain_ref, gain_sem)
-    gain_copy.start()
+def project_kernel(cols, x_ref, own, oth, gain_ref, *refs):
+    out_ref, res_ref = refs[-2:]
     chips, deep, lanes = x_ref.shape
     slots = 2
     pieces = deep // slots
@@ -133,7 +131,6 @@
 
     hids = halves(hid_rows)
     start = 7 * (chip // 2) + 3 * (chip % 2)
-    gain_copy.wait()
     gains = halves([jnp.broadcast_to(gain_ref[pl.ds(start + i, 1), :], (rows, 128)) for i in range(4)])
     pad = jnp.zeros((rows, 256 - cols), F32)
     held, sent = [], []
@@ -180,21 +177,17 @@
     hbm = pl.BlockSpec(memory_space=pl.ANY)
     return pl.pallas_call(
         functools.partial(project_kernel, cols),
-        in_specs=[pl.BlockSpec(memory_space=pltpu.VMEM)] * 3 + [hbm] * (1 + len(arrived)),
+        in_specs=[pl.BlockSpec(memory_space=pltpu.VMEM)] * 4 + [hbm] * len(arrived),
         out_specs=[pl.BlockSpec(memory_space=pltpu.VMEM)] * 2,
         out_shape=[
             jax.ShapeDtypeStruct((peers, packed, 128), BF16),
             jax.ShapeDtypeStruct((4, rows, 128), F32),
         ],
-        scratch_shapes=[
-            pltpu.VMEM(gain.shape, F32),
-            pltpu.SemaphoreType.DMA,
-        ],
         compiler_params=pltpu.CompilerParams(vmem_limit_bytes=24 * 2**20),
         cost_estimate=pl.CostEstimate(
             flops=4 * rows * cols * depth, bytes_accessed=4 * cols * depth, transcendentals=0
         ),
-    )(messages, out_own, out_oth, in_hbm(gain), *arrived)
+    )(messages, out_own, out_oth, gain, *arrived)
 
 
 def ffn_kernel(

time: 92.9 us -> 92.2 us (level)
  no operation moved by 1% of the time
where the time goes in v9:
time: 92.2 us; the launch traced here: 92 us
  blocking collectives  62.5 us (68%)
  starting transfers between devices  15.3 us (17%)
  Pallas kernels  11.6 us (13%)
  waiting for transfers between devices  2.47 us (3%)
    all_to_all x1, blocking collectives, shards(): blocks = lax.all_to_all(block, both, 0, 0, axis_index_groups=cube)  24 us
    all_to_all x1, blocking collectives, shards(): parts = lax.all_to_all(partial, both, 0, 0, axis_index_groups=cube)  22 us
    all_to_all x1, blocking collectives, shards(): got = lax.all_to_all(message, 'dev', 0, 0, axis_index_groups=plane)  16.5 us
    ppermute x2, starting transfers between devices, shards(): token = lax.ppermute(token, both, link)  13.4 us
    pallas_call x1, Pallas kernels, attend(): pl.pallas_call(attend_kernel, in_specs=[pl.BlockSpec(memory_space=pltpu.S...  3.95 us
    pallas_call x1, Pallas kernels, feed_forward(): pl.pallas_call(functools.partial(ffn_kernel, chips, cols, width), in_spec...  3.45 us
    pallas_call x1, Pallas kernels, project(): pl.pallas_call(functools.partial(project_kernel, cols), in_specs=[pl.Bloc...  2.64 us
    ppermute x2, waiting for transfers between devices, shards(): token = lax.ppermute(token, both, link)  2.46 us
  transfers between devices with their start and end apart: 6, of which 2 were waited for; matrix products, arithmetic and copies ran while one was open for 0% of the time, Pallas kernels for 4%

profile of v9, /device:TPU:1, one launch (start us, length us, event | category | flops | bytes accessed | tf_op | source)
XLA Modules:
  0.0 92.0 jit_solution(15257541846608430959)
XLA Ops:
  0.0 0.0 copy-start
  0.0 0.0 copy-start.4
  0.0 1.4 %collective-permute-start.2 = (bf16[224,8192]{1,0:T(8,128)(2,1)}, bf16[224,8192]{1,0:T(8,128)(2,1)S(1)}, u32[]{:S(2)}, u32[]{:S(2)}) collective-permute-start(bf16[224,8192]{1,0:T(8,128)(2,1)} %bitcast.4), channel_id=1, source_target_pairs={{0,1},{1,0},{2,3},{3,2},{4,5},{5,4},{6,7},{7,6},{8,9},{9,8},{10,11... | collective-permute-start | bytes 11010056 | tf_op jit(solution)/shard_map/ppermute | solution.py:377
  1.4 0.0 collective-permute-start.3
  1.4 0.5 collective-permute-start.4
  1.9 0.0 collective-permute-start.5
  1.9 10.8 %collective-permute-start = (s32[2]{0:T(128)}, s32[2]{0:T(128)S(1)}, u32[]{:S(2)}, u32[]{:S(2)}) collective-permute-start(s32[2]{0:T(128)} %lengths_ref.3), channel_id=1, source_target_pairs={{1,85},{3,87},{5,89},{7,91},{9,93},{11,95},{13,65},{15,67},{17,69}... | collective-permute-start | bytes 32 | tf_op jit(solution)/shard_map/ppermute | solution.py:386
  12.7 0.8 collective-permute-done
  13.5 2.6 %collective-permute-start.1 = (s32[2]{0:T(128)S(1)}, s32[2]{0:T(128)S(1)}, u32[]{:S(2)}, u32[]{:S(2)}) collective-permute-start(s32[2]{0:T(128)S(1)} %collective-permute-done), channel_id=1, source_target_pairs={{1,3},{3,1},{5,7},{7,5},{9,11},{11,9},{13,15},{15,13},{17,19},{19,... | collective-permute-start | bytes 32 | tf_op jit(solution)/shard_map/ppermute | solution.py:386
  16.2 1.6 %collective-permute-done.1.token_hbm = s32[2]{0:T(128)S(1)} collective-permute-done((s32[2]{0:T(128)S(1)}, s32[2]{0:T(128)S(1)}, u32[]{:S(2)}, u32[]{:S(2)}) %collective-permute-start.1) | collective-permute-done | bytes 40 | tf_op jit(solution)/shard_map/ppermute | solution.py:386
  17.8 4.0 %shard_map.100 = bf16[16,16,1152]{2,1,0:T(8,128)(2,1)S(1)} custom-call(s32[2]{0:T(128)} %lengths_ref.3, bf16[2,8192]{1,0:T(2,128)(2,1)} %q_hbm.1, bf16[2,2048,256]{2,1,0:T(8,128)(2,1)} %k_hbm.1, bf16[2,2048,256]{2,1,0:T(8,128)(2,1)} %v_hbm.1, bf16[2,7168]{1,0:T(2,128)(2,1)} %hid_hbm.1, s32[2]{0:T(128)S(1)} %collective-permute-done.1.token_hbm), custom_call_target="tpu_custom_call" | custom-call | tf_op jit(solution)/shard_map/pallas_call | solution.py:86
  21.8 16.5 %all_to_all.15.x_ref = bf16[16,16,1152]{2,1,0:T(8,128)(2,1)S(1)} all-to-all(bf16[16,16,1152]{2,1,0:T(8,128)(2,1)S(1)} %shard_map.100), channel_id=1, replica_groups={{0,2,4,6,8,10,12,14,16,18,20,22,24,26,28,30},{1,3,5,7,9,11,13,15,17,19,..., dimensions={0} | all-to-all | bytes 1179648 | tf_op jit(solution)/shard_map/all_to_all | solution.py:388
  38.3 0.0 collective-permute-done.3.refs_0_.gx_ref
  38.3 0.0 collective-permute-done.4.refs_1_.ux_ref
  38.3 0.0 collective-permute-done.5.refs_2_.dx_ref
  38.3 0.0 collective-permute-done.2.oth
  38.3 0.0 copy-done
  38.3 0.0 copy-done.4
  38.3 0.0 copy-start.3
  38.4 2.6 %shard_map.101 = (bf16[64,112,128]{2,1,0:T(8,128)(2,1)S(1)}, f32[4,32,128]{2,1,0:T(8,128)S(1)}) custom-call(bf16[16,16,1152]{2,1,0:T(8,128)(2,1)S(1)} %all_to_all.15.x_ref, bf16[224,8192]{1,0:T(8,128)(2,1)S(1)} %bitcast.5, bf16[224,8192]{1,0:T(8,128)(2,1)S(1)} %collective-permute-done.2.oth, f32[56,128]{1,0:T(8,128)S(1)} %bitcast.6, ...), custom_call_target="tpu_custom_call" | custom-call | flops 234881024 | bytes 7340032 | tf_op jit(solution)/shard_map/pallas_call | solution.py:178
  41.0 0.0 copy-start.1
  41.0 0.0 copy-start.2
  41.0 24.0 %all_to_all.16 = bf16[64,112,128]{2,1,0:T(8,128)(2,1)S(1)} all-to-all(bf16[64,112,128]{2,1,0:T(8,128)(2,1)S(1)} %get-tuple-element.7), channel_id=1, replica_groups={{0,2,4,6,8,10,12,14,16,18,20,22,24,26,28,30,32,34,36,38,40,42,44,46,48,..., dimensions={0} | all-to-all | bytes 3670016 | tf_op jit(solution)/shard_map/all_to_all | solution.py:392
  65.0 0.0 copy-done.3
  65.0 0.0 copy-done.1
  65.0 0.0 copy-done.2
  65.0 3.5 %shard_map.102 = bf16[64,16,896]{2,1,0:T(8,128)(2,1)S(1)} custom-call(bf16[4,16,112,128]{3,2,1,0:T(8,128)(2,1)S(1)} %bitcast.3, bf16[7168,128]{1,0:T(8,128)(2,1)S(1)} %copy-done.1, bf16[7168,128]{1,0:T(8,128)(2,1)S(1)} %collective-permute-done.3.refs_0_.gx_ref, bf16[7168,128]{1,0:T(8,128)(2,1)S(1)} %copy-done.2, ...), custom_call_target="tpu_custom_call" | custom-call | flops 1409286144 | bytes 12845056 | tf_op jit(solution)/shard_map/pallas_call | solution.py:305
  68.5 22.0 %all_to_all.17.parts_ref = bf16[64,16,896]{2,1,0:T(8,128)(2,1)S(1)} all-to-all(bf16[64,16,896]{2,1,0:T(8,128)(2,1)S(1)} %shard_map.102), channel_id=1, replica_groups={{0,2,4,6,8,10,12,14,16,18,20,22,24,26,28,30,32,34,36,38,40,42,44,46,48,..., dimensions={0} | all-to-all | bytes 3670016 | tf_op jit(solution)/shard_map/all_to_all | solution.py:394
  90.5 1.5 %shard_map.103 = bf16[2,7168]{1,0:T(2,128)(2,1)} custom-call(s32[2]{0:T(128)} %lengths_ref.3, bf16[64,16,896]{2,1,0:T(8,128)(2,1)S(1)} %all_to_all.17.parts_ref), custom_call_target="tpu_custom_call" | custom-call | tf_op jit(solution)/shard_map/pallas_call | solution.py:341
Async XLA Ops:
  0.0 38.3 %copy-start = (bf16[8192,224]{0,1:T(8,128)(2,1)S(1)}, bf16[8192,224]{0,1:T(8,128)(2,1)}, u32[]{:S(2)}) copy-start(bf16[8192,224]{0,1:T(8,128)(2,1)} %param.15) | copy-start | bytes 11010052
  0.0 38.3 %copy-start.4 = (f32[7168]{0:T(1024)S(1)}, f32[7168]{0:T(1024)}, u32[]{:S(2)}) copy-start(f32[7168]{0:T(1024)} %param.16) | copy-start | bytes 86020
  0.0 38.3 %collective-permute-start.2 = (bf16[224,8192]{1,0:T(8,128)(2,1)}, bf16[224,8192]{1,0:T(8,128)(2,1)S(1)}, u32[]{:S(2)}, u32[]{:S(2)}) collective-permute-start(bf16[224,8192]{1,0:T(8,128)(2,1)} %bitcast.4), channel_id=1, source_target_pairs={{0,1},{1,0},{2,3},{3,2},{4,5},{5,4},{6,7},{7,6},{8,9},{9,8},{10,11... | collective-permute-start | bytes 11010056 | tf_op jit(solution)/shard_map/ppermute | solution.py:377
  1.4 36.9 %collective-permute-start.3 = (bf16[7168,128]{1,0:T(8,128)(2,1)}, bf16[7168,128]{1,0:T(8,128)(2,1)S(1)}, u32[]{:S(2)}, u32[]{:S(2)}) collective-permute-start(bf16[7168,128]{1,0:T(8,128)(2,1)} %go_ref.1), channel_id=1, source_target_pairs={{0,1},{1,0},{2,3},{3,2},{4,5},{5,4},{6,7},{7,6},{8,9},{9,8},{10,11... | collective-permute-start | bytes 5505032 | tf_op jit(solution)/shard_map/ppermute | solution.py:377
  1.4 36.9 %collective-permute-start.4 = (bf16[7168,128]{1,0:T(8,128)(2,1)}, bf16[7168,128]{1,0:T(8,128)(2,1)S(1)}, u32[]{:S(2)}, u32[]{:S(2)}) collective-permute-start(bf16[7168,128]{1,0:T(8,128)(2,1)} %uo_ref.1), channel_id=1, source_target_pairs={{0,1},{1,0},{2,3},{3,2},{4,5},{5,4},{6,7},{7,6},{8,9},{9,8},{10,11... | collective-permute-start | bytes 5505032 | tf_op jit(solution)/shard_map/ppermute | solution.py:377
  1.9 36.4 %collective-permute-start.5 = (bf16[7168,128]{1,0:T(8,128)(2,1)}, bf16[7168,128]{1,0:T(8,128)(2,1)S(1)}, u32[]{:S(2)}, u32[]{:S(2)}) collective-permute-start(bf16[7168,128]{1,0:T(8,128)(2,1)} %do_ref.1), channel_id=1, source_target_pairs={{0,1},{1,0},{2,3},{3,2},{4,5},{5,4},{6,7},{7,6},{8,9},{9,8},{10,11... | collective-permute-start | bytes 5505032 | tf_op jit(solution)/shard_map/ppermute | solution.py:377
  1.9 11.6 %collective-permute-start = (s32[2]{0:T(128)}, s32[2]{0:T(128)S(1)}, u32[]{:S(2)}, u32[]{:S(2)}) collective-permute-start(s32[2]{0:T(128)} %lengths_ref.3), channel_id=1, source_target_pairs={{1,85},{3,87},{5,89},{7,91},{9,93},{11,95},{13,65},{15,67},{17,69}... | collective-permute-start | bytes 32 | tf_op jit(solution)/shard_map/ppermute | solution.py:386
  13.5 4.3 %collective-permute-start.1 = (s32[2]{0:T(128)S(1)}, s32[2]{0:T(128)S(1)}, u32[]{:S(2)}, u32[]{:S(2)}) collective-permute-start(s32[2]{0:T(128)S(1)} %collective-permute-done), channel_id=1, source_target_pairs={{1,3},{3,1},{5,7},{7,5},{9,11},{11,9},{13,15},{15,13},{17,19},{19,... | collective-permute-start | bytes 32 | tf_op jit(solution)/shard_map/ppermute | solution.py:386
  38.3 26.6 %copy-start.3 = (bf16[7168,128]{1,0:T(8,128)(2,1)S(1)}, bf16[7168,128]{1,0:T(8,128)(2,1)}, u32[]{:S(2)}) copy-start(bf16[7168,128]{1,0:T(8,128)(2,1)} %do_ref.1) | copy-start | bytes 5505028
  41.0 24.0 %copy-start.1 = (bf16[7168,128]{1,0:T(8,128)(2,1)S(1)}, bf16[7168,128]{1,0:T(8,128)(2,1)}, u32[]{:S(2)}) copy-start(bf16[7168,128]{1,0:T(8,128)(2,1)} %go_ref.1) | copy-start | bytes 5505028
  41.0 24.0 %copy-start.2 = (bf16[7168,128]{1,0:T(8,128)(2,1)S(1)}, bf16[7168,128]{1,0:T(8,128)(2,1)}, u32[]{:S(2)}) copy-start(bf16[7168,128]{1,0:T(8,128)(2,1)} %uo_ref.1) | copy-start | bytes 5505028

commit v10 on v9

--- a/solution.py
+++ b/solution.py
@@ -114,7 +114,9 @@
     x = jnp.dot(order, x_ref[...].reshape(chips * deep, lanes), preferred_element_type=F32)
     hid_rows = [x[i * rows : (i + 1) * rows, wide:] for i in range(4)]
     x = jnp.concatenate([x[i * rows : (i + 1) * rows, :wide] for i in range(pieces)], axis=1).astype(BF16)
-    sums = [lax.dot_general(x, w[...], NT, preferred_element_type=F32) for w in (own, oth)]
+    wider = jnp.concatenate([own[...], oth[...]], axis=0)
+    both = lax.dot_general(wider, x, NT, preferred_element_type=F32)
+    sums = [both[:cols].T, both[cols:].T]
     me = lax.axis_index("dev")
     core, chip = me % 2, me // 2
     lane = lax.broadcasted_iota(jnp.int32, (rows, 128), 1)
@@ -382,7 +384,7 @@
         up = (up_weight, swap(up_weight))
         down = (down_weight, swap(down_weight))
         token = lengths
-        for link in (far, near):
+        for link in (near, far):
             token = lax.ppermute(token, both, link)
         message = attend(lengths, query, key_cache, value_cache, hidden, token, chips)
         got = lax.all_to_all(message, "dev", 0, 0, axis_index_groups=plane)

time: 92.2 us -> 92.2 us (level)
  no operation moved by 1% of the time
where the time goes in v10:
time: 92.2 us; the launch traced here: 91.9 us
  blocking collectives  62.5 us (68%)
  starting transfers between devices  16 us (17%)
  Pallas kernels  11.5 us (12%)
  waiting for transfers between devices  1.76 us (2%)
    all_to_all x1, blocking collectives, shards(): blocks = lax.all_to_all(block, both, 0, 0, axis_index_groups=cube)  24 us
    all_to_all x1, blocking collectives, shards(): parts = lax.all_to_all(partial, both, 0, 0, axis_index_groups=cube)  22.3 us
    all_to_all x1, blocking collectives, shards(): got = lax.all_to_all(message, 'dev', 0, 0, axis_index_groups=plane)  16.2 us
    ppermute x2, starting transfers between devices, shards(): token = lax.ppermute(token, both, link)  14.1 us
    pallas_call x1, Pallas kernels, attend(): pl.pallas_call(attend_kernel, in_specs=[pl.BlockSpec(memory_space=pltpu.S...  3.95 us
    pallas_call x1, Pallas kernels, feed_forward(): pl.pallas_call(functools.partial(ffn_kernel, chips, cols, width), in_spec...  3.46 us
    pallas_call x1, Pallas kernels, project(): pl.pallas_call(functools.partial(project_kernel, cols), in_specs=[pl.Bloc...  2.56 us
    ppermute x4, starting transfers between devices, swap(): return lax.ppermute(w, 'dev', other)  1.94 us
  transfers between devices with their start and end apart: 6, of which 2 were waited for; matrix products, arithmetic and copies ran while one was open for 0% of the time, Pallas kernels for 4%

profile of v10, /device:TPU:1, one launch (start us, length us, event | category | flops | bytes accessed | tf_op | source)
XLA Modules:
  0.0 91.9 jit_solution(5333611702187507093)
XLA Ops:
  0.0 0.0 copy-start
  0.0 0.0 copy-start.4
  0.0 1.4 %collective-permute-start.2 = (bf16[224,8192]{1,0:T(8,128)(2,1)}, bf16[224,8192]{1,0:T(8,128)(2,1)S(1)}, u32[]{:S(2)}, u32[]{:S(2)}) collective-permute-start(bf16[224,8192]{1,0:T(8,128)(2,1)} %bitcast.4), channel_id=1, source_target_pairs={{0,1},{1,0},{2,3},{3,2},{4,5},{5,4},{6,7},{7,6},{8,9},{9,8},{10,11... | collective-permute-start | bytes 11010056 | tf_op jit(solution)/shard_map/ppermute | solution.py:379
  1.4 0.0 collective-permute-start.3
  1.4 0.5 collective-permute-start.4
  1.9 0.0 collective-permute-start.5
  1.9 3.7 %collective-permute-start = (s32[2]{0:T(128)}, s32[2]{0:T(128)S(1)}, u32[]{:S(2)}, u32[]{:S(2)}) collective-permute-start(s32[2]{0:T(128)} %lengths_ref.3), channel_id=1, source_target_pairs={{1,3},{3,1},{5,7},{7,5},{9,11},{11,9},{13,15},{15,13},{17,19},{19,... | collective-permute-start | bytes 32 | tf_op jit(solution)/shard_map/ppermute | solution.py:388
  5.7 1.0 %collective-permute-done = s32[2]{0:T(128)S(1)} collective-permute-done((s32[2]{0:T(128)}, s32[2]{0:T(128)S(1)}, u32[]{:S(2)}, u32[]{:S(2)}) %collective-permute-start) | collective-permute-done | bytes 40 | tf_op jit(solution)/shard_map/ppermute | solution.py:388
  6.7 10.4 %collective-permute-start.1 = (s32[2]{0:T(128)S(1)}, s32[2]{0:T(128)S(1)}, u32[]{:S(2)}, u32[]{:S(2)}) collective-permute-start(s32[2]{0:T(128)S(1)} %collective-permute-done), channel_id=1, source_target_pairs={{1,85},{3,87},{5,89},{7,91},{9,93},{11,95},{13,65},{15,67},{17,69}... | collective-permute-start | bytes 32 | tf_op jit(solution)/shard_map/ppermute | solution.py:388
  17.1 0.7 collective-permute-done.1.token_hbm
  17.8 4.0 %shard_map.100 = bf16[16,16,1152]{2,1,0:T(8,128)(2,1)S(1)} custom-call(s32[2]{0:T(128)} %lengths_ref.3, bf16[2,8192]{1,0:T(2,128)(2,1)} %q_hbm.1, bf16[2,2048,256]{2,1,0:T(8,128)(2,1)} %k_hbm.1, bf16[2,2048,256]{2,1,0:T(8,128)(2,1)} %v_hbm.1, bf16[2,7168]{1,0:T(2,128)(2,1)} %hid_hbm.1, s32[2]{0:T(128)S(1)} %collective-permute-done.1.token_hbm), custom_call_target="tpu_custom_call" | custom-call | tf_op jit(solution)/shard_map/pallas_call | solution.py:86
  21.8 16.2 %all_to_all.15.x_ref = bf16[16,16,1152]{2,1,0:T(8,128)(2,1)S(1)} all-to-all(bf16[16,16,1152]{2,1,0:T(8,128)(2,1)S(1)} %shard_map.100), channel_id=1, replica_groups={{0,2,4,6,8,10,12,14,16,18,20,22,24,26,28,30},{1,3,5,7,9,11,13,15,17,19,..., dimensions={0} | all-to-all | bytes 1179648 | tf_op jit(solution)/shard_map/all_to_all | solution.py:390
  38.0 0.0 collective-permute-done.3.refs_0_.gx_ref
  38.0 0.0 collective-permute-done.4.refs_1_.ux_ref
  38.0 0.0 collective-permute-done.5.refs_2_.dx_ref
  38.0 0.0 collective-permute-done.2.oth
  38.0 0.0 copy-done
  38.0 0.0 copy-done.4
  38.0 0.0 copy-start.3
  38.0 2.6 %shard_map.101 = (bf16[64,112,128]{2,1,0:T(8,128)(2,1)S(1)}, f32[4,32,128]{2,1,0:T(8,128)S(1)}) custom-call(bf16[16,16,1152]{2,1,0:T(8,128)(2,1)S(1)} %all_to_all.15.x_ref, bf16[224,8192]{1,0:T(8,128)(2,1)S(1)} %bitcast.5, bf16[224,8192]{1,0:T(8,128)(2,1)S(1)} %collective-permute-done.2.oth, f32[56,128]{1,0:T(8,128)S(1)} %bitcast.6, ...), custom_call_target="tpu_custom_call" | custom-call | flops 234881024 | bytes 7340032 | tf_op jit(solution)/shard_map/pallas_call | solution.py:180
  40.6 0.0 copy-start.1
  40.6 0.0 copy-start.2
  40.6 24.0 %all_to_all.16 = bf16[64,112,128]{2,1,0:T(8,128)(2,1)S(1)} all-to-all(bf16[64,112,128]{2,1,0:T(8,128)(2,1)S(1)} %get-tuple-element.7), channel_id=1, replica_groups={{0,2,4,6,8,10,12,14,16,18,20,22,24,26,28,30,32,34,36,38,40,42,44,46,48,..., dimensions={0} | all-to-all | bytes 3670016 | tf_op jit(solution)/shard_map/all_to_all | solution.py:394
  64.6 0.0 copy-done.3
  64.6 0.0 copy-done.1
  64.6 0.0 copy-done.2
  64.6 3.5 %shard_map.102 = bf16[64,16,896]{2,1,0:T(8,128)(2,1)S(1)} custom-call(bf16[4,16,112,128]{3,2,1,0:T(8,128)(2,1)S(1)} %bitcast.3, bf16[7168,128]{1,0:T(8,128)(2,1)S(1)} %copy-done.1, bf16[7168,128]{1,0:T(8,128)(2,1)S(1)} %collective-permute-done.3.refs_0_.gx_ref, bf16[7168,128]{1,0:T(8,128)(2,1)S(1)} %copy-done.2, ...), custom_call_target="tpu_custom_call" | custom-call | flops 1409286144 | bytes 12845056 | tf_op jit(solution)/shard_map/pallas_call | solution.py:307
  68.0 22.3 %all_to_all.17.parts_ref = bf16[64,16,896]{2,1,0:T(8,128)(2,1)S(1)} all-to-all(bf16[64,16,896]{2,1,0:T(8,128)(2,1)S(1)} %shard_map.102), channel_id=1, replica_groups={{0,2,4,6,8,10,12,14,16,18,20,22,24,26,28,30,32,34,36,38,40,42,44,46,48,..., dimensions={0} | all-to-all | bytes 3670016 | tf_op jit(solution)/shard_map/all_to_all | solution.py:396
  90.4 1.5 %shard_map.103 = bf16[2,7168]{1,0:T(2,128)(2,1)} custom-call(s32[2]{0:T(128)} %lengths_ref.3, bf16[64,16,896]{2,1,0:T(8,128)(2,1)S(1)} %all_to_all.17.parts_ref), custom_call_target="tpu_custom_call" | custom-call | tf_op jit(solution)/shard_map/pallas_call | solution.py:343
Async XLA Ops:
  0.0 38.0 %copy-start = (bf16[8192,224]{0,1:T(8,128)(2,1)S(1)}, bf16[8192,224]{0,1:T(8,128)(2,1)}, u32[]{:S(2)}) copy-start(bf16[8192,224]{0,1:T(8,128)(2,1)} %param.15) | copy-start | bytes 11010052
  0.0 38.0 %copy-start.4 = (f32[7168]{0:T(1024)S(1)}, f32[7168]{0:T(1024)}, u32[]{:S(2)}) copy-start(f32[7168]{0:T(1024)} %param.16) | copy-start | bytes 86020
  0.0 38.0 %collective-permute-start.2 = (bf16[224,8192]{1,0:T(8,128)(2,1)}, bf16[224,8192]{1,0:T(8,128)(2,1)S(1)}, u32[]{:S(2)}, u32[]{:S(2)}) collective-permute-start(bf16[224,8192]{1,0:T(8,128)(2,1)} %bitcast.4), channel_id=1, source_target_pairs={{0,1},{1,0},{2,3},{3,2},{4,5},{5,4},{6,7},{7,6},{8,9},{9,8},{10,11... | collective-permute-start | bytes 11010056 | tf_op jit(solution)/shard_map/ppermute | solution.py:379
  1.4 36.5 %collective-permute-start.3 = (bf16[7168,128]{1,0:T(8,128)(2,1)}, bf16[7168,128]{1,0:T(8,128)(2,1)S(1)}, u32[]{:S(2)}, u32[]{:S(2)}) collective-permute-start(bf16[7168,128]{1,0:T(8,128)(2,1)} %go_ref.1), channel_id=1, source_target_pairs={{0,1},{1,0},{2,3},{3,2},{4,5},{5,4},{6,7},{7,6},{8,9},{9,8},{10,11... | collective-permute-start | bytes 5505032 | tf_op jit(solution)/shard_map/ppermute | solution.py:379
  1.4 36.5 %collective-permute-start.4 = (bf16[7168,128]{1,0:T(8,128)(2,1)}, bf16[7168,128]{1,0:T(8,128)(2,1)S(1)}, u32[]{:S(2)}, u32[]{:S(2)}) collective-permute-start(bf16[7168,128]{1,0:T(8,128)(2,1)} %uo_ref.1), channel_id=1, source_target_pairs={{0,1},{1,0},{2,3},{3,2},{4,5},{5,4},{6,7},{7,6},{8,9},{9,8},{10,11... | collective-permute-start | bytes 5505032 | tf_op jit(solution)/shard_map/ppermute | solution.py:379
  1.9 36.0 %collective-permute-start.5 = (bf16[7168,128]{1,0:T(8,128)(2,1)}, bf16[7168,128]{1,0:T(8,128)(2,1)S(1)}, u32[]{:S(2)}, u32[]{:S(2)}) collective-permute-start(bf16[7168,128]{1,0:T(8,128)(2,1)} %do_ref.1), channel_id=1, source_target_pairs={{0,1},{1,0},{2,3},{3,2},{4,5},{5,4},{6,7},{7,6},{8,9},{9,8},{10,11... | collective-permute-start | bytes 5505032 | tf_op jit(solution)/shard_map/ppermute | solution.py:379
  1.9 4.8 %collective-permute-start = (s32[2]{0:T(128)}, s32[2]{0:T(128)S(1)}, u32[]{:S(2)}, u32[]{:S(2)}) collective-permute-start(s32[2]{0:T(128)} %lengths_ref.3), channel_id=1, source_target_pairs={{1,3},{3,1},{5,7},{7,5},{9,11},{11,9},{13,15},{15,13},{17,19},{19,... | collective-permute-start | bytes 32 | tf_op jit(solution)/shard_map/ppermute | solution.py:388
  6.7 11.1 %collective-permute-start.1 = (s32[2]{0:T(128)S(1)}, s32[2]{0:T(128)S(1)}, u32[]{:S(2)}, u32[]{:S(2)}) collective-permute-start(s32[2]{0:T(128)S(1)} %collective-permute-done), channel_id=1, source_target_pairs={{1,85},{3,87},{5,89},{7,91},{9,93},{11,95},{13,65},{15,67},{17,69}... | collective-permute-start | bytes 32 | tf_op jit(solution)/shard_map/ppermute | solution.py:388
  38.0 26.6 %copy-start.3 = (bf16[7168,128]{1,0:T(8,128)(2,1)S(1)}, bf16[7168,128]{1,0:T(8,128)(2,1)}, u32[]{:S(2)}) copy-start(bf16[7168,128]{1,0:T(8,128)(2,1)} %do_ref.1) | copy-start | bytes 5505028
  40.6 24.0 %copy-start.1 = (bf16[7168,128]{1,0:T(8,128)(2,1)S(1)}, bf16[7168,128]{1,0:T(8,128)(2,1)}, u32[]{:S(2)}) copy-start(bf16[7168,128]{1,0:T(8,128)(2,1)} %go_ref.1) | copy-start | bytes 5505028
  40.6 24.0 %copy-start.2 = (bf16[7168,128]{1,0:T(8,128)(2,1)S(1)}, bf16[7168,128]{1,0:T(8,128)(2,1)}, u32[]{:S(2)}) copy-start(bf16[7168,128]{1,0:T(8,128)(2,1)} %uo_ref.1) | copy-start | bytes 5505028
